TPU v7x, 32 devices: a whole 2x2x4 slice. The times are simulated.
32 devices in a mesh: groups: 2 (over y), ctx: 4 (over z), head: 2 (over x), sess: 2 (over core).
Axes of the slice: x: 2, y: 2, z: 4, core: 2. Of those that a mesh axis runs over, the one named last changes fastest.
Arguments:
- head_input: bfloat16 [8, 512, 8192], P(('groups', 'sess'), 'ctx', 'head'), parts along dimension 0, may hold values from -6 to 6
- gate_input: bfloat16 [8, 512, 8192], P(('groups', 'sess'), 'ctx', 'head'), parts along dimension 0, may hold values from -6 to 6
- state_in_proj: bfloat16 [8, 512, 8, 128], P(('groups', 'sess'), 'ctx'), parts along dimension 0, may hold values from -1.796875 to 1.796875
- state_out_proj: bfloat16 [8, 512, 8, 128], P(('groups', 'sess'), 'ctx'), parts along dimension 0, may hold values from -1.796875 to 1.796875
- step_raw: float32 [8, 512, 128], P(('groups', 'sess'), 'ctx', 'head'), parts along dimension 0, may hold values from -2.5 to 12.5
- head_step_bias: float32 [128], P('head'), may hold values from -5.3 to -2.25
- decay_log: float32 [128], P('head'), may hold values from -7.7 to 0
- skip_gain: float32 [128], P('head'), may hold values from 0.5 to 2
- norm_gain: float32 [8192], P('head'), may hold values from 0.1 to 1.9
- out_weight: bfloat16 [8192, 4096], P('head', 'ctx'), may hold values from -0.09375 to 0.09375
- pool_states: float32 [16, 128, 64, 128], P(('groups', 'sess'), 'head', None, 'ctx'), parts along dimension 0, may hold values from -6 to 6
- slot_map: int32 [8], P('groups'), parts along dimension 0, may hold values from 0 to 7, as said below
- span_lengths: int32 [8], P('groups'), parts along dimension 0, may hold values from 1 to 4, as said below
Outputs:
- mixed: bfloat16 [8, 512, 4096], P(('groups', 'sess'), 'ctx', 'head'), parts along dimension 0
- final_states: float32 [8, 128, 64, 128], P(('groups', 'sess'), 'head', None, 'ctx'), parts along dimension 0
There are 2 independent parts, one for each index of `groups`. A program takes and returns all parts, laid end to end along the dimension named above; an argument that names none is the same for every part. Nothing has to cross between parts.
Inputs may be any that keep to these rules, and one draw needn't show every extreme that they name: `slot_map`: the sessions of a group take distinct decode slots. `span_lengths`: some session of every group fills all 4 units.
All inputs are finite; a program needn't handle non-finite values.
Results may differ from a plain program's by a relative error of at most 0.018.
Values may be sent and summed in bfloat16 or wider, within the bound.
No kernel may reach another device: no remote copies, remote signals or barrier semaphores. Data moves between devices by JAX's collectives and lax.ppermute only.
A program may use at most 128 MiB of HBM per device.

v0:
```python
import jax
import jax.numpy as jnp
from jax import lax
from jax.sharding import PartitionSpec as P

HEADS = 128
GROUPS = 8
SPAN = 128


highest = lax.Precision.HIGHEST
norm_eps = 1e-05


def shifted(value, axis, by):
    length = lax.axis_size(axis)
    pairs = [(i, i + by) for i in range(length) if 0 <= i + by < length]
    return lax.ppermute(value, axis, pairs)


def from_root(block, axis, owner):
    block = jnp.where(lax.axis_index(axis) == owner, block, jnp.zeros_like(block))
    return lax.psum(block, axis)


def shards(
    head_input,
    gate_input,
    state_in_proj,
    state_out_proj,
    step_raw,
    head_step_bias,
    decay_log,
    skip_gain,
    norm_gain,
    out_weight,
    pool_states,
    slot_map,
    span_lengths,
):
    ctx_count = lax.axis_size("ctx")
    ctx_index = lax.axis_index("ctx")
    sess_index = lax.axis_index("sess")
    head_index = lax.axis_index("head")
    sessions, tokens, inner = head_input.shape
    heads = step_raw.shape[2]
    head_dim = inner // heads
    state_cols = pool_states.shape[3]
    group_heads = HEADS // GROUPS
    spans = tokens // SPAN
    first_session = sess_index * sessions
    own_lengths = lax.dynamic_slice_in_dim(span_lengths, first_session, sessions)
    position = ctx_index * tokens + jnp.arange(tokens, dtype=jnp.int32)
    live_rows = (position[None, :] < own_lengths[:, None] * SPAN).astype(jnp.float32)
    step_size = jax.nn.softplus(step_raw + head_step_bias) * live_rows[:, :, None]
    log_keep = -jnp.exp(decay_log) * step_size
    pooled = lax.all_gather(pool_states.astype(jnp.bfloat16), "sess", axis=0, tiled=True).astype(
        pool_states.dtype
    )
    own_slots = lax.dynamic_slice_in_dim(slot_map, first_session, sessions)
    start_cols = jnp.take(pooled, own_slots, axis=0)
    start_state = lax.all_gather(start_cols.astype(jnp.bfloat16), "ctx", axis=3, tiled=True).astype(
        start_cols.dtype
    )
    first_head = head_index * heads
    group_count = max(1, heads // group_heads)
    repeats = min(heads, group_heads)
    first_group = first_head // group_heads
    state_size = state_in_proj.shape[3]
    group_shape = (sessions, spans, SPAN, group_count, state_size)
    b_groups = (
        lax.dynamic_slice_in_dim(state_in_proj, first_group, group_count, 2)
        .astype(jnp.float32)
        .reshape(group_shape)
    )
    c_groups = (
        lax.dynamic_slice_in_dim(state_out_proj, first_group, group_count, 2)
        .astype(jnp.float32)
        .reshape(group_shape)
    )
    b_heads = jnp.repeat(b_groups, repeats, axis=3)
    c_heads = jnp.repeat(c_groups, repeats, axis=3)
    inputs = head_input.astype(jnp.float32).reshape(sessions, spans, SPAN, heads, head_dim)
    cum_log = jnp.cumsum(log_keep.reshape(sessions, spans, SPAN, heads), axis=2)
    cum_heads = jnp.moveaxis(cum_log, 3, 2)
    size_heads = jnp.moveaxis(step_size.reshape(sessions, spans, SPAN, heads), 3, 2)
    causal = jnp.arange(SPAN)[:, None] >= jnp.arange(SPAN)[None, :]
    log_gap = cum_heads[..., :, None] - cum_heads[..., None, :]
    decay_pairs = (
        jnp.where(causal, jnp.exp(jnp.where(causal, log_gap, 0.0)), 0.0) * size_heads[..., None, :]
    )
    products_cb = jnp.einsum("sclgn,scmgn->scglm", c_groups, b_groups, precision=highest)
    score_values = jnp.repeat(products_cb, repeats, axis=2) * decay_pairs
    inside_span = jnp.einsum("schlm,scmhp->sclhp", score_values, inputs, precision=highest)
    tail_weight = jnp.exp(cum_heads[..., -1:] - cum_heads) * size_heads
    span_states = jnp.einsum(
        "schm,scmhp,scmhn->schpn", tail_weight, inputs, b_heads, precision=highest
    )
    span_log = cum_heads[..., -1]
    running = jnp.zeros((sessions, heads, head_dim, state_size), jnp.float32)
    entering = [running]
    running = jnp.exp(span_log[:, 0])[..., None, None] * running + span_states[:, 0]
    local_end = running
    shard_log = jnp.sum(span_log, axis=1)
    entry_states = jnp.stack(entering, axis=1)
    prior_log = jnp.cumsum(span_log, axis=1) - span_log
    from_entry = (
        jnp.einsum("sclhn,schpn->sclhp", c_heads, entry_states, precision=highest)
        * jnp.exp(cum_log)[..., None]
    )

    def relay_turn(turn_index, carried):
        outgoing = jnp.exp(shard_log)[..., None, None] * carried + local_end
        incoming = shifted(outgoing.astype(jnp.bfloat16), "ctx", 1).astype(outgoing.dtype)
        return jnp.where(ctx_index == 0, start_state, incoming)

    carried = lax.fori_loop(0, ctx_count - 1, relay_turn, start_state)
    from_start = cum_log + prior_log[:, :, None, :]
    from_carry = (
        jnp.einsum("sclhn,shpn->sclhp", c_heads, carried, precision=highest)
        * jnp.exp(from_start)[..., None]
    )
    ssd_out = inside_span + from_entry + from_carry + skip_gain[:, None] * inputs
    gated = ssd_out.reshape(sessions, tokens, inner) * jax.nn.silu(gate_input.astype(jnp.float32))
    grouped = gated.reshape(sessions, tokens, heads // group_heads, group_heads * head_dim)
    norm_scale = lax.rsqrt(jnp.mean(grouped * grouped, axis=3, keepdims=True) + norm_eps)
    normed = (grouped * norm_scale).reshape(sessions, tokens, inner)
    normed = (normed * norm_gain).astype(jnp.bfloat16)
    partial_out = jnp.einsum(
        "stk,kd->std",
        normed,
        lax.all_gather(out_weight, "ctx", axis=1, tiled=True),
        preferred_element_type=jnp.float32,
    )
    summed = lax.psum_scatter(
        partial_out.astype(jnp.bfloat16), "head", scatter_dimension=2, tiled=True
    ).astype(jnp.float32)
    mixed = (summed * live_rows[:, :, None]).astype(jnp.bfloat16)
    end_state = jnp.exp(shard_log)[..., None, None] * carried + local_end
    whole_end = from_root(end_state.astype(jnp.bfloat16), "ctx", ctx_count - 1).astype(
        end_state.dtype
    )
    final_states = lax.dynamic_slice_in_dim(whole_end, ctx_index * state_cols, state_cols, 3)
    return (mixed, final_states)


def solution(mesh):
    placed = (
        P(("groups", "sess"), "ctx", "head"),
        P(("groups", "sess"), "ctx", "head"),
        P(("groups", "sess"), "ctx", None, None),
        P(("groups", "sess"), "ctx", None, None),
        P(("groups", "sess"), "ctx", "head"),
        P("head"),
        P("head"),
        P("head"),
        P("head"),
        P("head", "ctx"),
        P(("groups", "sess"), "head", None, "ctx"),
        P("groups"),
        P("groups"),
    )
    return jax.shard_map(
        shards,
        mesh=mesh,
        in_specs=placed,
        out_specs=(
            P(("groups", "sess"), "ctx", "head"),
            P(("groups", "sess"), "head", None, "ctx"),
        ),
        check_vma=False,
    )
```

profile of v0, /device:TPU:12, one launch (start us, length us, event | category | flops | bytes accessed | tf_op | source)
XLA Modules:
  0.0 938.1 jit_solution(13627045292249434513)
XLA Ops:
  7.2 4.0 convert_element_type.59
  11.4 15.0 %all-gather.4.cloned.1.call-done = bf16[8,64,64,32]{2,3,1,0:T(8,128)(2,1)} async-done(((bf16[4,64,64,32]{2,3,1,0:T(8,128)(2,1)}), bf16[8,64,64,32]{2,3,1,0:T(8,128)(2,1)}) %all-gather.4.cloned.1.call-update) | async-done | bytes 2097168 | tf_op jit(solution)/shard_map/all_gather | solution.py:57
  40.7 17.8 %fusion.33 = f32[2,64,64,128]{3,2,1,0:T(8,128)} fusion(f32[2,128,64,128]{3,1,2,0:T(8,128)S(1)} %bitcast.69), kind=kOutput, calls=%fused_computation.41 | convolution fusion | flops 1610612736 | bytes 12582912 | tf_op jit(solution)/shard_map/sclhn,schpn->sclhp/dot_general | solution.py:108
  60.1 9.1 fusion.27
  70.2 11.9 %fusion.2 = f32[2,64,128,64]{2,3,1,0:T(8,128)} fusion(bf16[2,128,64,64]{1,3,2,0:T(8,128)(2,1)S(1)} %bitcast.76, f32[2,64,128,128]{3,2,1,0:T(8,128)S(1)} %bitcast.74, f32[2,64,128]{2,1,0:T(8,128)S(1)} %copy.85, f32[2,64,128]{2,1,0:T(8,128)S(1)} %copy.83, pred[128,128]{1,0:T(8,128)(4,1)S(1)} %iota_compare_fusion), kind=kOutput, calls=%fused_computation.5 | convolution fusion | flops 1621098496 | bytes 14827520 | tf_op jit(solution)/shard_map/schlm,scmhp->sclhp/dot_general | solution.py:94
  82.1 27.9 %all-gather.6.cloned.1.call-done = bf16[2,64,64,128]{2,3,1,0:T(8,128)(2,1)} async-done(((bf16[2,64,64,32]{2,3,1,0:T(8,128)(2,1)}), bf16[2,64,64,128]{2,3,1,0:T(8,128)(2,1)}) %all-gather.6.cloned.1.call-update) | async-done | bytes 2097168 | tf_op jit(solution)/shard_map/all_gather | solution.py:62
  110.0 5.2 copy.89
  115.2 5.0 copy.107
  120.2 454.1 %while.12 = (s32[]{:T(128)}, f32[2,64,64,128]{3,2,1,0:T(8,128)}, pred[]{:T(512)}, f32[2,64,1,1]{1,0,3,2:T(2,128)S(1)}, f32[2,64,64,128]{3,2,1,0:T(8,128)}, /*index=5*/f32[2,64,64,128]{3,2,1,0:T(8,128)}, s32[]{:T(128)}) while((s32[]{:T(128)}, f32[2,64,64,128]{3,2,1,0:T(8,128)}, pred[]{:T(512)}, f32[2,64,1,1]{1,0,3,2:T(2,128)S(1)}, ...), condition=%wide.region_2.3_spmd, body=%wide.region_1.2_spmd.sunk | while | flops 5242882 | bytes 29360756 | solution.py:117
  120.2 6.6 add_convert_fusion.3
  126.8 4.7 collective-permute-start
  131.5 133.4 %collective-permute-done = bf16[2,64,64,128]{3,2,1,0:T(8,128)(2,1)} collective-permute-done((bf16[2,64,64,128]{3,2,1,0:T(8,128)(2,1)S(1)}, bf16[2,64,64,128]{3,2,1,0:T(8,128)(2,1)}, u32[]{:S(2)}, u32[]{:S(2)}) %collective-permute-start) | collective-permute-done | bytes 2097184 | tf_op jit(solution)/shard_map/while/body/eval_jaxpr/ppermute | solution.py:18
  264.9 4.6 convert_select_fusion.2
  269.5 4.1 add_convert_fusion.3
  273.7 15.8 %collective-permute-start = (bf16[2,64,64,128]{3,2,1,0:T(8,128)(2,1)S(1)}, bf16[2,64,64,128]{3,2,1,0:T(8,128)(2,1)}, u32[]{:S(2)}, u32[]{:S(2)}) collective-permute-start(bf16[2,64,64,128]{3,2,1,0:T(8,128)(2,1)S(1)} %add_convert_fusion.3), channel_id=1, source_target_pairs={{0,4},{4,8},{8,12},{1,5},{5,9},{9,13},{2,6},{6,10},{10,14},{3,7},{... | collective-permute-start | bytes 6291464 | tf_op jit(solution)/shard_map/while/body/eval_jaxpr/ppermute | solution.py:18
  289.5 133.3 %collective-permute-done = bf16[2,64,64,128]{3,2,1,0:T(8,128)(2,1)} collective-permute-done((bf16[2,64,64,128]{3,2,1,0:T(8,128)(2,1)S(1)}, bf16[2,64,64,128]{3,2,1,0:T(8,128)(2,1)}, u32[]{:S(2)}, u32[]{:S(2)}) %collective-permute-start) | collective-permute-done | bytes 2097184 | tf_op jit(solution)/shard_map/while/body/eval_jaxpr/ppermute | solution.py:18
  422.8 4.6 convert_select_fusion.2
  427.4 4.0 add_convert_fusion.3
  431.4 6.5 collective-permute-start
  437.9 131.7 %collective-permute-done = bf16[2,64,64,128]{3,2,1,0:T(8,128)(2,1)} collective-permute-done((bf16[2,64,64,128]{3,2,1,0:T(8,128)(2,1)S(1)}, bf16[2,64,64,128]{3,2,1,0:T(8,128)(2,1)}, u32[]{:S(2)}, u32[]{:S(2)}) %collective-permute-start) | collective-permute-done | bytes 2097184 | tf_op jit(solution)/shard_map/while/body/eval_jaxpr/ppermute | solution.py:18
  569.7 4.6 convert_select_fusion.2
  574.3 22.6 %fusion.17 = f32[2,1,128,64,64]{2,4,3,0,1:T(8,128)} fusion(f32[2,64,64,128]{3,2,1,0:T(8,128)} %fusion.33, f32[2,64,128,64]{2,3,1,0:T(8,128)} %fusion.2, f32[2,1,128,64,64]{2,4,3,0,1:T(8,128)} %bitcast.72, f32[2,64,64,128]{3,2,1,0:T(8,128)} %get-tuple-element.76, f32[2,128,64,128]{3,1,2,0:T(8,128)} %bitcast.70, f32[64]{0:T(128)S(1)} %copy-done.8, ...), kind=kOutput, calls=%fused_computation.21 | convolution fusion | flops 1616904192 | bytes 29491456 | tf_op jit(solution)/shard_map/sclhn,shpn->sclhp/dot_general | solution.py:120
  596.9 5.8 copy.93
  602.7 5.3 fusion.45
  608.0 6.0 mul.183
  619.5 6.1 mul.185
  625.6 5.5 fusion.30
  631.2 174.7 %all-gather.8.cloned.1.call-done = bf16[4096,4096]{1,0:T(8,128)(2,1)} async-done(((bf16[4096,1024]{1,0:T(8,128)(2,1)}), bf16[4096,4096]{1,0:T(8,128)(2,1)}) %all-gather.8.cloned.1.call-update) | async-done | bytes 33554448 | tf_op jit(solution)/shard_map/all_gather | solution.py:132
  805.9 19.4 %fusion.9 = bf16[2,128,4096]{2,1,0:T(8,128)(2,1)} fusion(bf16[4096,4096]{1,0:T(8,128)(2,1)} %all-gather.8.cloned.1.call-done, f32[2,128,4096]{2,1,0:T(8,128)} %mul.185, f32[4096]{0:T(1024)S(1)} %copy-done.10, f32[2,128,4096]{2,1,0:T(8,128)} %copy.93, bf16[2,128,4096]{2,1,0:T(8,128)(2,1)S(1)} %copy-done.3), kind=kOutput, calls=%fused_computation.14 | convolution fusion | flops 8600420352 | bytes 46153728 | tf_op jit(solution)/shard_map/stk,kd->std/dot_general | solution.py:129
  825.4 69.4 %all-reduce.2.cloned.1.call-done = bf16[2,64,64,128]{3,2,1,0:T(8,128)(2,1)} async-done(((bf16[2,64,64,128]{3,2,1,0:T(8,128)(2,1)}), bf16[2,64,64,128]{3,2,1,0:T(8,128)(2,1)}) %all-reduce.2.cloned.1.call-update) | async-done | bytes 2097168 | tf_op jit(solution)/shard_map/psum | solution.py:23
  894.7 4.3 dynamic-slice_convert_fusion
  902.8 26.4 %reduce-scatter.2.cloned.1.call-done = bf16[2,128,2048]{2,1,0:T(8,128)(2,1)} async-done(((bf16[2,128,4096]{2,1,0:T(8,128)(2,1)}), bf16[2,128,2048]{2,1,0:T(8,128)(2,1)}) %reduce-scatter.2.cloned.1.call-update) | async-done | bytes 1048592 | tf_op jit(solution)/shard_map/reduce_scatter | solution.py:135
  (71 shorter events, 28.5 us)
Async XLA Ops:
  7.2 4.1 copy-start.9
  7.2 19.3 %all-gather.4.cloned.1.call-start = ((), (), s32[]{:S(2)}) async-start(), calls=%async_computation.1 | async-start | bytes 6291456 | tf_op jit(solution)/shard_map/all_gather | solution.py:57
  11.2 98.8 %all-gather.6.cloned.1.call-start = ((), (), s32[]{:S(2)}) async-start(), calls=%async_computation.2 | async-start | bytes 5242880 | tf_op jit(solution)/shard_map/all_gather | solution.py:62
  30.7 1.6 copy-start.1
  30.7 775.3 %all-gather.8.cloned.1.call-start = ((), (), s32[]{:S(2)}) async-start(), calls=%async_computation.3 | async-start | bytes 41943040 | tf_op jit(solution)/shard_map/all_gather | solution.py:132
  31.4 863.3 %all-reduce.2.cloned.1.call-start = ((), (), s32[]{:S(2)}) async-start(), calls=%async_computation.5 | async-start | bytes 4194304 | tf_op jit(solution)/shard_map/psum | solution.py:23
  34.7 3.0 copy-start.6
  34.7 3.1 copy-start.11
  34.7 3.2 copy-start.12
  34.7 3.3 copy-start.7
  34.7 4.2 copy-start.4
  34.7 4.2 copy-start.5
  40.7 17.8 %copy-start = (f32[2,128,4,16,128]{4,1,3,2,0:T(8,128)}, f32[2,128,4,16,128]{4,1,3,2,0:T(8,128)S(1)}, u32[]{:S(2)}) copy-start(f32[2,128,4,16,128]{4,1,3,2,0:T(8,128)S(1)} %broadcast_in_dim.68) | copy-start | bytes 25165828
  58.5 1.6 copy-start.2
  120.2 454.1 %copy-start.8 = (f32[64]{0:T(128)S(1)}, f32[64]{0:T(128)}, u32[]{:S(2)}) copy-start(f32[64]{0:T(128)} %param.22) | copy-start | bytes 772
  126.8 138.1 %collective-permute-start = (bf16[2,64,64,128]{3,2,1,0:T(8,128)(2,1)S(1)}, bf16[2,64,64,128]{3,2,1,0:T(8,128)(2,1)}, u32[]{:S(2)}, u32[]{:S(2)}) collective-permute-start(bf16[2,64,64,128]{3,2,1,0:T(8,128)(2,1)S(1)} %add_convert_fusion.3), channel_id=1, source_target_pairs={{0,4},{4,8},{8,12},{1,5},{5,9},{9,13},{2,6},{6,10},{10,14},{3,7},{... | collective-permute-start | bytes 6291464 | tf_op jit(solution)/shard_map/while/body/eval_jaxpr/ppermute | solution.py:18
  273.7 149.1 %collective-permute-start = (bf16[2,64,64,128]{3,2,1,0:T(8,128)(2,1)S(1)}, bf16[2,64,64,128]{3,2,1,0:T(8,128)(2,1)}, u32[]{:S(2)}, u32[]{:S(2)}) collective-permute-start(bf16[2,64,64,128]{3,2,1,0:T(8,128)(2,1)S(1)} %add_convert_fusion.3), channel_id=1, source_target_pairs={{0,4},{4,8},{8,12},{1,5},{5,9},{9,13},{2,6},{6,10},{10,14},{3,7},{... | collective-permute-start | bytes 6291464 | tf_op jit(solution)/shard_map/while/body/eval_jaxpr/ppermute | solution.py:18
  431.4 138.2 %collective-permute-start = (bf16[2,64,64,128]{3,2,1,0:T(8,128)(2,1)S(1)}, bf16[2,64,64,128]{3,2,1,0:T(8,128)(2,1)}, u32[]{:S(2)}, u32[]{:S(2)}) collective-permute-start(bf16[2,64,64,128]{3,2,1,0:T(8,128)(2,1)S(1)} %add_convert_fusion.3), channel_id=1, source_target_pairs={{0,4},{4,8},{8,12},{1,5},{5,9},{9,13},{2,6},{6,10},{10,14},{3,7},{... | collective-permute-start | bytes 6291464 | tf_op jit(solution)/shard_map/while/body/eval_jaxpr/ppermute | solution.py:18
  596.9 5.8 copy-start.3
  625.6 180.3 %copy-start.10 = (f32[4096]{0:T(1024)S(1)}, f32[4096]{0:T(1024)}, u32[]{:S(2)}) copy-start(f32[4096]{0:T(1024)} %param.23) | copy-start | bytes 49156
  631.2 298.0 %reduce-scatter.2.cloned.1.call-start = ((), (), s32[]{:S(2)}) async-start(), calls=%async_computation.4 | async-start | bytes 3145728 | tf_op jit(solution)/shard_map/reduce_scatter | solution.py:135
Sparse Core Ops, SparseCore 0:
  11.4 15.0 all-gather.3
  30.8 79.2 all-gather.5
  111.6 694.2 all-gather.7
  808.7 85.9 all-reduce.1
  896.9 32.1 reduce-scatter.1
where the time goes:
time: 941 us; the launch traced here: 938 us
  waiting for transfers between devices  713 us (76%)
  matrix products  81.1 us (9%)
  other arithmetic  55 us (6%)
  local copies, waits for them, and re-layouts  48.1 us (5%)
  starting transfers between devices  27.1 us (3%)
  between operations  14 us (1%)
    ppermute x3, waiting for transfers between devices, shifted(): return lax.ppermute(value, axis, pairs)  398 us
    all_gather x1, waiting for transfers between devices, shards(): lax.all_gather(out_weight, 'ctx', axis=1, tiled=True)  175 us
    psum x1, waiting for transfers between devices, from_root(): return lax.psum(block, axis)  69.4 us
    all_gather x1, waiting for transfers between devices, shards(): lax.all_gather(start_cols.astype(jnp.bfloat16), 'ctx', axis=3, tiled=True)  27.9 us
    ppermute x3, starting transfers between devices, shifted(): return lax.ppermute(value, axis, pairs)  26.9 us
    reduce_scatter x1, waiting for transfers between devices, shards(): lax.psum_scatter(partial_out.astype(jnp.bfloat16), 'head', scatter_dimens...  26.4 us
    dot_general x1, matrix products, shards(): jnp.einsum('sclhn,shpn->sclhp', c_heads, carried, precision=highest)  22.6 us
    dot_general x1, matrix products, shards(): jnp.einsum('stk,kd->std', normed, lax.all_gather(out_weight, 'ctx', axis=...  19.4 us
  transfers between devices with their start and end apart: 8, of which 8 were waited for; matrix products, arithmetic and copies ran while one was open for 18% of the time, Pallas kernels for 0%

commit v1 on v0

v1 whole, which is shorter than its diff:
```python
import functools

import jax
import jax.numpy as jnp
from jax import lax
from jax.experimental import pallas as pl
from jax.experimental.pallas import tpu as pltpu
from jax.sharding import PartitionSpec as P

HEADS = 128
GROUPS = 8
SPAN = 128
GROUP_HEADS = HEADS // GROUPS
PIECES = 2

norm_eps = 1e-05
far = -1e30


def spread(values, head_dim):
    heads = values.shape[1]
    high = values.astype(jnp.bfloat16)
    low = (values - high.astype(jnp.float32)).astype(jnp.bfloat16)
    both = jnp.concatenate([high, low], axis=1)
    row = lax.broadcasted_iota(jnp.int32, (2 * heads, heads * head_dim), 0)
    col = lax.broadcasted_iota(jnp.int32, (2 * heads, heads * head_dim), 1)
    ones = (col // head_dim == row % heads).astype(jnp.bfloat16)
    return jnp.dot(both, ones, preferred_element_type=jnp.float32)


def local_kernel(
    limit_ref,
    x_ref,
    b_ref,
    c_ref,
    raw_ref,
    raw_t_ref,
    bias_ref,
    bias_t_ref,
    rate_ref,
    rate_t_ref,
    skip_ref,
    y_ref,
    end_ref,
    keep_ref,
    grow_ref,
):
    tokens, width = x_ref.shape[1:]
    heads = raw_ref.shape[3]
    head_dim = width // heads
    limit = limit_ref[pl.program_id(0)]
    token = lax.broadcasted_iota(jnp.int32, (tokens, heads), 0)
    token_t = lax.broadcasted_iota(jnp.int32, (heads, tokens), 1)
    size = jax.nn.softplus(raw_ref[0, 0] + bias_ref[0]) * (token < limit).astype(jnp.float32)
    size_t = jax.nn.softplus(raw_t_ref[0, 0] + bias_t_ref[0]) * (token_t < limit).astype(
        jnp.float32
    )
    log_keep = -jnp.exp(rate_ref[0]) * size
    log_keep_t = -jnp.exp(rate_t_ref[0]) * size_t
    row = lax.broadcasted_iota(jnp.int32, (tokens, tokens), 0)
    col = lax.broadcasted_iota(jnp.int32, (tokens, tokens), 1)
    causal = row >= col
    cum = jnp.dot(
        causal.astype(jnp.float32), log_keep, precision=lax.Precision.HIGHEST
    )
    cum_t = jnp.dot(
        log_keep_t, (row <= col).astype(jnp.float32), precision=lax.Precision.HIGHEST
    )
    shift_t = cum_t - jnp.where(size_t > 0, jnp.log(jnp.where(size_t > 0, size_t, 1.0)), far)
    b = b_ref[0, 0]
    scores = lax.dot_general(
        c_ref[0, 0], b, (((1,), (1,)), ((), ())), preferred_element_type=jnp.float32
    )
    lane = lax.broadcasted_iota(jnp.int32, (tokens, 2 * head_dim), 1)
    for pair in range(heads // 2):
        decayed = []
        for head in (2 * pair, 2 * pair + 1):
            gap = cum[:, head : head + 1] - shift_t[head : head + 1, :]
            decayed.append((scores * jnp.exp(jnp.where(causal, gap, far))).astype(jnp.bfloat16))
        here = pl.ds(pair * 2 * head_dim, 2 * head_dim)
        x = x_ref[0, :, here]
        zero = jnp.zeros_like(x)
        apart = jnp.concatenate(
            [jnp.where(lane < head_dim, x, zero), jnp.where(lane >= head_dim, x, zero)], axis=0
        )
        y = jnp.dot(
            jnp.concatenate(decayed, axis=1), apart, preferred_element_type=jnp.float32
        )
        y_ref[0, :, here] = y + skip_ref[0, :, here] * x.astype(jnp.float32)
    last = cum[tokens - 1 : tokens, :]
    tail = spread(jnp.exp(last - cum) * size, head_dim)
    weighted = (tail * x_ref[0].astype(jnp.float32)).astype(jnp.bfloat16)
    b_t = b.astype(jnp.float32).T.astype(jnp.bfloat16)
    end_ref[0, 0] = jnp.dot(b_t, weighted, preferred_element_type=jnp.float32)
    keep_ref[0, 0] = spread(jnp.broadcast_to(jnp.exp(last), (8, heads)), head_dim)
    grow_ref[0, 0] = jnp.exp(cum)


def norm_kernel(place_ref, state_ref, c_ref, grow_ref, y_ref, gate_ref, gain_ref, out_ref):
    width = y_ref.shape[2]
    heads = grow_ref.shape[3]
    from_state = jnp.dot(c_ref[0, 0], state_ref[0, 0], preferred_element_type=jnp.float32)
    ssd_out = y_ref[0] + from_state * spread(grow_ref[0, 0], width // heads)
    gate = gate_ref[0].astype(jnp.float32)
    gated = ssd_out * (gate / (1.0 + jnp.exp(-gate)))
    scale = lax.rsqrt(jnp.mean(gated * gated, axis=1, keepdims=True) + norm_eps)
    out_ref[0] = (gated * scale * gain_ref[0]).astype(jnp.bfloat16)


def local_part(limits, x, b, c, raw, bias, rate, skip):
    sessions, tokens, inner = x.shape
    groups = b.shape[1]
    state = b.shape[3]
    heads = raw.shape[3]
    width = inner // groups

    def by_group(*block):
        return pl.BlockSpec((1, *block), lambda s, g, _: (g, 0, 0))

    def by_both(*block):
        return pl.BlockSpec((1, 1, *block), lambda s, g, _: (s, g, 0, 0))

    def by_turn(*block):
        return pl.BlockSpec((1, 1, *block), lambda s, g, _: (g, s, 0, 0))

    flat = pl.BlockSpec((1, tokens, width), lambda s, g, _: (s, 0, g))
    f32 = jnp.float32
    return pl.pallas_call(
        local_kernel,
        grid_spec=pltpu.PrefetchScalarGridSpec(
            num_scalar_prefetch=1,
            grid=(sessions, groups),
            in_specs=[
                flat,
                by_both(tokens, state),
                by_both(tokens, state),
                by_both(tokens, heads),
                by_both(heads, tokens),
                by_group(1, heads),
                by_group(heads, 1),
                by_group(1, heads),
                by_group(heads, 1),
                by_group(1, width),
            ],
            out_specs=[
                flat,
                by_turn(state, width),
                by_turn(8, width),
                by_both(tokens, heads),
            ],
        ),
        out_shape=[
            jax.ShapeDtypeStruct((sessions, tokens, inner), f32),
            jax.ShapeDtypeStruct((groups, sessions, state, width), f32),
            jax.ShapeDtypeStruct((groups, sessions, 8, width), f32),
            jax.ShapeDtypeStruct((sessions, groups, tokens, heads), f32),
        ],
        compiler_params=pltpu.CompilerParams(vmem_limit_bytes=32 * 1024 * 1024),
        cost_estimate=pl.CostEstimate(
            flops=4 * 10**9, bytes_accessed=14 * 2**20, transcendentals=2**22
        ),
        name="local_part",
    )(
        limits,
        x,
        b,
        c,
        raw,
        raw.swapaxes(2, 3),
        bias[:, None, :],
        bias[:, :, None],
        rate[:, None, :],
        rate[:, :, None],
        skip,
    )


def normed_part(places, states, c, grow, y, gate, gain):
    sessions, tokens, inner = y.shape
    groups = c.shape[1]
    state = c.shape[3]
    heads = grow.shape[3]
    width = inner // groups
    flat = pl.BlockSpec((1, tokens, width), lambda s, g, _: (s, 0, g))
    return pl.pallas_call(
        norm_kernel,
        grid_spec=pltpu.PrefetchScalarGridSpec(
            num_scalar_prefetch=1,
            grid=(sessions, groups),
            in_specs=[
                pl.BlockSpec((1, 1, state, width), lambda s, g, place: (place[g], s, 0, 0)),
                pl.BlockSpec((1, 1, tokens, state), lambda s, g, _: (s, g, 0, 0)),
                pl.BlockSpec((1, 1, tokens, heads), lambda s, g, _: (s, g, 0, 0)),
                flat,
                flat,
                pl.BlockSpec((1, 1, width), lambda s, g, _: (g, 0, 0)),
            ],
            out_specs=flat,
        ),
        out_shape=jax.ShapeDtypeStruct((sessions, tokens, inner), jnp.bfloat16),
        compiler_params=pltpu.CompilerParams(vmem_limit_bytes=32 * 1024 * 1024),
        cost_estimate=pl.CostEstimate(
            flops=5 * 10**8, bytes_accessed=12 * 2**20, transcendentals=2**21
        ),
        name="normed_part",
    )(places, states, c, grow, y, gate, gain)


def shards(
    head_input,
    gate_input,
    state_in_proj,
    state_out_proj,
    step_raw,
    head_step_bias,
    decay_log,
    skip_gain,
    norm_gain,
    out_weight,
    pool_states,
    slot_map,
    span_lengths,
):
    turns = lax.axis_size("ctx")
    turn = lax.axis_index("ctx")
    lanes = lax.axis_size("groups")
    lane = lax.axis_index("groups")
    cores = lax.axis_size("sess")
    core = lax.axis_index("sess")
    head_count = lax.axis_size("head")
    head_index = lax.axis_index("head")
    sessions, tokens, inner = head_input.shape
    heads = step_raw.shape[2]
    head_dim = inner // heads
    slots = pool_states.shape[0]
    state_cols = pool_states.shape[3]
    groups = heads // GROUP_HEADS
    width = inner // groups
    bf16 = jnp.bfloat16

    def columns_of(slot):
        held = lax.dynamic_index_in_dim(pool_states, slot % slots, 0, keepdims=False)
        held = held.astype(bf16).transpose(2, 0, 1)
        return held.reshape(state_cols, groups, width).transpose(1, 0, 2)

    def slots_of(which):
        return lax.dynamic_slice_in_dim(slot_map, which * sessions, sessions)

    own_slots = slots_of(core)
    start = jnp.zeros((groups, sessions, state_cols, width), bf16)
    for by in range(cores):
        asked = slots_of((core - by) % cores)
        found = jnp.stack([columns_of(asked[s]) for s in range(sessions)], axis=1)
        if by:
            found = lax.ppermute(found, "sess", [(i, (i - by) % cores) for i in range(cores)])
            holder = (core + by) % cores
        else:
            holder = core
        here = (own_slots // slots == holder)[None, :, None, None]
        start = jnp.where(here, found, start)
    columns = [start]
    for other in range(1, turns):
        columns.append(lax.ppermute(start, "ctx", [(other, 0)]))
    first_state = jnp.concatenate(columns, axis=2)

    carriers = lanes * cores
    rows = inner // carriers
    carrier = lane * cores + core
    mine = lax.dynamic_slice_in_dim(out_weight, carrier * rows, rows, 0)
    piece_rows = rows // PIECES

    def share(block, holders):
        got = {(0, 0): block}
        for by in range(1, lanes):
            pairs = [
                (y * turns + z, (y - by) % lanes * turns + z) for y in range(lanes) for z in holders
            ]
            got[by, 0] = lax.ppermute(block, ("groups", "ctx"), pairs)
        for by_lane in range(lanes):
            for by in range(1, cores):
                pairs = [
                    (z * cores + c, z * cores + (c - by) % cores)
                    for z in holders
                    for c in range(cores)
                ]
                got[by_lane, by] = lax.ppermute(got[by_lane, 0], ("ctx", "sess"), pairs)
        return got

    up = {}
    down = {}
    for piece in range(PIECES):
        block = mine[piece * piece_rows : (piece + 1) * piece_rows]
        ahead = back = block
        for hop in range(1, turns):
            ahead = lax.ppermute(ahead, "ctx", [(i, i + 1) for i in range(hop - 1, turns - 1)])
            back = lax.ppermute(back, "ctx", [(i + 1, i) for i in range(turns - hop)])
            up[hop, piece] = share(ahead, range(hop, turns))
            down[hop, piece] = share(back, range(turns - hop))

    first_session = core * sessions
    own_lengths = lax.dynamic_slice_in_dim(span_lengths, first_session, sessions)
    limits = jnp.clip(own_lengths * SPAN - turn * tokens, 0, tokens)
    first_group = head_index * groups

    def grouped(proj):
        return lax.dynamic_slice_in_dim(proj, first_group, groups, 2).swapaxes(1, 2)

    b = grouped(state_in_proj)
    c = grouped(state_out_proj)
    raw = step_raw.reshape(sessions, tokens, groups, GROUP_HEADS).swapaxes(1, 2)
    skip = jnp.repeat(skip_gain, head_dim).reshape(groups, 1, width)
    y, local_end, keep, grow = local_part(
        limits,
        head_input,
        b,
        c,
        raw,
        head_step_bias.reshape(groups, GROUP_HEADS),
        decay_log.reshape(groups, GROUP_HEADS),
        skip,
    )

    waves = groups + turns - 2
    arrived = []
    coming = first_state[0]
    for wave in range(waves):
        at = jnp.clip(wave - turn, 0, groups - 1)
        if wave < groups:
            coming = jnp.where(turn == 0, first_state[wave], coming)
        gone = lax.dynamic_index_in_dim(keep, at, 0, keepdims=False)[:, :1]
        added = lax.dynamic_index_in_dim(local_end, at, 0, keepdims=False)
        leaving = (gone * coming.astype(jnp.float32) + added).astype(bf16)
        pairs = [(i, i + 1) for i in range(turns - 1) if 0 <= wave - i < groups]
        coming = lax.ppermute(leaving, "ctx", pairs)
        arrived.append(coming)
    states = jnp.concatenate([first_state, jnp.stack(arrived)], axis=0)
    places = jnp.arange(groups, dtype=jnp.int32)
    places = places + jnp.where(turn == 0, 0, groups + turn - 1)

    own_states = lax.dynamic_slice_in_dim(states, places[0], groups, 0)
    ended = (keep[:, :, :1] * own_states.astype(jnp.float32) + local_end).astype(bf16)
    final = ended[:, :, (turns - 1) * state_cols :]
    for other in range(turns - 1):
        part = ended[:, :, other * state_cols : (other + 1) * state_cols]
        part = lax.ppermute(part, "ctx", [(turns - 1, other)])
        final = jnp.where(turn == other, part, final)
    final = final.transpose(1, 2, 0, 3).reshape(sessions, state_cols, heads, head_dim)
    final_states = final.astype(jnp.float32).transpose(0, 2, 3, 1)

    normed = normed_part(
        places, states, c, grow, y, gate_input, norm_gain.reshape(groups, 1, width)
    ).reshape(sessions * tokens, inner)

    def product(parts):
        total = 0.0
        for by_lane in range(lanes):
            for by in range(cores):
                owner = (lane + by_lane) % lanes * cores + (core + by) % cores
                for piece in range(PIECES):
                    at = owner * rows + piece * piece_rows
                    left = lax.dynamic_slice_in_dim(normed, at, piece_rows, 1)
                    total = total + jnp.dot(
                        left, parts[piece][by_lane, by], preferred_element_type=jnp.float32
                    )
        return total

    blocks = [jnp.dot(normed, out_weight, preferred_element_type=jnp.float32).astype(bf16)]
    for by in range(1, turns):
        from_up = product([up[turns - by, piece] for piece in range(PIECES)])
        from_down = product([down[by, piece] for piece in range(PIECES)])
        blocks.append(jnp.where(turn + by < turns, from_down, from_up).astype(bf16))
    blocks = jnp.stack(blocks)
    blocks = lax.dynamic_slice_in_dim(
        jnp.concatenate([blocks, blocks], axis=0), (turns - turn) % turns, turns, 0
    )
    partial = blocks.transpose(1, 0, 2).reshape(sessions, tokens, -1)
    if head_count == 2:
        share_cols = partial.shape[2] // 2
        halves = partial.reshape(sessions, tokens, 2, share_cols)
        other = lax.dynamic_index_in_dim(halves, 1 - head_index, 2, keepdims=False)
        own = lax.dynamic_index_in_dim(halves, head_index, 2, keepdims=False)
        other = lax.ppermute(other, "head", [(0, 1), (1, 0)])
        summed = own.astype(jnp.float32) + other.astype(jnp.float32)
    else:
        summed = lax.psum_scatter(partial, "head", scatter_dimension=2, tiled=True).astype(
            jnp.float32
        )
    live = (jnp.arange(tokens, dtype=jnp.int32)[None, :] < limits[:, None]).astype(jnp.float32)
    mixed = (summed * live[:, :, None]).astype(bf16)
    return (mixed, final_states)


def solution(mesh):
    placed = (
        P(("groups", "sess"), "ctx", "head"),
        P(("groups", "sess"), "ctx", "head"),
        P(("groups", "sess"), "ctx", None, None),
        P(("groups", "sess"), "ctx", None, None),
        P(("groups", "sess"), "ctx", "head"),
        P("head"),
        P("head"),
        P("head"),
        P("head"),
        P("head", "ctx"),
        P(("groups", "sess"), "head", None, "ctx"),
        P("groups"),
        P("groups"),
    )
    return jax.shard_map(
        shards,
        mesh=mesh,
        in_specs=placed,
        out_specs=(
            P(("groups", "sess"), "ctx", "head"),
            P(("groups", "sess"), "head", None, "ctx"),
        ),
        check_vma=False,
    )
```

time: 941 us -> 557 us (0.59)
  the two profiles are of different devices: /device:TPU:12 before, /device:TPU:0 now
where the time goes in v1:
time: 557 us; the launch traced here: 546 us
  starting transfers between devices  226 us (41%)
  waiting for transfers between devices  195 us (35%)
  local copies, waits for them, and re-layouts  45.4 us (8%)
  matrix products  36.1 us (6%)
  other arithmetic  17.6 us (3%)
  Pallas kernels  15.3 us (3%)
  between operations  10.7 us (2%)
    ppermute x12, starting transfers between devices, share(): got[by, 0] = lax.ppermute(block, ('groups', 'ctx'), pairs)  94.9 us
    ppermute x6, waiting for transfers between devices, shards(): back = lax.ppermute(back, 'ctx', [(i + 1, i) for i in range(turns - hop)])  74.7 us
    ppermute x24, starting transfers between devices, share(): got[by_lane, by] = lax.ppermute(got[by_lane, 0], ('ctx', 'sess'), pairs)  66.2 us
    ppermute x12, waiting for transfers between devices, share(): got[by, 0] = lax.ppermute(block, ('groups', 'ctx'), pairs)  52.1 us
    ppermute x3, waiting for transfers between devices, shards(): part = lax.ppermute(part, 'ctx', [(turns - 1, other)])  38.1 us
    dot_general x48, matrix products, product(): jnp.dot(left, parts[piece][by_lane, by], preferred_element_type=jnp.float32)  30.3 us
    ppermute x3, waiting for transfers between devices, shards(): columns.append(lax.ppermute(start, 'ctx', [(other, 0)]))  19.5 us
    unnamed x65, local copies, waits for them, and re-layouts  17.8 us
  transfers between devices with their start and end apart: 62, of which 12 were waited for; matrix products, arithmetic and copies ran while one was open for 11% of the time, Pallas kernels for 3%

profile of v1, /device:TPU:0, one launch (start us, length us, event | category | flops | bytes accessed | tf_op | source)
XLA Modules:
  0.0 546.3 jit_solution(9618508066606036499)
XLA Ops:
  13.5 7.1 %collective-permute-start = (bf16[4,2,32,1024]{3,2,1,0:T(8,128)(2,1)S(1)}, bf16[4,2,32,1024]{3,2,1,0:T(8,128)(2,1)S(1)}, u32[]{:S(2)}, u32[]{:S(2)}) collective-permute-start(bf16[4,2,32,1024]{3,2,1,0:T(8,128)(2,1)S(1)} %pad_maximum_fusion.1), channel_id=1, source_target_pairs={{0,1},{1,0},{2,3},{3,2},{4,5},{5,4},{6,7},{7,6},{8,9},{9,8},{10,11... | collective-permute-start | bytes 1572872 | tf_op jit(solution)/shard_map/ppermute | solution.py:255
  32.2 10.3 %local_part.1 = (f32[2,128,4096]{2,1,0:T(8,128)S(1)}, f32[4,2,128,1024]{3,2,1,0:T(8,128)S(1)}, f32[4,2,8,1024]{3,2,1,0:T(8,128)S(1)}, f32[2,4,128,16]{3,2,1,0:T(8,128)S(1)}) custom-call(s32[2]{0:T(128)S(1)} %subtract_clamp_fusion.limit_ref, bf16[2,128,4096]{2,1,0:T(8,128)(2,1)S(1)} %copy-done.9, bf16[2,4,128,128]{3,2,1,0:T(8,128)(2,1)S(1)} %bitcast.268, ...), custom_call_target="tpu_custom_call" | custom-call | flops 4000000000 | bytes 14680064 | tf_op jit(solution)/shard_map/local_part/pallas_call | solution.py:128
  44.6 19.5 %collective-permute-done.1 = bf16[4,2,32,1024]{3,2,1,0:T(8,128)(2,1)S(1)} collective-permute-done((bf16[4,2,32,1024]{3,2,1,0:T(8,128)(2,1)S(1)}, bf16[4,2,32,1024]{3,2,1,0:T(8,128)(2,1)S(1)}, u32[]{:S(2)}, u32[]{:S(2)}) %collective-permute-start.1) | collective-permute-done | bytes 524320 | tf_op jit(solution)/shard_map/ppermute | solution.py:263
  64.9 3.2 pad_maximum_fusion
  71.4 10.5 %collective-permute-done.4 = bf16[2,128,1024]{2,1,0:T(8,128)(2,1)} collective-permute-done((bf16[2,128,1024]{2,1,0:T(8,128)(2,1)}, bf16[2,128,1024]{2,1,0:T(8,128)(2,1)}, u32[]{:S(2)}, u32[]{:S(2)}) %collective-permute-start.4) | collective-permute-done | bytes 524320 | tf_op jit(solution)/shard_map/ppermute | solution.py:334
  83.3 4.8 collective-permute-start.5
  94.3 8.0 %collective-permute-start.10 = (bf16[512,1024]{1,0:T(8,128)(2,1)}, bf16[512,1024]{1,0:T(8,128)(2,1)}, u32[]{:S(2)}, u32[]{:S(2)}) collective-permute-start(bf16[512,1024]{1,0:T(8,128)(2,1)} %get-tuple-element.14), channel_id=1, source_target_pairs={{4,0},{8,4},{12,8},{5,1},{9,5},{13,9},{6,2},{10,6},{14,10},{7,3},{... | collective-permute-start | bytes 3145736 | tf_op jit(solution)/shard_map/ppermute | solution.py:296
  102.6 4.5 collective-permute-start.6
  107.1 14.0 %collective-permute-done.11 = bf16[512,1024]{1,0:T(8,128)(2,1)} collective-permute-done((bf16[512,1024]{1,0:T(8,128)(2,1)}, bf16[512,1024]{1,0:T(8,128)(2,1)}, u32[]{:S(2)}, u32[]{:S(2)}) %collective-permute-start.11) | collective-permute-done | bytes 1048608 | tf_op jit(solution)/shard_map/ppermute | solution.py:296
  122.3 5.5 %collective-permute-start.21 = (bf16[512,1024]{1,0:T(8,128)(2,1)}, bf16[512,1024]{1,0:T(8,128)(2,1)}, u32[]{:S(2)}, u32[]{:S(2)}) collective-permute-start(bf16[512,1024]{1,0:T(8,128)(2,1)} %get-tuple-element.15), channel_id=1, source_target_pairs={{0,4},{4,8},{8,12},{1,5},{5,9},{9,13},{2,6},{6,10},{10,14},{3,7},{... | collective-permute-start | bytes 3145736 | tf_op jit(solution)/shard_map/ppermute | solution.py:295
  129.0 3.4 collective-permute-start.7
  132.4 11.1 %collective-permute-done.10 = bf16[512,1024]{1,0:T(8,128)(2,1)} collective-permute-done((bf16[512,1024]{1,0:T(8,128)(2,1)}, bf16[512,1024]{1,0:T(8,128)(2,1)}, u32[]{:S(2)}, u32[]{:S(2)}) %collective-permute-start.10) | collective-permute-done | bytes 1048608 | tf_op jit(solution)/shard_map/ppermute | solution.py:296
  144.8 5.5 %collective-permute-start.18 = (bf16[512,1024]{1,0:T(8,128)(2,1)}, bf16[512,1024]{1,0:T(8,128)(2,1)}, u32[]{:S(2)}, u32[]{:S(2)}) collective-permute-start(bf16[512,1024]{1,0:T(8,128)(2,1)} %get-tuple-element.14), channel_id=1, source_target_pairs={{0,4},{4,8},{8,12},{1,5},{5,9},{9,13},{2,6},{6,10},{10,14},{3,7},{... | collective-permute-start | bytes 3145736 | tf_op jit(solution)/shard_map/ppermute | solution.py:295
  150.4 15.6 %collective-permute-done.31 = bf16[512,1024]{1,0:T(8,128)(2,1)} collective-permute-done((bf16[512,1024]{1,0:T(8,128)(2,1)}, bf16[512,1024]{1,0:T(8,128)(2,1)}, u32[]{:S(2)}, u32[]{:S(2)}) %collective-permute-start.31) | collective-permute-done | bytes 1048608 | tf_op jit(solution)/shard_map/ppermute | solution.py:296
  172.4 16.0 %collective-permute-done.30 = bf16[512,1024]{1,0:T(8,128)(2,1)} collective-permute-done((bf16[512,1024]{1,0:T(8,128)(2,1)}, bf16[512,1024]{1,0:T(8,128)(2,1)}, u32[]{:S(2)}, u32[]{:S(2)}) %collective-permute-start.30) | collective-permute-done | bytes 1048608 | tf_op jit(solution)/shard_map/ppermute | solution.py:296
  193.9 17.1 %collective-permute-done.45 = bf16[512,1024]{1,0:T(8,128)(2,1)} collective-permute-done((bf16[512,1024]{1,0:T(8,128)(2,1)}, bf16[512,1024]{1,0:T(8,128)(2,1)}, u32[]{:S(2)}, u32[]{:S(2)}) %collective-permute-start.45) | collective-permute-done | bytes 1048608 | tf_op jit(solution)/shard_map/ppermute | solution.py:296
  214.6 3.4 collective-permute-start.49
  221.3 5.1 normed_part.1
  232.8 6.2 %collective-permute-start.54 = (bf16[512,1024]{1,0:T(8,128)(2,1)}, bf16[512,1024]{1,0:T(8,128)(2,1)S(1)}, u32[]{:S(2)}, u32[]{:S(2)}) collective-permute-start(bf16[512,1024]{1,0:T(8,128)(2,1)} %collective-permute-done.18), channel_id=1, source_target_pairs={{4,20},{8,24},{12,28},{20,4},{24,8},{28,12},{5,21},{9,25},{13,29},... | collective-permute-start | bytes 3145736 | tf_op jit(solution)/shard_map/ppermute | solution.py:278
  239.1 3.8 collective-permute-start.48
  247.1 19.3 %collective-permute-done.48 = bf16[512,1024]{1,0:T(8,128)(2,1)S(1)} collective-permute-done((bf16[512,1024]{1,0:T(8,128)(2,1)S(1)}, bf16[512,1024]{1,0:T(8,128)(2,1)S(1)}, u32[]{:S(2)}, u32[]{:S(2)}) %collective-permute-start.48) | collective-permute-done | bytes 1048608 | tf_op jit(solution)/shard_map/ppermute | solution.py:278
  276.2 3.6 collective-permute-start.35
  292.4 11.9 %collective-permute-done.35 = bf16[512,1024]{1,0:T(8,128)(2,1)S(1)} collective-permute-done((bf16[512,1024]{1,0:T(8,128)(2,1)}, bf16[512,1024]{1,0:T(8,128)(2,1)S(1)}, u32[]{:S(2)}, u32[]{:S(2)}) %collective-permute-start.35) | collective-permute-done | bytes 1048608 | tf_op jit(solution)/shard_map/ppermute | solution.py:278
  305.4 20.9 %collective-permute-done.34 = bf16[512,1024]{1,0:T(8,128)(2,1)S(1)} collective-permute-done((bf16[512,1024]{1,0:T(8,128)(2,1)}, bf16[512,1024]{1,0:T(8,128)(2,1)S(1)}, u32[]{:S(2)}, u32[]{:S(2)}) %collective-permute-start.34) | collective-permute-done | bytes 1048608 | tf_op jit(solution)/shard_map/ppermute | solution.py:278
  328.7 29.5 %collective-permute-start.15 = (bf16[512,1024]{1,0:T(8,128)(2,1)}, bf16[512,1024]{1,0:T(8,128)(2,1)S(1)}, u32[]{:S(2)}, u32[]{:S(2)}) collective-permute-start(bf16[512,1024]{1,0:T(8,128)(2,1)} %collective-permute-done.11), channel_id=1, source_target_pairs={{0,16},{4,20},{8,24},{16,0},{20,4},{24,8},{1,17},{5,21},{9,25},{17... | collective-permute-start | bytes 3145736 | tf_op jit(solution)/shard_map/ppermute | solution.py:278
  361.1 40.8 %collective-permute-start.14 = (bf16[512,1024]{1,0:T(8,128)(2,1)}, bf16[512,1024]{1,0:T(8,128)(2,1)S(1)}, u32[]{:S(2)}, u32[]{:S(2)}) collective-permute-start(bf16[512,1024]{1,0:T(8,128)(2,1)} %collective-permute-done.10), channel_id=1, source_target_pairs={{0,16},{4,20},{8,24},{16,0},{20,4},{24,8},{1,17},{5,21},{9,25},{17... | collective-permute-start | bytes 3145736 | tf_op jit(solution)/shard_map/ppermute | solution.py:278
  407.5 5.8 %constant_dynamic-update-slice_fusion.8 = (bf16[8,256,1024]{2,1,0:T(8,128)(2,1)S(1)}, bf16[1,256,1024]{2,1,0:T(8,128)(2,1)S(1)}) fusion(bf16[256,4096]{1,0:T(8,128)(2,1)S(1)} %bitcast.245, bf16[4096,1024]{1,0:T(8,128)(2,1)} %param.22), kind=kOutput, calls=%fused_computation.199 | convolution fusion | flops 2147745792 | bytes 11534336 | tf_op jit(solution)/shard_map/dot_general | solution.py:367
  416.1 32.5 %collective-permute-start.57 = (bf16[512,1024]{1,0:T(8,128)(2,1)S(1)}, bf16[512,1024]{1,0:T(8,128)(2,1)S(1)}, u32[]{:S(2)}, u32[]{:S(2)}) collective-permute-start(bf16[512,1024]{1,0:T(8,128)(2,1)S(1)} %collective-permute-done.55), channel_id=1, source_target_pairs={{4,5},{5,4},{8,9},{9,8},{12,13},{13,12},{6,7},{7,6},{10,11},{11,10... | collective-permute-start | bytes 3145736 | tf_op jit(solution)/shard_map/ppermute | solution.py:286
  478.7 4.0 copy.37
  482.7 4.0 reshape_reshape.4
  489.2 4.8 collective-permute-start.58
  498.0 38.1 %collective-permute-done.61 = bf16[4,2,32,1024]{3,2,1,0:T(8,128)(2,1)} collective-permute-done((bf16[4,2,32,1024]{3,2,1,0:T(8,128)(2,1)}, bf16[4,2,32,1024]{3,2,1,0:T(8,128)(2,1)}, u32[]{:S(2)}, u32[]{:S(2)}) %collective-permute-start.61) | collective-permute-done | bytes 524320 | tf_op jit(solution)/shard_map/ppermute | solution.py:345
  (267 shorter events, 146.0 us)
Async XLA Ops:
  25.6 38.6 %collective-permute-start.1 = (bf16[4,2,32,1024]{3,2,1,0:T(8,128)(2,1)S(1)}, bf16[4,2,32,1024]{3,2,1,0:T(8,128)(2,1)S(1)}, u32[]{:S(2)}, u32[]{:S(2)}) collective-permute-start(bf16[4,2,32,1024]{3,2,1,0:T(8,128)(2,1)S(1)} %fusion.52), channel_id=1, source_target_pairs={{4,0},{5,1},{6,2},{7,3},{20,16},{21,17},{22,18},{23,19}} | collective-permute-start | bytes 1572872 | tf_op jit(solution)/shard_map/ppermute | solution.py:263
  26.9 37.3 %collective-permute-start.2 = (bf16[4,2,32,1024]{3,2,1,0:T(8,128)(2,1)S(1)}, bf16[4,2,32,1024]{3,2,1,0:T(8,128)(2,1)}, u32[]{:S(2)}, u32[]{:S(2)}) collective-permute-start(bf16[4,2,32,1024]{3,2,1,0:T(8,128)(2,1)S(1)} %fusion.52), channel_id=1, source_target_pairs={{8,0},{9,1},{10,2},{11,3},{24,16},{25,17},{26,18},{27,19}} | collective-permute-start | bytes 1572872 | tf_op jit(solution)/shard_map/ppermute | solution.py:263
  28.2 36.8 %collective-permute-start.3 = (bf16[4,2,32,1024]{3,2,1,0:T(8,128)(2,1)S(1)}, bf16[4,2,32,1024]{3,2,1,0:T(8,128)(2,1)}, u32[]{:S(2)}, u32[]{:S(2)}) collective-permute-start(bf16[4,2,32,1024]{3,2,1,0:T(8,128)(2,1)S(1)} %fusion.52), channel_id=1, source_target_pairs={{12,0},{13,1},{14,2},{15,3},{28,16},{29,17},{30,18},{31,19}} | collective-permute-start | bytes 1572872 | tf_op jit(solution)/shard_map/ppermute | solution.py:263
  94.3 49.2 %collective-permute-start.10 = (bf16[512,1024]{1,0:T(8,128)(2,1)}, bf16[512,1024]{1,0:T(8,128)(2,1)}, u32[]{:S(2)}, u32[]{:S(2)}) collective-permute-start(bf16[512,1024]{1,0:T(8,128)(2,1)} %get-tuple-element.14), channel_id=1, source_target_pairs={{4,0},{8,4},{12,8},{5,1},{9,5},{13,9},{6,2},{10,6},{14,10},{7,3},{... | collective-permute-start | bytes 3145736 | tf_op jit(solution)/shard_map/ppermute | solution.py:296
  121.1 44.9 %collective-permute-start.31 = (bf16[512,1024]{1,0:T(8,128)(2,1)}, bf16[512,1024]{1,0:T(8,128)(2,1)}, u32[]{:S(2)}, u32[]{:S(2)}) collective-permute-start(bf16[512,1024]{1,0:T(8,128)(2,1)} %collective-permute-done.11), channel_id=1, source_target_pairs={{4,0},{8,4},{5,1},{9,5},{6,2},{10,6},{7,3},{11,7},{20,16},{24,20},... | collective-permute-start | bytes 3145736 | tf_op jit(solution)/shard_map/ppermute | solution.py:296
  122.3 47.4 %collective-permute-start.21 = (bf16[512,1024]{1,0:T(8,128)(2,1)}, bf16[512,1024]{1,0:T(8,128)(2,1)}, u32[]{:S(2)}, u32[]{:S(2)}) collective-permute-start(bf16[512,1024]{1,0:T(8,128)(2,1)} %get-tuple-element.15), channel_id=1, source_target_pairs={{0,4},{4,8},{8,12},{1,5},{5,9},{9,13},{2,6},{6,10},{10,14},{3,7},{... | collective-permute-start | bytes 3145736 | tf_op jit(solution)/shard_map/ppermute | solution.py:295
  129.0 38.3 %collective-permute-start.7 = (bf16[2,128,1024]{2,1,0:T(8,128)(2,1)}, bf16[2,128,1024]{2,1,0:T(8,128)(2,1)S(1)}, u32[]{:S(2)}, u32[]{:S(2)}) collective-permute-start(bf16[2,128,1024]{2,1,0:T(8,128)(2,1)} %fusion.40), channel_id=1, source_target_pairs={{0,4},{4,8},{8,12},{1,5},{5,9},{9,13},{2,6},{6,10},{10,14},{3,7},{... | collective-permute-start | bytes 1572872 | tf_op jit(solution)/shard_map/ppermute | solution.py:334
  143.5 44.9 %collective-permute-start.30 = (bf16[512,1024]{1,0:T(8,128)(2,1)}, bf16[512,1024]{1,0:T(8,128)(2,1)}, u32[]{:S(2)}, u32[]{:S(2)}) collective-permute-start(bf16[512,1024]{1,0:T(8,128)(2,1)} %collective-permute-done.10), channel_id=1, source_target_pairs={{4,0},{8,4},{5,1},{9,5},{6,2},{10,6},{7,3},{11,7},{20,16},{24,20},... | collective-permute-start | bytes 3145736 | tf_op jit(solution)/shard_map/ppermute | solution.py:296
  144.8 83.2 %collective-permute-start.18 = (bf16[512,1024]{1,0:T(8,128)(2,1)}, bf16[512,1024]{1,0:T(8,128)(2,1)}, u32[]{:S(2)}, u32[]{:S(2)}) collective-permute-start(bf16[512,1024]{1,0:T(8,128)(2,1)} %get-tuple-element.14), channel_id=1, source_target_pairs={{0,4},{4,8},{8,12},{1,5},{5,9},{9,13},{2,6},{6,10},{10,14},{3,7},{... | collective-permute-start | bytes 3145736 | tf_op jit(solution)/shard_map/ppermute | solution.py:295
  166.0 44.9 %collective-permute-start.45 = (bf16[512,1024]{1,0:T(8,128)(2,1)}, bf16[512,1024]{1,0:T(8,128)(2,1)}, u32[]{:S(2)}, u32[]{:S(2)}) collective-permute-start(bf16[512,1024]{1,0:T(8,128)(2,1)} %collective-permute-done.31), channel_id=1, source_target_pairs={{4,0},{5,1},{6,2},{7,3},{20,16},{21,17},{22,18},{23,19}} | collective-permute-start | bytes 3145736 | tf_op jit(solution)/shard_map/ppermute | solution.py:296
  169.7 73.6 %collective-permute-start.53 = (bf16[512,1024]{1,0:T(8,128)(2,1)}, bf16[512,1024]{1,0:T(8,128)(2,1)S(1)}, u32[]{:S(2)}, u32[]{:S(2)}) collective-permute-start(bf16[512,1024]{1,0:T(8,128)(2,1)} %collective-permute-done.21), channel_id=1, source_target_pairs={{4,5},{5,4},{8,9},{9,8},{12,13},{13,12},{6,7},{7,6},{10,11},{11,10... | collective-permute-start | bytes 3145736 | tf_op jit(solution)/shard_map/ppermute | solution.py:286
  188.5 44.4 %collective-permute-start.44 = (bf16[512,1024]{1,0:T(8,128)(2,1)}, bf16[512,1024]{1,0:T(8,128)(2,1)S(1)}, u32[]{:S(2)}, u32[]{:S(2)}) collective-permute-start(bf16[512,1024]{1,0:T(8,128)(2,1)} %collective-permute-done.30), channel_id=1, source_target_pairs={{4,0},{5,1},{6,2},{7,3},{20,16},{21,17},{22,18},{23,19}} | collective-permute-start | bytes 3145736 | tf_op jit(solution)/shard_map/ppermute | solution.py:296
  214.6 30.1 %collective-permute-start.49 = (bf16[512,1024]{1,0:T(8,128)(2,1)}, bf16[512,1024]{1,0:T(8,128)(2,1)S(1)}, u32[]{:S(2)}, u32[]{:S(2)}) collective-permute-start(bf16[512,1024]{1,0:T(8,128)(2,1)} %collective-permute-done.45), channel_id=1, source_target_pairs={{0,16},{16,0},{1,17},{17,1},{2,18},{18,2},{3,19},{19,3}} | collective-permute-start | bytes 3145736 | tf_op jit(solution)/shard_map/ppermute | solution.py:278
  232.8 35.9 %collective-permute-start.54 = (bf16[512,1024]{1,0:T(8,128)(2,1)}, bf16[512,1024]{1,0:T(8,128)(2,1)S(1)}, u32[]{:S(2)}, u32[]{:S(2)}) collective-permute-start(bf16[512,1024]{1,0:T(8,128)(2,1)} %collective-permute-done.18), channel_id=1, source_target_pairs={{4,20},{8,24},{12,28},{20,4},{24,8},{28,12},{5,21},{9,25},{13,29},... | collective-permute-start | bytes 3145736 | tf_op jit(solution)/shard_map/ppermute | solution.py:278
  243.3 32.9 %collective-permute-start.52 = (bf16[512,1024]{1,0:T(8,128)(2,1)}, bf16[512,1024]{1,0:T(8,128)(2,1)S(1)}, u32[]{:S(2)}, u32[]{:S(2)}) collective-permute-start(bf16[512,1024]{1,0:T(8,128)(2,1)} %collective-permute-done.18), channel_id=1, source_target_pairs={{4,5},{5,4},{8,9},{9,8},{12,13},{13,12},{6,7},{7,6},{10,11},{11,10... | collective-permute-start | bytes 3145736 | tf_op jit(solution)/shard_map/ppermute | solution.py:286
  244.7 35.1 %collective-permute-start.22 = (bf16[512,1024]{1,0:T(8,128)(2,1)}, bf16[512,1024]{1,0:T(8,128)(2,1)S(1)}, u32[]{:S(2)}, u32[]{:S(2)}) collective-permute-start(bf16[512,1024]{1,0:T(8,128)(2,1)} %collective-permute-done.21), channel_id=1, source_target_pairs={{4,8},{8,12},{5,9},{9,13},{6,10},{10,14},{7,11},{11,15},{20,24},{2... | collective-permute-start | bytes 3145736 | tf_op jit(solution)/shard_map/ppermute | solution.py:295
  245.9 34.6 %collective-permute-start.19 = (bf16[512,1024]{1,0:T(8,128)(2,1)}, bf16[512,1024]{1,0:T(8,128)(2,1)S(1)}, u32[]{:S(2)}, u32[]{:S(2)}) collective-permute-start(bf16[512,1024]{1,0:T(8,128)(2,1)} %collective-permute-done.18), channel_id=1, source_target_pairs={{4,8},{8,12},{5,9},{9,13},{6,10},{10,14},{7,11},{11,15},{20,24},{2... | collective-permute-start | bytes 3145736 | tf_op jit(solution)/shard_map/ppermute | solution.py:295
  268.8 184.9 %collective-permute-start.13 = (bf16[512,1024]{1,0:T(8,128)(2,1)}, bf16[512,1024]{1,0:T(8,128)(2,1)S(1)}, u32[]{:S(2)}, u32[]{:S(2)}) collective-permute-start(bf16[512,1024]{1,0:T(8,128)(2,1)} %collective-permute-done.11), channel_id=1, source_target_pairs={{0,1},{1,0},{4,5},{5,4},{8,9},{9,8},{2,3},{3,2},{6,7},{7,6},{10,11... | collective-permute-start | bytes 3145736 | tf_op jit(solution)/shard_map/ppermute | solution.py:286
  286.0 40.3 %collective-permute-start.34 = (bf16[512,1024]{1,0:T(8,128)(2,1)}, bf16[512,1024]{1,0:T(8,128)(2,1)S(1)}, u32[]{:S(2)}, u32[]{:S(2)}) collective-permute-start(bf16[512,1024]{1,0:T(8,128)(2,1)} %collective-permute-done.30), channel_id=1, source_target_pairs={{0,16},{4,20},{16,0},{20,4},{1,17},{5,21},{17,1},{21,5},{2,18},{6,... | collective-permute-start | bytes 3145736 | tf_op jit(solution)/shard_map/ppermute | solution.py:278
  288.8 38.7 %collective-permute-start.39 = (bf16[512,1024]{1,0:T(8,128)(2,1)S(1)}, bf16[512,1024]{1,0:T(8,128)(2,1)S(1)}, u32[]{:S(2)}, u32[]{:S(2)}) collective-permute-start(bf16[512,1024]{1,0:T(8,128)(2,1)S(1)} %collective-permute-done.22), channel_id=1, source_target_pairs={{8,9},{9,8},{12,13},{13,12},{10,11},{11,10},{14,15},{15,14},{24,25... | collective-permute-start | bytes 3145736 | tf_op jit(solution)/shard_map/ppermute | solution.py:286
  290.0 38.7 %collective-permute-start.32 = (bf16[512,1024]{1,0:T(8,128)(2,1)}, bf16[512,1024]{1,0:T(8,128)(2,1)S(1)}, u32[]{:S(2)}, u32[]{:S(2)}) collective-permute-start(bf16[512,1024]{1,0:T(8,128)(2,1)} %collective-permute-done.30), channel_id=1, source_target_pairs={{0,1},{1,0},{4,5},{5,4},{2,3},{3,2},{6,7},{7,6},{16,17},{17,16},{2... | collective-permute-start | bytes 3145736 | tf_op jit(solution)/shard_map/ppermute | solution.py:286
  304.3 54.4 %collective-permute-start.41 = (bf16[512,1024]{1,0:T(8,128)(2,1)S(1)}, bf16[512,1024]{1,0:T(8,128)(2,1)S(1)}, u32[]{:S(2)}, u32[]{:S(2)}) collective-permute-start(bf16[512,1024]{1,0:T(8,128)(2,1)S(1)} %collective-permute-done.22), channel_id=1, source_target_pairs={{8,24},{12,28},{24,8},{28,12},{9,25},{13,29},{25,9},{29,13},{10,26... | collective-permute-start | bytes 3145736 | tf_op jit(solution)/shard_map/ppermute | solution.py:278
  326.3 33.5 %collective-permute-start.40 = (bf16[512,1024]{1,0:T(8,128)(2,1)S(1)}, bf16[512,1024]{1,0:T(8,128)(2,1)S(1)}, u32[]{:S(2)}, u32[]{:S(2)}) collective-permute-start(bf16[512,1024]{1,0:T(8,128)(2,1)S(1)} %collective-permute-done.19), channel_id=1, source_target_pairs={{8,24},{12,28},{24,8},{28,12},{9,25},{13,29},{25,9},{29,13},{10,26... | collective-permute-start | bytes 3145736 | tf_op jit(solution)/shard_map/ppermute | solution.py:278
  327.5 33.5 %collective-permute-start.38 = (bf16[512,1024]{1,0:T(8,128)(2,1)S(1)}, bf16[512,1024]{1,0:T(8,128)(2,1)S(1)}, u32[]{:S(2)}, u32[]{:S(2)}) collective-permute-start(bf16[512,1024]{1,0:T(8,128)(2,1)S(1)} %collective-permute-done.19), channel_id=1, source_target_pairs={{8,9},{9,8},{12,13},{13,12},{10,11},{11,10},{14,15},{15,14},{24,25... | collective-permute-start | bytes 3145736 | tf_op jit(solution)/shard_map/ppermute | solution.py:286
  328.7 123.8 %collective-permute-start.15 = (bf16[512,1024]{1,0:T(8,128)(2,1)}, bf16[512,1024]{1,0:T(8,128)(2,1)S(1)}, u32[]{:S(2)}, u32[]{:S(2)}) collective-permute-start(bf16[512,1024]{1,0:T(8,128)(2,1)} %collective-permute-done.11), channel_id=1, source_target_pairs={{0,16},{4,20},{8,24},{16,0},{20,4},{24,8},{1,17},{5,21},{9,25},{17... | collective-permute-start | bytes 3145736 | tf_op jit(solution)/shard_map/ppermute | solution.py:278
  358.7 46.3 %collective-permute-start.25 = (bf16[512,1024]{1,0:T(8,128)(2,1)S(1)}, bf16[512,1024]{1,0:T(8,128)(2,1)S(1)}, u32[]{:S(2)}, u32[]{:S(2)}) collective-permute-start(bf16[512,1024]{1,0:T(8,128)(2,1)S(1)} %collective-permute-done.23), channel_id=1, source_target_pairs={{12,13},{13,12},{14,15},{15,14},{28,29},{29,28},{30,31},{31,30}} | collective-permute-start | bytes 3145736 | tf_op jit(solution)/shard_map/ppermute | solution.py:286
  359.9 46.5 %collective-permute-start.27 = (bf16[512,1024]{1,0:T(8,128)(2,1)S(1)}, bf16[512,1024]{1,0:T(8,128)(2,1)S(1)}, u32[]{:S(2)}, u32[]{:S(2)}) collective-permute-start(bf16[512,1024]{1,0:T(8,128)(2,1)S(1)} %collective-permute-done.23), channel_id=1, source_target_pairs={{12,28},{28,12},{13,29},{29,13},{14,30},{30,14},{15,31},{31,15}} | collective-permute-start | bytes 3145736 | tf_op jit(solution)/shard_map/ppermute | solution.py:278
  361.1 95.4 %collective-permute-start.14 = (bf16[512,1024]{1,0:T(8,128)(2,1)}, bf16[512,1024]{1,0:T(8,128)(2,1)S(1)}, u32[]{:S(2)}, u32[]{:S(2)}) collective-permute-start(bf16[512,1024]{1,0:T(8,128)(2,1)} %collective-permute-done.10), channel_id=1, source_target_pairs={{0,16},{4,20},{8,24},{16,0},{20,4},{24,8},{1,17},{5,21},{9,25},{17... | collective-permute-start | bytes 3145736 | tf_op jit(solution)/shard_map/ppermute | solution.py:278
  413.3 44.3 %collective-permute-start.12 = (bf16[512,1024]{1,0:T(8,128)(2,1)}, bf16[512,1024]{1,0:T(8,128)(2,1)S(1)}, u32[]{:S(2)}, u32[]{:S(2)}) collective-permute-start(bf16[512,1024]{1,0:T(8,128)(2,1)} %collective-permute-done.10), channel_id=1, source_target_pairs={{0,1},{1,0},{4,5},{5,4},{8,9},{9,8},{2,3},{3,2},{6,7},{7,6},{10,11... | collective-permute-start | bytes 3145736 | tf_op jit(solution)/shard_map/ppermute | solution.py:286
  416.1 42.8 %collective-permute-start.57 = (bf16[512,1024]{1,0:T(8,128)(2,1)S(1)}, bf16[512,1024]{1,0:T(8,128)(2,1)S(1)}, u32[]{:S(2)}, u32[]{:S(2)}) collective-permute-start(bf16[512,1024]{1,0:T(8,128)(2,1)S(1)} %collective-permute-done.55), channel_id=1, source_target_pairs={{4,5},{5,4},{8,9},{9,8},{12,13},{13,12},{6,7},{7,6},{10,11},{11,10... | collective-permute-start | bytes 3145736 | tf_op jit(solution)/shard_map/ppermute | solution.py:286
  489.2 52.1 %collective-permute-start.58 = (bf16[2,128,2048]{1,0,2:T(2,128)(2,1)}, bf16[2,128,2048]{1,0,2:T(2,128)(2,1)}, u32[]{:S(2)}, u32[]{:S(2)}) collective-permute-start(bf16[2,128,2048]{1,0,2:T(2,128)(2,1)} %dynamic-slice_bitcast_fusion.1), channel_id=1, source_target_pairs={{0,2},{2,0},{1,3},{3,1},{4,6},{6,4},{5,7},{7,5},{8,10},{10,8},{9,1... | collective-permute-start | bytes 3145736 | tf_op jit(solution)/shard_map/ppermute | solution.py:382
  496.6 39.5 %collective-permute-start.61 = (bf16[4,2,32,1024]{3,2,1,0:T(8,128)(2,1)}, bf16[4,2,32,1024]{3,2,1,0:T(8,128)(2,1)}, u32[]{:S(2)}, u32[]{:S(2)}) collective-permute-start(bf16[4,2,32,1024]{3,2,1,0:T(8,128)(2,1)} %get-tuple-element.20), channel_id=1, source_target_pairs={{12,0},{13,1},{14,2},{15,3},{28,16},{29,17},{30,18},{31,19}} | collective-permute-start | bytes 1572872 | tf_op jit(solution)/shard_map/ppermute | solution.py:345
  (53 other events, 749.2 us)

commit v2 on v1

v2 whole, which is shorter than its diff:
```python
import functools

import jax
import jax.numpy as jnp
from jax import lax
from jax.experimental import pallas as pl
from jax.experimental.pallas import tpu as pltpu
from jax.sharding import PartitionSpec as P

HEADS = 128
GROUPS = 8
SPAN = 128
GROUP_HEADS = HEADS // GROUPS
SPLIT = (1, 1)
TILE = 512
VMEM = 20 * 1024 * 1024

norm_eps = 1e-05
far = -1e30


def spread(values, head_dim):
    heads = values.shape[1]
    high = values.astype(jnp.bfloat16)
    low = (values - high.astype(jnp.float32)).astype(jnp.bfloat16)
    both = jnp.concatenate([high, low], axis=1)
    row = lax.broadcasted_iota(jnp.int32, (2 * heads, heads * head_dim), 0)
    col = lax.broadcasted_iota(jnp.int32, (2 * heads, heads * head_dim), 1)
    ones = (col // head_dim == row % heads).astype(jnp.bfloat16)
    return jnp.dot(both, ones, preferred_element_type=jnp.float32)


def local_kernel(
    limit_ref, x_ref, b_ref, c_ref, raw_ref, bias_ref, rate_ref, skip_ref, y_ref, end_ref, keep_ref, grow_ref
):
    tokens, width = x_ref.shape[1:]
    heads = raw_ref.shape[2]
    head_dim = width // heads
    f32 = jnp.float32
    token = lax.broadcasted_iota(jnp.int32, (heads, tokens), 1)
    size = jax.nn.softplus(raw_ref[0, 0] + bias_ref[0])
    size = size * (token < limit_ref[pl.program_id(0)]).astype(f32)
    log_keep = -jnp.exp(rate_ref[0]) * size
    row = lax.broadcasted_iota(jnp.int32, (tokens, tokens), 0)
    col = lax.broadcasted_iota(jnp.int32, (tokens, tokens), 1)
    causal = row >= col
    cum = jnp.dot(log_keep, (row <= col).astype(f32), precision=lax.Precision.HIGHEST)
    cum_t = cum.T
    shifted = cum - jnp.where(size > 0, jnp.log(jnp.where(size > 0, size, 1.0)), far)
    b = b_ref[0, 0]
    scores = lax.dot_general(
        c_ref[0, 0], b, (((1,), (1,)), ((), ())), preferred_element_type=f32
    )
    lane = lax.broadcasted_iota(jnp.int32, (tokens, 2 * head_dim), 1)
    for pair in range(heads // 2):
        decayed = []
        for head in (2 * pair, 2 * pair + 1):
            gap = cum_t[:, head : head + 1] - shifted[head : head + 1, :]
            decayed.append((scores * jnp.exp(jnp.where(causal, gap, far))).astype(jnp.bfloat16))
        here = pl.ds(pair * 2 * head_dim, 2 * head_dim)
        x = x_ref[0, :, here]
        zero = jnp.zeros_like(x)
        apart = jnp.concatenate(
            [jnp.where(lane < head_dim, x, zero), jnp.where(lane >= head_dim, x, zero)], axis=0
        )
        y = jnp.dot(jnp.concatenate(decayed, axis=1), apart, preferred_element_type=f32)
        y_ref[0, :, here] = y + skip_ref[0, :, here] * x.astype(f32)
    last = cum[:, tokens - 1 : tokens]
    tail = spread((jnp.exp(last - cum) * size).T, head_dim)
    weighted = (tail * x_ref[0].astype(f32)).astype(jnp.bfloat16)
    b_t = b.astype(f32).T.astype(jnp.bfloat16)
    end_ref[0, 0] = jnp.dot(b_t, weighted, preferred_element_type=f32)
    grow = jnp.exp(cum_t)
    keep_ref[0, 0] = spread(jnp.broadcast_to(grow[tokens - 1 :], (8, heads)), head_dim)
    grow_ref[0, 0] = grow


def leave_kernel(count, kind, *refs):
    at_ref, refs = refs[0], refs[1:]
    keep_ref, end_ref, state_ref, leaving_ref = refs[-4:]
    state = None
    if kind != "only":
        state = refs[0][0].astype(jnp.float32)
        refs = refs[1:]
    if count:
        first = jnp.concatenate([r[0, 0].astype(jnp.float32) for r in refs[:count]], axis=0)
        state = first if state is None else jnp.where(at_ref[1] == 0, first, state)
    state_ref[0] = state.astype(jnp.bfloat16)
    leaving_ref[0] = (keep_ref[0, 0, :1] * state + end_ref[0, 0]).astype(jnp.bfloat16)


def leave_part(at, coming, first, inside, keep, end):
    groups, sessions, state_size, width = end.shape
    by_turn = lambda s, at: (at[0], s, 0, 0)
    whole = pl.BlockSpec((1, state_size, width), lambda s, at: (s, 0, 0))
    operands, specs = [], []
    if coming is not None:
        operands.append(coming)
        specs.append(whole)
    if first is not None:
        operands += first
        specs += [
            pl.BlockSpec((1, 1, *f.shape[2:]), lambda s, at: (inside, s, 0, 0)) for f in first
        ]
    operands += [keep, end]
    specs += [
        pl.BlockSpec((1, 1, *keep.shape[2:]), by_turn),
        pl.BlockSpec((1, 1, state_size, width), by_turn),
    ]
    kind = None if first is None else ("only" if coming is None else "both")
    shape = jax.ShapeDtypeStruct((sessions, state_size, width), jnp.bfloat16)
    return pl.pallas_call(
        functools.partial(leave_kernel, 0 if first is None else len(first), kind),
        grid_spec=pltpu.PrefetchScalarGridSpec(
            num_scalar_prefetch=1, grid=(sessions,), in_specs=specs, out_specs=[whole, whole]
        ),
        out_shape=[shape, shape],
        compiler_params=pltpu.CompilerParams(vmem_limit_bytes=VMEM),
        cost_estimate=pl.CostEstimate(flops=10**6, bytes_accessed=3 * 2**20, transcendentals=0),
        name="leave_part",
    )(at, *operands)


def normed_kernel(at_ref, state_ref, c_ref, grow_ref, y_ref, gate_ref, gain_ref, _, out_ref):
    width = y_ref.shape[2]
    heads = grow_ref.shape[3]
    from_state = jnp.dot(c_ref[0, 0], state_ref[0], preferred_element_type=jnp.float32)
    ssd_out = y_ref[0] + from_state * spread(grow_ref[0, 0], width // heads)
    gate = gate_ref[0].astype(jnp.float32)
    gated = ssd_out * (gate / (1.0 + jnp.exp(-gate)))
    scale = lax.rsqrt(jnp.mean(gated * gated, axis=1, keepdims=True) + norm_eps)
    out_ref[0, 0] = (gated * scale * gain_ref[0]).astype(jnp.bfloat16)


def normed_part(index, at, state, c, grow, y, gate, gain, normed):
    sessions, tokens, inner = y.shape
    groups, state_size = c.shape[1], c.shape[3]
    width = inner // groups
    heads = grow.shape[3]
    by_both = lambda s, at: (s, at[0], 0, 0)
    flat = pl.BlockSpec((1, tokens, width), lambda s, at: (s, 0, at[0]))
    return pl.pallas_call(
        normed_kernel,
        grid_spec=pltpu.PrefetchScalarGridSpec(
            num_scalar_prefetch=1,
            grid=(sessions,),
            in_specs=[
                pl.BlockSpec((1, state_size, width), lambda s, at: (s, 0, 0)),
                pl.BlockSpec((1, 1, tokens, state_size), by_both),
                pl.BlockSpec((1, 1, tokens, heads), by_both),
                flat,
                flat,
                pl.BlockSpec((1, 1, width), lambda s, at: (at[0], 0, 0)),
                pl.BlockSpec(memory_space=pl.ANY),
            ],
            out_specs=pl.BlockSpec((1, 1, tokens, width), lambda s, at: (index, s, 0, 0)),
        ),
        out_shape=jax.ShapeDtypeStruct(normed.shape, normed.dtype),
        input_output_aliases={7: 0},
        compiler_params=pltpu.CompilerParams(vmem_limit_bytes=VMEM),
        cost_estimate=pl.CostEstimate(
            flops=10**8, bytes_accessed=4 * 2**20, transcendentals=2**19
        ),
        name="normed_part",
    )(at, state, c, grow, y, gate, gain, normed)


def pick_kernel(slot_ref, pool_ref, out_ref):
    heads, cols, head_dim = pool_ref.shape[1:]
    groups = out_ref.shape[0]
    per = heads // groups
    for g in range(groups):
        held = [pool_ref[0, g * per + h] for h in range(per)]
        out_ref[g, 0] = jnp.concatenate(held, axis=1).astype(jnp.bfloat16)


def pick_part(asked, pool, groups):
    _, heads, cols, head_dim = pool.shape
    count = asked.shape[0]
    width = heads // groups * head_dim
    return pl.pallas_call(
        pick_kernel,
        grid_spec=pltpu.PrefetchScalarGridSpec(
            num_scalar_prefetch=1,
            grid=(count,),
            in_specs=[pl.BlockSpec((1, heads, cols, head_dim), lambda i, slot: (slot[i], 0, 0, 0))],
            out_specs=pl.BlockSpec((groups, 1, cols, width), lambda i, slot: (0, i, 0, 0)),
        ),
        out_shape=jax.ShapeDtypeStruct((groups, count, cols, width), jnp.bfloat16),
        compiler_params=pltpu.CompilerParams(vmem_limit_bytes=VMEM),
        name="pick_part",
    )(asked, pool)


def final_kernel(turn_ref, *refs):
    parts, out_ref = refs[:-1], refs[-1]
    heads, _, head_dim = out_ref.shape[1:]
    value = parts[0][0, 0].astype(jnp.float32)
    for k in range(1, len(parts)):
        value = jnp.where(turn_ref[0] == k, parts[k][0, 0].astype(jnp.float32), value)
    for h in range(heads):
        out_ref[0, h] = value[:, h * head_dim : (h + 1) * head_dim]


def final_part(turn, parts, heads, head_dim):
    groups, sessions, cols, width = parts[0].shape
    per = heads // groups
    return pl.pallas_call(
        final_kernel,
        grid_spec=pltpu.PrefetchScalarGridSpec(
            num_scalar_prefetch=1,
            grid=(sessions, groups),
            in_specs=[pl.BlockSpec((1, 1, cols, width), lambda s, g, _: (g, s, 0, 0)) for _ in parts],
            out_specs=pl.BlockSpec((1, per, cols, head_dim), lambda s, g, _: (s, g, 0, 0)),
        ),
        out_shape=jax.ShapeDtypeStruct((sessions, heads, cols, head_dim), jnp.float32),
        compiler_params=pltpu.CompilerParams(vmem_limit_bytes=VMEM),
        name="final_part",
    )(turn.reshape(1).astype(jnp.int32), *parts)


def local_part(limits, x, b, c, raw, bias, rate, skip):
    sessions, tokens, inner = x.shape
    groups = b.shape[1]
    state = b.shape[3]
    heads = raw.shape[2]
    width = inner // groups

    def by_group(*block):
        return pl.BlockSpec((1, *block), lambda s, g, _: (g, 0, 0))

    def by_both(*block):
        return pl.BlockSpec((1, 1, *block), lambda s, g, _: (s, g, 0, 0))

    def by_turn(*block):
        return pl.BlockSpec((1, 1, *block), lambda s, g, _: (g, s, 0, 0))

    flat = pl.BlockSpec((1, tokens, width), lambda s, g, _: (s, 0, g))
    f32 = jnp.float32
    return pl.pallas_call(
        local_kernel,
        grid_spec=pltpu.PrefetchScalarGridSpec(
            num_scalar_prefetch=1,
            grid=(sessions, groups),
            in_specs=[
                flat,
                by_both(tokens, state),
                by_both(tokens, state),
                by_both(heads, tokens),
                by_group(heads, 1),
                by_group(heads, 1),
                by_group(1, width),
            ],
            out_specs=[
                flat,
                by_turn(state, width),
                by_turn(8, width),
                by_both(tokens, heads),
            ],
        ),
        out_shape=[
            jax.ShapeDtypeStruct((sessions, tokens, inner), f32),
            jax.ShapeDtypeStruct((groups, sessions, state, width), f32),
            jax.ShapeDtypeStruct((groups, sessions, 8, width), f32),
            jax.ShapeDtypeStruct((sessions, groups, tokens, heads), f32),
        ],
        compiler_params=pltpu.CompilerParams(vmem_limit_bytes=VMEM),
        cost_estimate=pl.CostEstimate(
            flops=4 * 10**9, bytes_accessed=14 * 2**20, transcendentals=2**22
        ),
        name="local_part",
    )(
        limits,
        x,
        b,
        c,
        raw,
        bias[:, :, None],
        rate[:, :, None],
        skip,
    )


def product_kernel(layout, parts, base_ref, order_ref, *refs):
    lefts, weights, out_ref, held = refs[:parts], refs[parts:-2], refs[-2], refs[-1]

    @pl.when(pl.program_id(0) == 0)
    def _():
        for k in range(parts):
            held[k] = lefts[k][0]

    total = jnp.zeros(out_ref.shape, jnp.float32)
    for (part, low), weight in zip(layout, weights):
        depth = weight.shape[0]
        left = held[order_ref[part], :, low : low + depth]
        total += jnp.dot(left, weight[...], preferred_element_type=jnp.float32)
    out_ref[...] = total.astype(out_ref.dtype)


def product(base, order, lefts, layout, weights, specs):
    parts = len(lefts)
    tokens, rows = lefts[0][0].shape[1:]
    cols = weights[0].shape[1]
    tile = min(cols, TILE)

    def left_spec(place):
        return pl.BlockSpec((1, tokens, rows), lambda j, base, _: (place(base[0]), 0, 0))

    return pl.pallas_call(
        functools.partial(product_kernel, layout, parts),
        grid_spec=pltpu.PrefetchScalarGridSpec(
            num_scalar_prefetch=2,
            grid=(cols // tile,),
            in_specs=[left_spec(place) for _, place in lefts]
            + [pl.BlockSpec((depth, tile), place) for depth, place in specs],
            out_specs=pl.BlockSpec((tokens, tile), lambda j, *_: (0, j)),
            scratch_shapes=[pltpu.VMEM((parts, tokens, rows), jnp.bfloat16)],
        ),
        out_shape=jax.ShapeDtypeStruct((tokens, cols), jnp.bfloat16),
        compiler_params=pltpu.CompilerParams(vmem_limit_bytes=VMEM),
        cost_estimate=pl.CostEstimate(
            flops=2 * tokens * parts * rows * cols,
            bytes_accessed=2 * (tokens * parts * rows + parts * rows * cols + tokens * cols),
            transcendentals=0,
        ),
        name="product",
    )(base.reshape(1).astype(jnp.int32), order, *[left for left, _ in lefts], *weights)


def row_block(k):
    return lambda j, *_: (k, j)


class Clock:
    def __init__(self):
        self.due = {}

    def send(self, key, value, axis, pairs, due):
        with jax.named_scope("_".join(str(k) for k in key)):
            self.due.setdefault(due, {})[key] = lax.ppermute(value, axis, pairs)

    def done(self, tick):
        return self.due.pop(tick, {})


def shards(
    head_input,
    gate_input,
    state_in_proj,
    state_out_proj,
    step_raw,
    head_step_bias,
    decay_log,
    skip_gain,
    norm_gain,
    out_weight,
    pool_states,
    slot_map,
    span_lengths,
):
    turns = lax.axis_size("ctx")
    turn = lax.axis_index("ctx")
    lanes = lax.axis_size("groups")
    lane = lax.axis_index("groups")
    cores = lax.axis_size("sess")
    core = lax.axis_index("sess")
    head_count = lax.axis_size("head")
    head_index = lax.axis_index("head")
    sessions, tokens, inner = head_input.shape
    heads = step_raw.shape[2]
    head_dim = inner // heads
    slots = pool_states.shape[0]
    state_cols = pool_states.shape[3]
    groups = heads // GROUP_HEADS
    width = inner // groups
    bf16 = jnp.bfloat16

    carriers = lanes * cores
    rows = inner // carriers
    carrier = lane * cores + core
    mine = lax.dynamic_slice_in_dim(out_weight, carrier * rows, rows, 0)
    unit = rows // sum(SPLIT)
    lows = [sum(SPLIT[:p]) * unit for p in range(len(SPLIT))]
    pieces = [mine[low : low + size * unit] for low, size in zip(lows, SPLIT)]

    def slots_of(which):
        return lax.dynamic_slice_in_dim(slot_map, which * sessions, sessions)

    own_slots = slots_of(core)
    asked = jnp.concatenate([slots_of((core - by) % cores) for by in range(cores)])
    picked = pick_part(asked % slots, pool_states.transpose(0, 1, 3, 2), groups)
    start = picked[:, :sessions]
    for by in range(1, cores):
        found = picked[:, by * sessions : (by + 1) * sessions]
        found = lax.ppermute(found, "sess", [(i, (i - by) % cores) for i in range(cores)])
        here = (own_slots // slots == (core + by) % cores)[None, :, None, None]
        start = jnp.where(here, found, start)

    first_session = core * sessions
    own_lengths = lax.dynamic_slice_in_dim(span_lengths, first_session, sessions)
    limits = jnp.clip(own_lengths * SPAN - turn * tokens, 0, tokens)
    first_group = head_index * groups

    def grouped(proj):
        return lax.dynamic_slice_in_dim(proj, first_group, groups, 2).swapaxes(1, 2)

    b = grouped(state_in_proj)
    c = grouped(state_out_proj)
    raw = step_raw.swapaxes(1, 2).reshape(sessions, groups, GROUP_HEADS, tokens)
    skip = jnp.repeat(skip_gain, head_dim).reshape(groups, 1, width)
    gain = norm_gain.reshape(groups, 1, width)

    waves = groups + turns - 2
    first_wave = 2
    clock = Clock()
    hops = range(1, turns - 1)
    count = len(SPLIT)
    starts = {}

    def plan(tick, *what):
        starts.setdefault(tick, []).append(what)

    up_due, down_due = {}, {}
    for hop in hops:
        pairs_up = [(i, i + 1) for i in range(hop - 1, turns - 1)]
        pairs_down = [(i + 1, i) for i in range(turns - hop)]
        for p in range(count):
            if hop == 1:
                at, due = ((0, 1), (1, 2))[p]
            else:
                at, due = ((2, 3), (5, 7))[p]
                at, due = at + 3 * (hop - 2), due + 3 * (hop - 2)
            up_due[hop, p] = due
            plan(at, ("up", hop, p), ("up", hop - 1, p), "ctx", pairs_up, due)
            if hop == 1:
                at, due = ((2, 3), (3, 4))[p]
            else:
                at, due = ((4, 5), (5, 6))[p]
                at, due = at + 3 * (hop - 2), due + 3 * (hop - 2)
            down_due[hop, p] = due
            plan(at, ("down", hop, p), ("down", hop - 1, p), "ctx", pairs_down, due)
    ready = {}
    for j in range(1, turns):
        holders = range(turns)
        for p in range(count):
            if j == 1:
                holders = range(turns - 1)
                at, due = ((4, 5), (5, 6))[p]
            elif j == turns - 1:
                holders = range(1, turns)
                at, due = ((2, 3), (3, 4))[p]
            else:
                at = max(down_due[j, p], up_due[turns - j, p]) + 1
                due = at + 1
            for by_lane in range(1, lanes):
                pairs = [
                    (y * turns + z, (y - by_lane) % lanes * turns + z)
                    for y in range(lanes)
                    for z in holders
                ]
                plan(at, ("part", j, p, by_lane, 0), ("part", j, p, 0, 0), ("groups", "ctx"), pairs, due)
            for by_lane in range(lanes):
                for by in range(1, cores):
                    pairs = [
                        (z * cores + k, z * cores + (k - by) % cores)
                        for z in holders
                        for k in range(cores)
                    ]
                    plan(
                        due + 1,
                        ("part", j, p, by_lane, by),
                        ("part", j, p, by_lane, 0),
                        ("ctx", "sess"),
                        pairs,
                        due + 1,
                    )
            ready[j, p] = due + 1
    half = max(1, groups // 2)
    begun = [range(0, half), range(half, groups)]
    for k, part in enumerate(begun):
        for other in range(1, turns):
            if len(part):
                plan(1 + k, ("first", k, other), ("start", k), "ctx", [(other, 0)], 1 + 2 * k)
    last_tick = max(max(starts), first_wave + waves) + 1

    have = {}
    for p in range(count):
        have["up", 0, p] = have["down", 0, p] = pieces[p]
    for k, part in enumerate(begun):
        have["start", k] = start[part.start : part.stop]

    def resolve(key):
        if key in have:
            return have[key]
        if key[0] == "part" and key[3:] == (0, 0):
            _, j, p = key[:3]
            if j == 1:
                have[key] = have["down", 1, p]
            elif j == turns - 1:
                have[key] = have["up", 1, p]
            else:
                have[key] = jnp.where(turn + j < turns, have["down", j, p], have["up", turns - j, p])
        return have[key]

    normed = jnp.zeros((waves + 1, sessions, tokens, width), bf16)
    leavings, lent = [], []
    y = end = keep = grow = None
    batches = [(0, groups)] if groups < 3 else [(0, 2)] + [(g, g + 1) for g in range(2, groups)]
    for tick in range(last_tick + 1):
        sends = starts.get(tick, [])
        values = clock.done(tick - 1)
        have.update(values)
        for key, source, axis, pairs, due in sends:
            values[source] = resolve(source)
        if tick == 1:
            values["x"] = head_input
        if tick == 2:
            values.update(y=y, end=end, keep=keep, grow=grow)
        have.update(zip(values, lax.optimization_barrier(tuple(values.values()))))
        if tick == 2:
            y, end, keep, grow = (have[k] for k in ("y", "end", "keep", "grow"))
        index = tick - first_wave
        if 0 <= index <= waves:
            at = jnp.clip(index - turn, 0, groups - 1)
            coming = have["wave", index - 1] if index else None
            first, inside = None, 0
            if index < groups:
                k = 0 if index < half else 1
                inside = index - begun[k].start
                first = [have["start", k]] + [have["first", k, other] for other in range(1, turns)]
            at = jnp.stack([at, turn]).astype(jnp.int32)
            state, leaving = leave_part(at, coming, first, inside, keep, end)
            leavings.append(leaving)
            if index < waves:
                pairs = [(i, i + 1) for i in range(turns - 1) if 0 <= index - i < groups]
                clock.send(("wave", index), leaving, "ctx", pairs, tick)
        for key, source, axis, pairs, due in sends:
            clock.send(key, have[source], axis, pairs, due)
        if tick == 1:
            y, end, keep, grow = local_part(
                limits,
                have["x"],
                b,
                c,
                raw,
                head_step_bias.reshape(groups, GROUP_HEADS),
                decay_log.reshape(groups, GROUP_HEADS),
                skip,
            )
        if 0 <= index <= waves:
            normed = normed_part(index, at, state, c, grow, y, gate_input, gain, normed)
        for low, high in batches:
            if index == turns - 2 + high:
                chunk = lax.dynamic_slice_in_dim(
                    normed, jnp.where(turn == 0, 0, turns - 1) + low, high - low, 0
                )
                chunk = chunk.reshape(high - low, sessions * tokens, width)
                clock.send(
                    ("inward", low),
                    chunk,
                    "ctx",
                    [(0, 1), (turns - 1, turns - 2)],
                    min(tick + 1, last_tick),
                )
    for late in sorted(clock.due):
        have.update(clock.due[late])

    ended = []
    for to in range(turns):
        cut = [leavings[turns - 1 + g][:, to * state_cols : (to + 1) * state_cols] for g in range(groups)]
        ended.append(jnp.stack(cut))
    tied = lax.optimization_barrier((*ended, have["inward", batches[-1][0]]))
    ended, have["inward", batches[-1][0]] = list(tied[:-1]), tied[-1]
    for to in range(turns - 1):
        ended[to] = lax.ppermute(ended[to], "ctx", [(turns - 1, to)])
    final_states = final_part(turn, ended, heads, head_dim).transpose(0, 1, 3, 2)

    def as_left(held):
        held = held.transpose(1, 0, 2).reshape(sessions * tokens, carriers, rows)
        return held.transpose(1, 0, 2)

    def at_place(k):
        return lambda base: base + k

    def at_fixed(k):
        return lambda base: k

    base = turn
    if groups == carriers:
        held = normed.reshape(waves + 1, sessions * tokens, width)
        left = [(held, at_place(k)) for k in range(carriers)]
        lent = [
            (have["inward", low], at_fixed(k)) for low, high in batches for k in range(high - low)
        ]
    else:
        held = lax.dynamic_slice_in_dim(normed, turn, groups, 0)
        held = as_left(held.reshape(groups, sessions * tokens, width))
        left = [(held, at_fixed(k)) for k in range(carriers)]
        held = jnp.concatenate([have["inward", low] for low, _ in batches], axis=0)
        held = as_left(held)
        lent = [(held, at_fixed(k)) for k in range(carriers)]
    order = jnp.stack(
        [
            (lane + by_lane) % lanes * cores + (core + by) % cores
            for by_lane in range(lanes)
            for by in range(cores)
        ]
    ).astype(jnp.int32)
    layout, specs = [], []
    for k in range(carriers):
        for p in range(count):
            layout.append((k, lows[p]))
            specs.append((SPLIT[p] * unit, row_block(0)))

    def parts_of(j):
        return [
            resolve(("part", j, p, by_lane, by))
            for by_lane in range(lanes)
            for by in range(cores)
            for p in range(count)
        ]

    blocks = {}
    blocks[0] = product(
        base,
        jnp.arange(carriers, dtype=jnp.int32),
        left,
        [(k, 0) for k in range(carriers)],
        [out_weight] * carriers,
        [(rows, row_block(k)) for k in range(carriers)],
    )
    for j in [1, turns - 1] + list(range(2, turns - 1)):
        blocks[j] = product(base, order, left, layout, parts_of(j), specs)
    if turns == 4:
        far_block = product(base, order, lent, layout, parts_of(2), specs)
    else:
        far_block = jnp.where(
            turn == 1,
            product(base, order, lent, layout, parts_of(turns - 2), specs),
            product(base, order, lent, layout, parts_of(2), specs),
        )
    live = (jnp.arange(tokens, dtype=jnp.int32)[None, :] < limits[:, None]).astype(jnp.float32)
    if head_count == 2:
        share = turns // 2

        def across(j, skipped):
            pairs = []
            for z in range(turns):
                to = (z + j) % turns // share
                if z not in skipped:
                    pairs.append((z * 2 + 1 - to, z * 2 + to))
            return lax.ppermute(blocks[j], ("ctx", "head"), pairs)

        skipped = {1: (turns - 1,), turns - 1: (0,)}
        other = {j: across(j, skipped.get(j, ())) for j in blocks}
        same = lax.ppermute(
            far_block, ("ctx", "head"), [(1 * 2 + 1, 0 * 2 + 1), ((turns - 2) * 2, (turns - 1) * 2)]
        )
        cross = lax.ppermute(
            far_block, ("ctx", "head"), [(1 * 2, 0 * 2 + 1), ((turns - 2) * 2 + 1, (turns - 1) * 2)]
        )
        sums = []
        for m in range(share):
            wanted = (head_index * share + m - turn) % turns
            ends = ((turn == 0) & (wanted == turns - 1)) | ((turn == turns - 1) & (wanted == 1))
            mine_now, theirs = same, cross
            for j in blocks:
                chosen = (wanted == j) & ~ends
                mine_now = jnp.where(chosen, blocks[j], mine_now)
                theirs = jnp.where(chosen, other[j], theirs)
            sums.append(mine_now.astype(jnp.float32) + theirs.astype(jnp.float32))
        summed = jnp.concatenate(sums, axis=1).reshape(sessions, tokens, -1)
    else:
        back = lax.ppermute(far_block, "ctx", [(1, 0), (turns - 2, turns - 1)])
        blocks[1] = jnp.where(turn == turns - 1, back, blocks[1])
        blocks[turns - 1] = jnp.where(turn == 0, back, blocks[turns - 1])
        stacked = jnp.stack([blocks[j] for j in range(turns)])
        stacked = lax.dynamic_slice_in_dim(
            jnp.concatenate([stacked, stacked], axis=0), (turns - turn) % turns, turns, 0
        )
        partial = stacked.transpose(1, 0, 2).reshape(sessions, tokens, -1)
        summed = lax.psum_scatter(partial, "head", scatter_dimension=2, tiled=True).astype(
            jnp.float32
        )
    mixed = (summed * live[:, :, None]).astype(bf16)
    return (mixed, final_states)


def solution(mesh):
    placed = (
        P(("groups", "sess"), "ctx", "head"),
        P(("groups", "sess"), "ctx", "head"),
        P(("groups", "sess"), "ctx", None, None),
        P(("groups", "sess"), "ctx", None, None),
        P(("groups", "sess"), "ctx", "head"),
        P("head"),
        P("head"),
        P("head"),
        P("head"),
        P("head", "ctx"),
        P(("groups", "sess"), "head", None, "ctx"),
        P("groups"),
        P("groups"),
    )
    return jax.shard_map(
        shards,
        mesh=mesh,
        in_specs=placed,
        out_specs=(
            P(("groups", "sess"), "ctx", "head"),
            P(("groups", "sess"), "head", None, "ctx"),
        ),
        check_vma=False,
    )
```

time: 557 us -> 313 us (0.56)
  the two profiles are of different devices: /device:TPU:0 before, /device:TPU:24 now
where the time goes in v2:
time: 313 us; the launch traced here: 311 us
  starting transfers between devices  108 us (35%)
  waiting for transfers between devices  72.8 us (23%)
  Pallas kernels  61.2 us (20%)
  local copies, waits for them, and re-layouts  57.9 us (18%)
  other arithmetic  9.28 us (3%)
    ppermute x41, starting transfers between devices, send(): self.due.setdefault(due, {})[key] = lax.ppermute(value, axis, pairs)  89.8 us
    ppermute x41, waiting for transfers between devices, send(): self.due.setdefault(due, {})[key] = lax.ppermute(value, axis, pairs)  58.7 us
    unnamed x140, local copies, waits for them, and re-layouts  46.2 us
    pallas_call x5, Pallas kernels, product(): pl.pallas_call(functools.partial(product_kernel, layout, parts), grid_spe...  24.1 us
    pallas_call x1, Pallas kernels, local_part(): pl.pallas_call(local_kernel, grid_spec=pltpu.PrefetchScalarGridSpec(num_s...  11.7 us
    pallas_call x7, Pallas kernels, normed_part(): pl.pallas_call(normed_kernel, grid_spec=pltpu.PrefetchScalarGridSpec(num_...  11.6 us
    ppermute x4, starting transfers between devices, across(): return lax.ppermute(blocks[j], ('ctx', 'head'), pairs)  11.2 us
    pallas_call x7, Pallas kernels, leave_part(): pl.pallas_call(functools.partial(leave_kernel, 0 if first is None else le...  9.28 us
  transfers between devices with their start and end apart: 51, of which 11 were waited for; matrix products, arithmetic and copies ran while one was open for 5% of the time, Pallas kernels for 19%

profile of v2, /device:TPU:24, one launch (start us, length us, event | category | flops | bytes accessed | tf_op | source)
XLA Modules:
  0.0 310.8 jit_solution(9244187258222011332)
XLA Ops:
  5.9 3.1 constant_dynamic-slice_fusion.6
  16.4 8.7 %collective-permute-start.5 = (bf16[2,2,32,1024]{3,2,1,0:T(8,128)(2,1)S(1)}, bf16[2,2,32,1024]{3,2,1,0:T(8,128)(2,1)S(1)}, u32[]{:S(2)}, u32[]{:S(2)}) collective-permute-start(bf16[2,2,32,1024]{3,2,1,0:T(8,128)(2,1)S(1)} %get-tuple-element.88.refs_1_.refs_2_), channel_id=1, source_target_pairs={{12,0},{13,1},{14,2},{15,3},{28,16},{29,17},{30,18},{31,19}} | collective-permute-start | bytes 786440 | tf_op jit(solution)/shard_map/first_0_3/ppermute | solution.py:340
  26.7 11.7 %local_part.1 = (f32[2,128,4096]{2,1,0:T(8,128)S(1)}, f32[4,2,128,1024]{3,2,1,0:T(8,128)S(1)}, f32[4,2,8,1024]{3,2,1,0:T(8,128)S(1)}, f32[2,4,128,16]{3,2,1,0:T(8,128)S(1)}) custom-call(s32[2]{0:T(128)S(1)} %get-tuple-element.203.limit_ref, bf16[2,128,4096]{2,1,0:T(8,128)(2,1)S(1)} %copy-done.57, bf16[2,4,128,128]{3,2,1,0:T(8,128)(2,1)S(1)} %bitcast.95, ...), custom_call_target="tpu_custom_call" | custom-call | flops 4000000000 | bytes 14680064 | tf_op jit(solution)/shard_map/local_part/pallas_call | solution.py:240
  45.5 2.9 collective-permute-start.9
  49.7 3.4 %collective-permute-start.11 = (bf16[512,1024]{1,0:T(8,128)(2,1)S(1)}, bf16[512,1024]{1,0:T(8,128)(2,1)}, u32[]{:S(2)}, u32[]{:S(2)}) collective-permute-start(bf16[512,1024]{1,0:T(8,128)(2,1)S(1)} %collective-permute-done.2.refs_4_), channel_id=1, source_target_pairs={{4,20},{8,24},{12,28},{20,4},{24,8},{28,12},{5,21},{9,25},{13,29},... | collective-permute-start | bytes 3145736 | tf_op jit(solution)/shard_map/part_3_0_1_0/ppermute | solution.py:340
  53.1 6.5 %collective-permute-done.1.refs_5_ = bf16[512,1024]{1,0:T(8,128)(2,1)} collective-permute-done((bf16[512,1024]{1,0:T(8,128)(2,1)}, bf16[512,1024]{1,0:T(8,128)(2,1)}, u32[]{:S(2)}, u32[]{:S(2)}) %collective-permute-start.1) | collective-permute-done | bytes 1048608 | tf_op jit(solution)/shard_map/up_1_1/ppermute | solution.py:340
  61.0 11.3 %collective-permute-start.14 = (bf16[2,2,32,1024]{3,2,1,0:T(8,128)(2,1)S(1)}, bf16[2,2,32,1024]{3,2,1,0:T(8,128)(2,1)}, u32[]{:S(2)}, u32[]{:S(2)}) collective-permute-start(bf16[2,2,32,1024]{3,2,1,0:T(8,128)(2,1)S(1)} %get-tuple-element.105.refs_2_), channel_id=1, source_target_pairs={{12,0},{13,1},{14,2},{15,3},{28,16},{29,17},{30,18},{31,19}} | collective-permute-start | bytes 786440 | tf_op jit(solution)/shard_map/first_1_3/ppermute | solution.py:340
  79.8 9.1 %collective-permute-start.7 = (bf16[512,1024]{1,0:T(8,128)(2,1)S(1)}, bf16[512,1024]{1,0:T(8,128)(2,1)}, u32[]{:S(2)}, u32[]{:S(2)}) collective-permute-start(bf16[512,1024]{1,0:T(8,128)(2,1)S(1)} %copy-done.59), channel_id=1, source_target_pairs={{4,0},{8,4},{12,8},{5,1},{9,5},{13,9},{6,2},{10,6},{14,10},{7,3},{... | collective-permute-start | bytes 3145736 | tf_op jit(solution)/shard_map/down_1_1/ppermute | solution.py:340
  88.8 3.4 %collective-permute-start.8 = (bf16[512,1024]{1,0:T(8,128)(2,1)}, bf16[512,1024]{1,0:T(8,128)(2,1)}, u32[]{:S(2)}, u32[]{:S(2)}) collective-permute-start(bf16[512,1024]{1,0:T(8,128)(2,1)} %collective-permute-done.1.refs_5_), channel_id=1, source_target_pairs={{4,20},{8,24},{12,28},{20,4},{24,8},{28,12},{5,21},{9,25},{13,29},... | collective-permute-start | bytes 3145736 | tf_op jit(solution)/shard_map/part_3_1_1_0/ppermute | solution.py:340
  94.2 2.4 collective-permute-start.18
  100.5 7.8 %collective-permute-done.7.refs_5_ = bf16[512,1024]{1,0:T(8,128)(2,1)} collective-permute-done((bf16[512,1024]{1,0:T(8,128)(2,1)S(1)}, bf16[512,1024]{1,0:T(8,128)(2,1)}, u32[]{:S(2)}, u32[]{:S(2)}) %collective-permute-start.7) | collective-permute-done | bytes 1048608 | tf_op jit(solution)/shard_map/down_1_1/ppermute | solution.py:340
  110.0 3.7 %collective-permute-done.8.refs_9_ = bf16[512,1024]{1,0:T(8,128)(2,1)} collective-permute-done((bf16[512,1024]{1,0:T(8,128)(2,1)}, bf16[512,1024]{1,0:T(8,128)(2,1)}, u32[]{:S(2)}, u32[]{:S(2)}) %collective-permute-start.8) | collective-permute-done | bytes 1048608 | tf_op jit(solution)/shard_map/part_3_1_1_0/ppermute | solution.py:340
  115.4 3.8 %collective-permute-done.16.refs_1_ = bf16[2,128,1024]{2,1,0:T(8,128)(2,1)S(1)} collective-permute-done((bf16[2,128,1024]{2,1,0:T(8,128)(2,1)S(1)}, bf16[2,128,1024]{2,1,0:T(8,128)(2,1)S(1)}, u32[]{:S(2)}, u32[]{:S(2)}) %collective-permute-start.16) | collective-permute-done | bytes 524320 | tf_op jit(solution)/shard_map/wave_2/ppermute | solution.py:340
  123.0 2.4 collective-permute-start.24
  128.6 2.4 leave_part.10
  134.8 2.3 broadcast_select_fusion.1.refs_4_
  138.7 9.0 %collective-permute-done.22.refs_1_ = bf16[2,128,1024]{2,1,0:T(8,128)(2,1)S(1)} collective-permute-done((bf16[2,128,1024]{2,1,0:T(8,128)(2,1)}, bf16[2,128,1024]{2,1,0:T(8,128)(2,1)S(1)}, u32[]{:S(2)}, u32[]{:S(2)}) %collective-permute-start.22) | collective-permute-done | bytes 524320 | tf_op jit(solution)/shard_map/wave_3/ppermute | solution.py:340
  176.3 6.9 %collective-permute-start.26 = (bf16[2,256,1024]{2,1,0:T(8,128)(2,1)}, bf16[2,256,1024]{2,1,0:T(8,128)(2,1)}, u32[]{:S(2)}, u32[]{:S(2)}) collective-permute-start(bf16[2,256,1024]{2,1,0:T(8,128)(2,1)} %bitcast.17), channel_id=1, source_target_pairs={{0,4},{12,8},{1,5},{13,9},{2,6},{14,10},{3,7},{15,11},{16,20},{28,... | collective-permute-start | bytes 3145736 | tf_op jit(solution)/shard_map/inward_0/ppermute | solution.py:340
  188.7 8.3 %collective-permute-done.19 = bf16[512,1024]{1,0:T(8,128)(2,1)} collective-permute-done((bf16[512,1024]{1,0:T(8,128)(2,1)}, bf16[512,1024]{1,0:T(8,128)(2,1)}, u32[]{:S(2)}, u32[]{:S(2)}) %collective-permute-start.19) | collective-permute-done | bytes 1048608 | tf_op jit(solution)/shard_map/up_2_1/ppermute | solution.py:340
  199.7 5.1 %collective-permute-done.26.refs_0_.refs_1_ = bf16[2,256,1024]{2,1,0:T(8,128)(2,1)} collective-permute-done((bf16[2,256,1024]{2,1,0:T(8,128)(2,1)}, bf16[2,256,1024]{2,1,0:T(8,128)(2,1)}, u32[]{:S(2)}, u32[]{:S(2)}) %collective-permute-start.26) | collective-permute-done | bytes 1048608 | tf_op jit(solution)/shard_map/inward_0/ppermute | solution.py:340
  204.8 7.6 %collective-permute-done.32.refs_1_ = bf16[2,128,1024]{2,1,0:T(8,128)(2,1)S(1)} collective-permute-done((bf16[2,128,1024]{2,1,0:T(8,128)(2,1)}, bf16[2,128,1024]{2,1,0:T(8,128)(2,1)S(1)}, u32[]{:S(2)}, u32[]{:S(2)}) %collective-permute-start.32) | collective-permute-done | bytes 524320 | tf_op jit(solution)/shard_map/wave_5/ppermute | solution.py:340
  232.2 6.8 %collective-permute-done.36.refs_3_ = bf16[1,256,1024]{2,1,0:T(8,128)(2,1)S(1)} collective-permute-done((bf16[1,256,1024]{2,1,0:T(8,128)(2,1)S(1)}, bf16[1,256,1024]{2,1,0:T(8,128)(2,1)S(1)}, u32[]{:S(2)}, u32[]{:S(2)}) %collective-permute-start.36) | collective-permute-done | bytes 524320 | tf_op jit(solution)/shard_map/inward_3/ppermute | solution.py:340
  242.0 3.8 %product.8 = bf16[256,1024]{1,0:T(8,128)(2,1)S(1)} custom-call(s32[1]{0:T(128)} %bitcast.base_ref.turn_ref, s32[4]{0:T(128)S(1)} %iota.10.order_ref, bf16[7,256,1024]{2,1,0:T(8,128)(2,1)S(1)} %bitcast.61, bf16[7,256,1024]{2,1,0:T(8,128)(2,1)S(1)} %bitcast.62, bf16[7,256,1024]{2,1,0:T(8,128)(2,1)S(1)} %bitcast.63, bf16[7,256,1024]{2,1,0:T(8,128)(2,1)S(1)} %bitcast.64, ...), custom_call_target="tpu_custom_call" | custom-call | flops 2147483648 | bytes 11010048 | tf_op jit(solution)/shard_map/product/pallas_call | solution.py:309
  245.9 4.8 %product.6 = bf16[256,1024]{1,0:T(8,128)(2,1)S(1)} custom-call(s32[1]{0:T(128)} %bitcast.base_ref.turn_ref, s32[4]{0:T(128)S(1)} %pad_add_fusion.order_ref, bf16[7,256,1024]{2,1,0:T(8,128)(2,1)S(1)} %bitcast.65, bf16[7,256,1024]{2,1,0:T(8,128)(2,1)S(1)} %bitcast.66, bf16[7,256,1024]{2,1,0:T(8,128)(2,1)S(1)} %bitcast.67, bf16[7,256,1024]{2,1,0:T(8,128)(2,1)S(1)} %bitcast.68, ...), custom_call_target="tpu_custom_call" | custom-call | flops 2147483648 | bytes 11010048 | tf_op jit(solution)/shard_map/product/pallas_call | solution.py:309
  250.7 3.4 %collective-permute-start.44 = (bf16[256,1024]{1,0:T(8,128)(2,1)S(1)}, bf16[256,1024]{1,0:T(8,128)(2,1)S(1)}, u32[]{:S(2)}, u32[]{:S(2)}) collective-permute-start(bf16[256,1024]{1,0:T(8,128)(2,1)S(1)} %product.6), channel_id=1, source_target_pairs={{6,4},{10,8},{12,14},{7,5},{11,9},{13,15},{22,20},{26,24},{28,30},... | collective-permute-start | bytes 1572872 | tf_op jit(solution)/shard_map/ppermute | solution.py:652
  258.2 5.4 %product.7 = bf16[256,1024]{1,0:T(8,128)(2,1)S(1)} custom-call(s32[1]{0:T(128)} %bitcast.base_ref.turn_ref, s32[4]{0:T(128)S(1)} %pad_add_fusion.order_ref, bf16[7,256,1024]{2,1,0:T(8,128)(2,1)S(1)} %bitcast.69, bf16[7,256,1024]{2,1,0:T(8,128)(2,1)S(1)} %bitcast.70, bf16[7,256,1024]{2,1,0:T(8,128)(2,1)S(1)} %bitcast.71, bf16[7,256,1024]{2,1,0:T(8,128)(2,1)S(1)} %bitcast.72, ...), custom_call_target="tpu_custom_call" | custom-call | flops 2147483648 | bytes 11010048 | tf_op jit(solution)/shard_map/product/pallas_call | solution.py:309
  265.1 4.5 %product.5 = bf16[256,1024]{1,0:T(8,128)(2,1)S(1)} custom-call(s32[1]{0:T(128)} %bitcast.base_ref.turn_ref, s32[4]{0:T(128)S(1)} %pad_add_fusion.order_ref, bf16[7,256,1024]{2,1,0:T(8,128)(2,1)S(1)} %bitcast.73, bf16[7,256,1024]{2,1,0:T(8,128)(2,1)S(1)} %bitcast.74, bf16[7,256,1024]{2,1,0:T(8,128)(2,1)S(1)} %bitcast.75, bf16[7,256,1024]{2,1,0:T(8,128)(2,1)S(1)} %bitcast.76, ...), custom_call_target="tpu_custom_call" | custom-call | flops 2147483648 | bytes 11010048 | tf_op jit(solution)/shard_map/product/pallas_call | solution.py:309
  269.6 5.5 %product.9 = bf16[256,1024]{1,0:T(8,128)(2,1)} custom-call(s32[1]{0:T(128)} %bitcast.base_ref.turn_ref, s32[4]{0:T(128)S(1)} %pad_add_fusion.order_ref, bf16[2,256,1024]{2,1,0:T(8,128)(2,1)} %collective-permute-done.26.refs_0_.refs_1_, bf16[2,256,1024]{2,1,0:T(8,128)(2,1)} %collective-permute-done.26.refs_0_.refs_1_, ...), custom_call_target="tpu_custom_call" | custom-call | flops 2147483648 | bytes 11010048 | tf_op jit(solution)/shard_map/product/pallas_call | solution.py:309
  275.1 5.1 %collective-permute-start.46 = (bf16[256,1024]{1,0:T(8,128)(2,1)S(1)}, bf16[256,1024]{1,0:T(8,128)(2,1)}, u32[]{:S(2)}, u32[]{:S(2)}) collective-permute-start(bf16[256,1024]{1,0:T(8,128)(2,1)S(1)} %product.8), channel_id=1, source_target_pairs={{2,0},{6,4},{8,10},{12,14},{3,1},{7,5},{9,11},{13,15},{18,16},{22,... | collective-permute-start | bytes 1572872 | tf_op jit(solution)/shard_map/ppermute | solution.py:652
  284.4 4.9 %collective-permute-done.50.refs_2_ = bf16[4,2,32,1024]{3,2,1,0:T(8,128)(2,1)S(1)} collective-permute-done((bf16[4,2,32,1024]{3,2,1,0:T(8,128)(2,1)S(1)}, bf16[4,2,32,1024]{3,2,1,0:T(8,128)(2,1)S(1)}, u32[]{:S(2)}, u32[]{:S(2)}) %collective-permute-start.50) | collective-permute-done | bytes 524320 | tf_op jit(solution)/shard_map/ppermute | solution.py:575
  294.7 3.3 %final_part.1 = f32[2,64,32,64]{3,2,1,0:T(8,128)} custom-call(s32[1]{0:T(128)} %bitcast.base_ref.turn_ref, bf16[4,2,32,1024]{3,2,1,0:T(8,128)(2,1)S(1)} %copy-done.40, bf16[4,2,32,1024]{3,2,1,0:T(8,128)(2,1)S(1)} %copy-done.42, bf16[4,2,32,1024]{3,2,1,0:T(8,128)(2,1)S(1)} %copy-done.44, bf16[4,2,32,1024]{3,2,1,0:T(8,128)(2,1)S(1)} %pad_maximum_fusion.4.refs_3_), custom_call_target="tpu_custom_call" | custom-call | tf_op jit(solution)/shard_map/final_part/pallas_call | solution.py:208
  298.0 9.2 %collective-permute-done.43 = bf16[256,1024]{1,0:T(8,128)(2,1)} collective-permute-done((bf16[256,1024]{1,0:T(8,128)(2,1)S(1)}, bf16[256,1024]{1,0:T(8,128)(2,1)}, u32[]{:S(2)}, u32[]{:S(2)}) %collective-permute-start.43) | collective-permute-done | bytes 524320 | tf_op jit(solution)/shard_map/ppermute | solution.py:652
  (271 shorter events, 130.2 us)
Async XLA Ops:
  9.0 31.4 %collective-permute-start.2 = (bf16[512,1024]{1,0:T(8,128)(2,1)}, bf16[512,1024]{1,0:T(8,128)(2,1)S(1)}, u32[]{:S(2)}, u32[]{:S(2)}) collective-permute-start(bf16[512,1024]{1,0:T(8,128)(2,1)} %get-tuple-element.102), channel_id=1, source_target_pairs={{0,4},{4,8},{8,12},{1,5},{5,9},{9,13},{2,6},{6,10},{10,14},{3,7},{... | collective-permute-start | bytes 3145736 | tf_op jit(solution)/shard_map/up_1_0/ppermute | solution.py:340
  12.9 46.7 %collective-permute-start.1 = (bf16[512,1024]{1,0:T(8,128)(2,1)}, bf16[512,1024]{1,0:T(8,128)(2,1)}, u32[]{:S(2)}, u32[]{:S(2)}) collective-permute-start(bf16[512,1024]{1,0:T(8,128)(2,1)} %get-tuple-element.100), channel_id=1, source_target_pairs={{0,4},{4,8},{8,12},{1,5},{5,9},{9,13},{2,6},{6,10},{10,14},{3,7},{... | collective-permute-start | bytes 3145736 | tf_op jit(solution)/shard_map/up_1_1/ppermute | solution.py:340
  15.0 25.4 %collective-permute-start.3 = (bf16[2,2,32,1024]{3,2,1,0:T(8,128)(2,1)S(1)}, bf16[2,2,32,1024]{3,2,1,0:T(8,128)(2,1)S(1)}, u32[]{:S(2)}, u32[]{:S(2)}) collective-permute-start(bf16[2,2,32,1024]{3,2,1,0:T(8,128)(2,1)S(1)} %get-tuple-element.88.refs_1_.refs_2_), channel_id=1, source_target_pairs={{4,0},{5,1},{6,2},{7,3},{20,16},{21,17},{22,18},{23,19}} | collective-permute-start | bytes 786440 | tf_op jit(solution)/shard_map/first_0_1/ppermute | solution.py:340
  15.7 24.7 %collective-permute-start.4 = (bf16[2,2,32,1024]{3,2,1,0:T(8,128)(2,1)S(1)}, bf16[2,2,32,1024]{3,2,1,0:T(8,128)(2,1)S(1)}, u32[]{:S(2)}, u32[]{:S(2)}) collective-permute-start(bf16[2,2,32,1024]{3,2,1,0:T(8,128)(2,1)S(1)} %get-tuple-element.88.refs_1_.refs_2_), channel_id=1, source_target_pairs={{8,0},{9,1},{10,2},{11,3},{24,16},{25,17},{26,18},{27,19}} | collective-permute-start | bytes 786440 | tf_op jit(solution)/shard_map/first_0_2/ppermute | solution.py:340
  45.5 43.3 %collective-permute-start.9 = (bf16[512,1024]{1,0:T(8,128)(2,1)}, bf16[512,1024]{1,0:T(8,128)(2,1)}, u32[]{:S(2)}, u32[]{:S(2)}) collective-permute-start(bf16[512,1024]{1,0:T(8,128)(2,1)} %get-tuple-element.102), channel_id=1, source_target_pairs={{4,0},{8,4},{12,8},{5,1},{9,5},{13,9},{6,2},{10,6},{14,10},{7,3},{... | collective-permute-start | bytes 3145736 | tf_op jit(solution)/shard_map/down_1_0/ppermute | solution.py:340
  48.4 43.9 %collective-permute-start.10 = (bf16[512,1024]{1,0:T(8,128)(2,1)S(1)}, bf16[512,1024]{1,0:T(8,128)(2,1)}, u32[]{:S(2)}, u32[]{:S(2)}) collective-permute-start(bf16[512,1024]{1,0:T(8,128)(2,1)S(1)} %collective-permute-done.2.refs_4_), channel_id=1, source_target_pairs={{4,8},{8,12},{5,9},{9,13},{6,10},{10,14},{7,11},{11,15},{20,24},{2... | collective-permute-start | bytes 3145736 | tf_op jit(solution)/shard_map/up_2_0/ppermute | solution.py:340
  49.7 42.6 %collective-permute-start.11 = (bf16[512,1024]{1,0:T(8,128)(2,1)S(1)}, bf16[512,1024]{1,0:T(8,128)(2,1)}, u32[]{:S(2)}, u32[]{:S(2)}) collective-permute-start(bf16[512,1024]{1,0:T(8,128)(2,1)S(1)} %collective-permute-done.2.refs_4_), channel_id=1, source_target_pairs={{4,20},{8,24},{12,28},{20,4},{24,8},{28,12},{5,21},{9,25},{13,29},... | collective-permute-start | bytes 3145736 | tf_op jit(solution)/shard_map/part_3_0_1_0/ppermute | solution.py:340
  79.8 28.6 %collective-permute-start.7 = (bf16[512,1024]{1,0:T(8,128)(2,1)S(1)}, bf16[512,1024]{1,0:T(8,128)(2,1)}, u32[]{:S(2)}, u32[]{:S(2)}) collective-permute-start(bf16[512,1024]{1,0:T(8,128)(2,1)S(1)} %copy-done.59), channel_id=1, source_target_pairs={{4,0},{8,4},{12,8},{5,1},{9,5},{13,9},{6,2},{10,6},{14,10},{7,3},{... | collective-permute-start | bytes 3145736 | tf_op jit(solution)/shard_map/down_1_1/ppermute | solution.py:340
  88.8 24.9 %collective-permute-start.8 = (bf16[512,1024]{1,0:T(8,128)(2,1)}, bf16[512,1024]{1,0:T(8,128)(2,1)}, u32[]{:S(2)}, u32[]{:S(2)}) collective-permute-start(bf16[512,1024]{1,0:T(8,128)(2,1)} %collective-permute-done.1.refs_5_), channel_id=1, source_target_pairs={{4,20},{8,24},{12,28},{20,4},{24,8},{28,12},{5,21},{9,25},{13,29},... | collective-permute-start | bytes 3145736 | tf_op jit(solution)/shard_map/part_3_1_1_0/ppermute | solution.py:340
  92.3 26.8 %collective-permute-start.17 = (bf16[512,1024]{1,0:T(8,128)(2,1)S(1)}, bf16[512,1024]{1,0:T(8,128)(2,1)S(1)}, u32[]{:S(2)}, u32[]{:S(2)}) collective-permute-start(bf16[512,1024]{1,0:T(8,128)(2,1)S(1)} %collective-permute-done.2.refs_4_), channel_id=1, source_target_pairs={{4,5},{5,4},{8,9},{9,8},{12,13},{13,12},{6,7},{7,6},{10,11},{11,10... | collective-permute-start | bytes 3145736 | tf_op jit(solution)/shard_map/part_3_0_0_1/ppermute | solution.py:340
  94.2 25.8 %collective-permute-start.18 = (bf16[512,1024]{1,0:T(8,128)(2,1)}, bf16[512,1024]{1,0:T(8,128)(2,1)S(1)}, u32[]{:S(2)}, u32[]{:S(2)}) collective-permute-start(bf16[512,1024]{1,0:T(8,128)(2,1)} %collective-permute-done.11.refs_8_), channel_id=1, source_target_pairs={{4,5},{5,4},{8,9},{9,8},{12,13},{13,12},{6,7},{7,6},{10,11},{11,10... | collective-permute-start | bytes 3145736 | tf_op jit(solution)/shard_map/part_3_0_1_1/ppermute | solution.py:340
  108.3 24.8 %collective-permute-start.20 = (bf16[512,1024]{1,0:T(8,128)(2,1)}, bf16[512,1024]{1,0:T(8,128)(2,1)}, u32[]{:S(2)}, u32[]{:S(2)}) collective-permute-start(bf16[512,1024]{1,0:T(8,128)(2,1)} %collective-permute-done.9.refs_4_), channel_id=1, source_target_pairs={{4,0},{8,4},{5,1},{9,5},{6,2},{10,6},{7,3},{11,7},{20,16},{24,20},... | collective-permute-start | bytes 3145736 | tf_op jit(solution)/shard_map/down_2_0/ppermute | solution.py:340
  121.1 26.7 %collective-permute-start.23 = (bf16[512,1024]{1,0:T(8,128)(2,1)}, bf16[512,1024]{1,0:T(8,128)(2,1)S(1)}, u32[]{:S(2)}, u32[]{:S(2)}) collective-permute-start(bf16[512,1024]{1,0:T(8,128)(2,1)} %collective-permute-done.1.refs_5_), channel_id=1, source_target_pairs={{4,5},{5,4},{8,9},{9,8},{12,13},{13,12},{6,7},{7,6},{10,11},{11,10... | collective-permute-start | bytes 3145736 | tf_op jit(solution)/shard_map/part_3_1_0_1/ppermute | solution.py:340
  123.0 25.8 %collective-permute-start.24 = (bf16[512,1024]{1,0:T(8,128)(2,1)}, bf16[512,1024]{1,0:T(8,128)(2,1)}, u32[]{:S(2)}, u32[]{:S(2)}) collective-permute-start(bf16[512,1024]{1,0:T(8,128)(2,1)} %collective-permute-done.8.refs_9_), channel_id=1, source_target_pairs={{4,5},{5,4},{8,9},{9,8},{12,13},{13,12},{6,7},{7,6},{10,11},{11,10... | collective-permute-start | bytes 3145736 | tf_op jit(solution)/shard_map/part_3_1_1_1/ppermute | solution.py:340
  133.1 25.7 %collective-permute-start.27 = (bf16[512,1024]{1,0:T(8,128)(2,1)}, bf16[512,1024]{1,0:T(8,128)(2,1)}, u32[]{:S(2)}, u32[]{:S(2)}) collective-permute-start(bf16[512,1024]{1,0:T(8,128)(2,1)} %collective-permute-done.7.refs_5_), channel_id=1, source_target_pairs={{4,0},{8,4},{5,1},{9,5},{6,2},{10,6},{7,3},{11,7},{20,16},{24,20},... | collective-permute-start | bytes 3145736 | tf_op jit(solution)/shard_map/down_2_1/ppermute | solution.py:340
  137.1 37.7 %collective-permute-start.28 = (bf16[512,1024]{1,0:T(8,128)(2,1)}, bf16[512,1024]{1,0:T(8,128)(2,1)}, u32[]{:S(2)}, u32[]{:S(2)}) collective-permute-start(bf16[512,1024]{1,0:T(8,128)(2,1)} %collective-permute-done.7.refs_5_), channel_id=1, source_target_pairs={{0,16},{4,20},{8,24},{16,0},{20,4},{24,8},{1,17},{5,21},{9,25},{17... | collective-permute-start | bytes 3145736 | tf_op jit(solution)/shard_map/part_1_1_1_0/ppermute | solution.py:340
  148.8 34.4 %collective-permute-start.30 = (bf16[512,1024]{1,0:T(8,128)(2,1)}, bf16[512,1024]{1,0:T(8,128)(2,1)}, u32[]{:S(2)}, u32[]{:S(2)}) collective-permute-start(bf16[512,1024]{1,0:T(8,128)(2,1)} %collective-permute-done.9.refs_4_), channel_id=1, source_target_pairs={{0,1},{1,0},{4,5},{5,4},{8,9},{9,8},{2,3},{3,2},{6,7},{7,6},{10,11... | collective-permute-start | bytes 3145736 | tf_op jit(solution)/shard_map/part_1_0_0_1/ppermute | solution.py:340
  150.5 32.7 %collective-permute-start.31 = (bf16[512,1024]{1,0:T(8,128)(2,1)}, bf16[512,1024]{1,0:T(8,128)(2,1)}, u32[]{:S(2)}, u32[]{:S(2)}) collective-permute-start(bf16[512,1024]{1,0:T(8,128)(2,1)} %collective-permute-done.21.refs_8_), channel_id=1, source_target_pairs={{0,1},{1,0},{4,5},{5,4},{8,9},{9,8},{2,3},{3,2},{6,7},{7,6},{10,11... | collective-permute-start | bytes 3145736 | tf_op jit(solution)/shard_map/part_1_0_1_1/ppermute | solution.py:340
  158.8 38.2 %collective-permute-start.19 = (bf16[512,1024]{1,0:T(8,128)(2,1)}, bf16[512,1024]{1,0:T(8,128)(2,1)}, u32[]{:S(2)}, u32[]{:S(2)}) collective-permute-start(bf16[512,1024]{1,0:T(8,128)(2,1)} %collective-permute-done.1.refs_5_), channel_id=1, source_target_pairs={{4,8},{8,12},{5,9},{9,13},{6,10},{10,14},{7,11},{11,15},{20,24},{2... | collective-permute-start | bytes 3145736 | tf_op jit(solution)/shard_map/up_2_1/ppermute | solution.py:340
  174.8 24.9 %collective-permute-start.25 = (bf16[512,1024]{1,0:T(8,128)(2,1)}, bf16[512,1024]{1,0:T(8,128)(2,1)}, u32[]{:S(2)}, u32[]{:S(2)}) collective-permute-start(bf16[512,1024]{1,0:T(8,128)(2,1)} %broadcast_select_fusion.1.refs_4_), channel_id=1, source_target_pairs={{0,16},{4,20},{8,24},{12,28},{16,0},{20,4},{24,8},{28,12},{1,17},{... | collective-permute-start | bytes 3145736 | tf_op jit(solution)/shard_map/part_2_0_1_0/ppermute | solution.py:340
  176.3 28.5 %collective-permute-start.26 = (bf16[2,256,1024]{2,1,0:T(8,128)(2,1)}, bf16[2,256,1024]{2,1,0:T(8,128)(2,1)}, u32[]{:S(2)}, u32[]{:S(2)}) collective-permute-start(bf16[2,256,1024]{2,1,0:T(8,128)(2,1)} %bitcast.17), channel_id=1, source_target_pairs={{0,4},{12,8},{1,5},{13,9},{2,6},{14,10},{3,7},{15,11},{16,20},{28,... | collective-permute-start | bytes 3145736 | tf_op jit(solution)/shard_map/inward_0/ppermute | solution.py:340
  183.2 29.2 %collective-permute-start.33 = (bf16[512,1024]{1,0:T(8,128)(2,1)}, bf16[512,1024]{1,0:T(8,128)(2,1)}, u32[]{:S(2)}, u32[]{:S(2)}) collective-permute-start(bf16[512,1024]{1,0:T(8,128)(2,1)} %collective-permute-done.7.refs_5_), channel_id=1, source_target_pairs={{0,1},{1,0},{4,5},{5,4},{8,9},{9,8},{2,3},{3,2},{6,7},{7,6},{10,11... | collective-permute-start | bytes 3145736 | tf_op jit(solution)/shard_map/part_1_1_0_1/ppermute | solution.py:340
  184.8 27.6 %collective-permute-start.34 = (bf16[512,1024]{1,0:T(8,128)(2,1)}, bf16[512,1024]{1,0:T(8,128)(2,1)}, u32[]{:S(2)}, u32[]{:S(2)}) collective-permute-start(bf16[512,1024]{1,0:T(8,128)(2,1)} %collective-permute-done.28.refs_9_), channel_id=1, source_target_pairs={{0,1},{1,0},{4,5},{5,4},{8,9},{9,8},{2,3},{3,2},{6,7},{7,6},{10,11... | collective-permute-start | bytes 3145736 | tf_op jit(solution)/shard_map/part_1_1_1_1/ppermute | solution.py:340
  212.5 26.5 %collective-permute-start.35 = (bf16[512,1024]{1,0:T(8,128)(2,1)S(1)}, bf16[512,1024]{1,0:T(8,128)(2,1)S(1)}, u32[]{:S(2)}, u32[]{:S(2)}) collective-permute-start(bf16[512,1024]{1,0:T(8,128)(2,1)S(1)} %broadcast_select_fusion.refs_5_), channel_id=1, source_target_pairs={{0,16},{4,20},{8,24},{12,28},{16,0},{20,4},{24,8},{28,12},{1,17},{... | collective-permute-start | bytes 3145736 | tf_op jit(solution)/shard_map/part_2_1_1_0/ppermute | solution.py:340
  239.0 24.6 %collective-permute-start.41 = (bf16[512,1024]{1,0:T(8,128)(2,1)S(1)}, bf16[512,1024]{1,0:T(8,128)(2,1)S(1)}, u32[]{:S(2)}, u32[]{:S(2)}) collective-permute-start(bf16[512,1024]{1,0:T(8,128)(2,1)S(1)} %collective-permute-done.35.refs_9_), channel_id=1, source_target_pairs={{0,1},{1,0},{4,5},{5,4},{8,9},{9,8},{12,13},{13,12},{2,3},{3,2},{6... | collective-permute-start | bytes 3145736 | tf_op jit(solution)/shard_map/part_2_1_1_1/ppermute | solution.py:340
  250.7 24.4 %collective-permute-start.44 = (bf16[256,1024]{1,0:T(8,128)(2,1)S(1)}, bf16[256,1024]{1,0:T(8,128)(2,1)S(1)}, u32[]{:S(2)}, u32[]{:S(2)}) collective-permute-start(bf16[256,1024]{1,0:T(8,128)(2,1)S(1)} %product.6), channel_id=1, source_target_pairs={{6,4},{10,8},{12,14},{7,5},{11,9},{13,15},{22,20},{26,24},{28,30},... | collective-permute-start | bytes 1572872 | tf_op jit(solution)/shard_map/ppermute | solution.py:652
  254.2 26.0 %collective-permute-start.48 = (bf16[4,2,32,1024]{3,2,1,0:T(8,128)(2,1)S(1)}, bf16[4,2,32,1024]{3,2,1,0:T(8,128)(2,1)S(1)}, u32[]{:S(2)}, u32[]{:S(2)}) collective-permute-start(bf16[4,2,32,1024]{3,2,1,0:T(8,128)(2,1)S(1)} %pad_maximum_fusion.1), channel_id=1, source_target_pairs={{12,0},{13,1},{14,2},{15,3},{28,16},{29,17},{30,18},{31,19}} | collective-permute-start | bytes 1572872 | tf_op jit(solution)/shard_map/ppermute | solution.py:575
  255.5 26.7 %collective-permute-start.49 = (bf16[4,2,32,1024]{3,2,1,0:T(8,128)(2,1)S(1)}, bf16[4,2,32,1024]{3,2,1,0:T(8,128)(2,1)S(1)}, u32[]{:S(2)}, u32[]{:S(2)}) collective-permute-start(bf16[4,2,32,1024]{3,2,1,0:T(8,128)(2,1)S(1)} %pad_maximum_fusion.2), channel_id=1, source_target_pairs={{12,4},{13,5},{14,6},{15,7},{28,20},{29,21},{30,22},{31,23}} | collective-permute-start | bytes 1572872 | tf_op jit(solution)/shard_map/ppermute | solution.py:575
  256.9 32.4 %collective-permute-start.50 = (bf16[4,2,32,1024]{3,2,1,0:T(8,128)(2,1)S(1)}, bf16[4,2,32,1024]{3,2,1,0:T(8,128)(2,1)S(1)}, u32[]{:S(2)}, u32[]{:S(2)}) collective-permute-start(bf16[4,2,32,1024]{3,2,1,0:T(8,128)(2,1)S(1)} %pad_maximum_fusion.3), channel_id=1, source_target_pairs={{12,8},{13,9},{14,10},{15,11},{28,24},{29,25},{30,26},{31,27}} | collective-permute-start | bytes 1572872 | tf_op jit(solution)/shard_map/ppermute | solution.py:575
  263.7 34.4 %collective-permute-start.45 = (bf16[256,1024]{1,0:T(8,128)(2,1)S(1)}, bf16[256,1024]{1,0:T(8,128)(2,1)}, u32[]{:S(2)}, u32[]{:S(2)}) collective-permute-start(bf16[256,1024]{1,0:T(8,128)(2,1)S(1)} %product.7), channel_id=1, source_target_pairs={{2,0},{4,6},{8,10},{3,1},{5,7},{9,11},{18,16},{20,22},{24,26},{19,... | collective-permute-start | bytes 1572872 | tf_op jit(solution)/shard_map/ppermute | solution.py:652
  281.0 26.2 %collective-permute-start.43 = (bf16[256,1024]{1,0:T(8,128)(2,1)S(1)}, bf16[256,1024]{1,0:T(8,128)(2,1)}, u32[]{:S(2)}, u32[]{:S(2)}) collective-permute-start(bf16[256,1024]{1,0:T(8,128)(2,1)S(1)} %product.5), channel_id=1, source_target_pairs={{0,2},{4,6},{10,8},{14,12},{1,3},{5,7},{11,9},{15,13},{16,18},{20,... | collective-permute-start | bytes 1572872 | tf_op jit(solution)/shard_map/ppermute | solution.py:652
  283.1 24.1 %collective-permute-start.47 = (bf16[256,1024]{1,0:T(8,128)(2,1)}, bf16[256,1024]{1,0:T(8,128)(2,1)}, u32[]{:S(2)}, u32[]{:S(2)}) collective-permute-start(bf16[256,1024]{1,0:T(8,128)(2,1)} %product.9), channel_id=1, source_target_pairs={{4,2},{10,12},{5,3},{11,13},{20,18},{26,28},{21,19},{27,29}} | collective-permute-start | bytes 1572872 | tf_op jit(solution)/shard_map/ppermute | solution.py:659
  (88 other events, 856.5 us)

commit v3 on v0

v3 whole, which is shorter than its diff:
```python
import functools

import jax
import jax.numpy as jnp
from jax import lax
from jax.experimental import pallas as pl
from jax.experimental.pallas import tpu as pltpu
from jax.sharding import PartitionSpec as P

HEADS = 128
GROUPS = 8
SPAN = 128
GROUP_HEADS = HEADS // GROUPS
TILE = 512
VMEM = 20 * 1024 * 1024

norm_eps = 1e-05
far = -1e30


def spread(values, head_dim):
    heads = values.shape[1]
    high = values.astype(jnp.bfloat16)
    low = (values - high.astype(jnp.float32)).astype(jnp.bfloat16)
    both = jnp.concatenate([high, low], axis=1)
    row = lax.broadcasted_iota(jnp.int32, (2 * heads, heads * head_dim), 0)
    col = lax.broadcasted_iota(jnp.int32, (2 * heads, heads * head_dim), 1)
    ones = (col // head_dim == row % heads).astype(jnp.bfloat16)
    return jnp.dot(both, ones, preferred_element_type=jnp.float32)


def decays(limit_ref, raw_ref, bias_ref, rate_ref):
    heads, tokens = raw_ref.shape[2:]
    f32 = jnp.float32
    token = lax.broadcasted_iota(jnp.int32, (heads, tokens), 1)
    size = jax.nn.softplus(raw_ref[0, 0] + bias_ref[0])
    size = size * (token < limit_ref[pl.program_id(0)]).astype(f32)
    log_keep = -jnp.exp(rate_ref[0]) * size
    row = lax.broadcasted_iota(jnp.int32, (tokens, tokens), 0)
    col = lax.broadcasted_iota(jnp.int32, (tokens, tokens), 1)
    cum = jnp.dot(log_keep, (row <= col).astype(f32), precision=lax.Precision.HIGHEST)
    return size, cum, row >= col


def end_kernel(
    limit_ref, x_ref, b_ref, raw_ref, bias_ref, rate_ref, end_ref, keep_ref, grow_ref
):
    tokens, width = x_ref.shape[1:]
    heads = raw_ref.shape[2]
    head_dim = width // heads
    f32 = jnp.float32
    size, cum, _ = decays(limit_ref, raw_ref, bias_ref, rate_ref)
    last = cum[:, tokens - 1 : tokens]
    tail = spread((jnp.exp(last - cum) * size).T, head_dim)
    weighted = (tail * x_ref[0].astype(f32)).astype(jnp.bfloat16)
    b_t = b_ref[0, 0].astype(f32).T.astype(jnp.bfloat16)
    end_ref[0, 0] = jnp.dot(b_t, weighted, preferred_element_type=f32)
    grow = jnp.exp(cum.T)
    keep_ref[0, 0] = spread(jnp.broadcast_to(grow[tokens - 1 :], (8, heads)), head_dim)
    grow_ref[0, 0] = grow


def inside_kernel(
    limit_ref, x_ref, b_ref, c_ref, raw_ref, bias_ref, rate_ref, skip_ref, y_ref
):
    tokens, width = x_ref.shape[1:]
    heads = raw_ref.shape[2]
    head_dim = width // heads
    f32 = jnp.float32
    size, cum, causal = decays(limit_ref, raw_ref, bias_ref, rate_ref)
    cum_t = cum.T
    shifted = cum - jnp.where(size > 0, jnp.log(jnp.where(size > 0, size, 1.0)), far)
    scores = lax.dot_general(
        c_ref[0, 0], b_ref[0, 0], (((1,), (1,)), ((), ())), preferred_element_type=f32
    )
    lane = lax.broadcasted_iota(jnp.int32, (tokens, 2 * head_dim), 1)
    for pair in range(heads // 2):
        decayed = []
        for head in (2 * pair, 2 * pair + 1):
            gap = cum_t[:, head : head + 1] - shifted[head : head + 1, :]
            decayed.append((scores * jnp.exp(jnp.where(causal, gap, far))).astype(jnp.bfloat16))
        here = pl.ds(pair * 2 * head_dim, 2 * head_dim)
        x = x_ref[0, :, here]
        zero = jnp.zeros_like(x)
        apart = jnp.concatenate(
            [jnp.where(lane < head_dim, x, zero), jnp.where(lane >= head_dim, x, zero)], axis=0
        )
        y = jnp.dot(jnp.concatenate(decayed, axis=1), apart, preferred_element_type=f32)
        y_ref[0, :, here] = y + skip_ref[0, :, here] * x.astype(f32)


def local_specs(x, b, raw):
    tokens, width = x.shape[1], x.shape[2] // b.shape[1]
    state, heads = b.shape[3], raw.shape[2]

    def by_group(*block):
        return pl.BlockSpec((1, *block), lambda s, g, _: (g, 0, 0))

    def by_both(*block):
        return pl.BlockSpec((1, 1, *block), lambda s, g, _: (s, g, 0, 0))

    flat = pl.BlockSpec((1, tokens, width), lambda s, g, _: (s, 0, g))
    return (
        flat,
        by_both(tokens, state),
        by_both(heads, tokens),
        by_group(heads, 1),
        by_group(1, width),
    )


def end_part(limits, x, b, raw, bias, rate):
    sessions, tokens, inner = x.shape
    groups, state, heads = b.shape[1], b.shape[3], raw.shape[2]
    width = inner // groups
    flat, proj, per_token, per_head, _ = local_specs(x, b, raw)
    f32 = jnp.float32
    by_turn = lambda s, g, _: (g, s, 0, 0)
    return pl.pallas_call(
        end_kernel,
        grid_spec=pltpu.PrefetchScalarGridSpec(
            num_scalar_prefetch=1,
            grid=(sessions, groups),
            in_specs=[flat, proj, per_token, per_head, per_head],
            out_specs=[
                pl.BlockSpec((1, 1, state, width), by_turn),
                pl.BlockSpec((1, 1, 8, width), by_turn),
                pl.BlockSpec((1, 1, tokens, heads), lambda s, g, _: (s, g, 0, 0)),
            ],
        ),
        out_shape=[
            jax.ShapeDtypeStruct((groups, sessions, state, width), f32),
            jax.ShapeDtypeStruct((groups, sessions, 8, width), f32),
            jax.ShapeDtypeStruct((sessions, groups, tokens, heads), f32),
        ],
        compiler_params=pltpu.CompilerParams(vmem_limit_bytes=VMEM),
        cost_estimate=pl.CostEstimate(
            flops=2 * 10**9, bytes_accessed=8 * 2**20, transcendentals=2**18
        ),
        name="end_part",
    )(limits, x, b, raw, bias[:, :, None], rate[:, :, None])


def inside_part(limits, x, b, c, raw, bias, rate, skip):
    sessions, tokens, inner = x.shape
    groups = b.shape[1]
    flat, proj, per_token, per_head, per_channel = local_specs(x, b, raw)
    return pl.pallas_call(
        inside_kernel,
        grid_spec=pltpu.PrefetchScalarGridSpec(
            num_scalar_prefetch=1,
            grid=(sessions, groups),
            in_specs=[flat, proj, proj, per_token, per_head, per_head, per_channel],
            out_specs=flat,
        ),
        out_shape=jax.ShapeDtypeStruct((sessions, tokens, inner), jnp.float32),
        compiler_params=pltpu.CompilerParams(vmem_limit_bytes=VMEM),
        cost_estimate=pl.CostEstimate(
            flops=4 * 10**9, bytes_accessed=8 * 2**20, transcendentals=2**22
        ),
        name="inside_part",
    )(limits, x, b, c, raw, bias[:, :, None], rate[:, :, None], skip)


def leave_kernel(count, kind, *refs):
    at_ref, refs = refs[0], refs[1:]
    keep_ref, end_ref, state_ref, leaving_ref = refs[-4:]
    state = None
    if kind != "only":
        state = refs[0][0].astype(jnp.float32)
        refs = refs[1:]
    if count:
        first = jnp.concatenate([r[0, 0].astype(jnp.float32) for r in refs[:count]], axis=0)
        state = first if state is None else jnp.where(at_ref[1] == 0, first, state)
    state_ref[0] = state.astype(jnp.bfloat16)
    leaving_ref[0] = (keep_ref[0, 0, :1] * state + end_ref[0, 0]).astype(jnp.bfloat16)


def leave_part(at, coming, first, inside, keep, end):
    groups, sessions, state_size, width = end.shape
    by_turn = lambda s, at: (at[0], s, 0, 0)
    whole = pl.BlockSpec((1, state_size, width), lambda s, at: (s, 0, 0))
    operands, specs = [], []
    if coming is not None:
        operands.append(coming)
        specs.append(whole)
    if first is not None:
        operands += first
        specs += [
            pl.BlockSpec((1, 1, *f.shape[2:]), lambda s, at: (inside, s, 0, 0)) for f in first
        ]
    operands += [keep, end]
    specs += [
        pl.BlockSpec((1, 1, *keep.shape[2:]), by_turn),
        pl.BlockSpec((1, 1, state_size, width), by_turn),
    ]
    kind = None if first is None else ("only" if coming is None else "both")
    shape = jax.ShapeDtypeStruct((sessions, state_size, width), jnp.bfloat16)
    return pl.pallas_call(
        functools.partial(leave_kernel, 0 if first is None else len(first), kind),
        grid_spec=pltpu.PrefetchScalarGridSpec(
            num_scalar_prefetch=1, grid=(sessions,), in_specs=specs, out_specs=[whole, whole]
        ),
        out_shape=[shape, shape],
        compiler_params=pltpu.CompilerParams(vmem_limit_bytes=VMEM),
        cost_estimate=pl.CostEstimate(flops=10**6, bytes_accessed=3 * 2**20, transcendentals=0),
        name="leave_part",
    )(at, *operands)


def normed_kernel(at_ref, state_ref, c_ref, grow_ref, y_ref, gate_ref, gain_ref, _, out_ref):
    width = y_ref.shape[2]
    heads = grow_ref.shape[3]
    from_state = jnp.dot(c_ref[0, 0], state_ref[0], preferred_element_type=jnp.float32)
    ssd_out = y_ref[0] + from_state * spread(grow_ref[0, 0], width // heads)
    gate = gate_ref[0].astype(jnp.float32)
    gated = ssd_out * (gate / (1.0 + jnp.exp(-gate)))
    scale = lax.rsqrt(jnp.mean(gated * gated, axis=1, keepdims=True) + norm_eps)
    out_ref[0, 0] = (gated * scale * gain_ref[0]).astype(jnp.bfloat16)


def normed_part(index, at, state, c, grow, y, gate, gain, normed):
    sessions, tokens, inner = y.shape
    groups, state_size = c.shape[1], c.shape[3]
    width = inner // groups
    heads = grow.shape[3]
    by_both = lambda s, at: (s, at[0], 0, 0)
    flat = pl.BlockSpec((1, tokens, width), lambda s, at: (s, 0, at[0]))
    return pl.pallas_call(
        normed_kernel,
        grid_spec=pltpu.PrefetchScalarGridSpec(
            num_scalar_prefetch=1,
            grid=(sessions,),
            in_specs=[
                pl.BlockSpec((1, state_size, width), lambda s, at: (s, 0, 0)),
                pl.BlockSpec((1, 1, tokens, state_size), by_both),
                pl.BlockSpec((1, 1, tokens, heads), by_both),
                flat,
                flat,
                pl.BlockSpec((1, 1, width), lambda s, at: (at[0], 0, 0)),
                pl.BlockSpec(memory_space=pl.ANY),
            ],
            out_specs=pl.BlockSpec((1, 1, tokens, width), lambda s, at: (index, s, 0, 0)),
        ),
        out_shape=jax.ShapeDtypeStruct(normed.shape, normed.dtype),
        input_output_aliases={7: 0},
        compiler_params=pltpu.CompilerParams(vmem_limit_bytes=VMEM),
        cost_estimate=pl.CostEstimate(
            flops=10**8, bytes_accessed=4 * 2**20, transcendentals=2**19
        ),
        name="normed_part",
    )(at, state, c, grow, y, gate, gain, normed)


def pick_kernel(slot_ref, pool_ref, out_ref):
    heads, cols, head_dim = pool_ref.shape[1:]
    groups = out_ref.shape[0]
    per = heads // groups
    for g in range(groups):
        held = [pool_ref[0, g * per + h] for h in range(per)]
        out_ref[g, 0] = jnp.concatenate(held, axis=1).astype(jnp.bfloat16)


def pick_part(asked, pool, groups):
    _, heads, cols, head_dim = pool.shape
    count = asked.shape[0]
    width = heads // groups * head_dim
    return pl.pallas_call(
        pick_kernel,
        grid_spec=pltpu.PrefetchScalarGridSpec(
            num_scalar_prefetch=1,
            grid=(count,),
            in_specs=[pl.BlockSpec((1, heads, cols, head_dim), lambda i, slot: (slot[i], 0, 0, 0))],
            out_specs=pl.BlockSpec((groups, 1, cols, width), lambda i, slot: (0, i, 0, 0)),
        ),
        out_shape=jax.ShapeDtypeStruct((groups, count, cols, width), jnp.bfloat16),
        compiler_params=pltpu.CompilerParams(vmem_limit_bytes=VMEM),
        name="pick_part",
    )(asked, pool)


def final_kernel(value_ref, out_ref):
    heads, _, head_dim = out_ref.shape[1:]
    value = value_ref[0, 0].astype(jnp.float32)
    for h in range(heads):
        out_ref[0, h] = value[:, h * head_dim : (h + 1) * head_dim]


def final_part(value, heads, head_dim):
    groups, sessions, cols, width = value.shape
    per = heads // groups
    return pl.pallas_call(
        final_kernel,
        grid=(sessions, groups),
        in_specs=[pl.BlockSpec((1, 1, cols, width), lambda s, g: (g, s, 0, 0))],
        out_specs=pl.BlockSpec((1, per, cols, head_dim), lambda s, g: (s, g, 0, 0)),
        out_shape=jax.ShapeDtypeStruct((sessions, heads, cols, head_dim), jnp.float32),
        compiler_params=pltpu.CompilerParams(vmem_limit_bytes=VMEM),
        name="final_part",
    )(value)


def product_kernel(parts, base_ref, block_ref, *refs):
    lefts, weights, out_ref, held = refs[:parts], refs[parts:-2], refs[-2], refs[-1]

    @pl.when((pl.program_id(0) == 0) & (pl.program_id(1) == 0))
    def _():
        for k in range(parts):
            held[k] = lefts[k][0]

    total = jnp.zeros(out_ref.shape, jnp.float32)
    for k in range(parts):
        total += jnp.dot(held[k], weights[k][...], preferred_element_type=jnp.float32)
    out_ref[...] = total.astype(out_ref.dtype)


def product(base, blocks, lefts, gathered, row_at):
    parts = len(lefts)
    tokens, rows = lefts[0][0].shape[1:]
    count = blocks.shape[0]
    cols = gathered.shape[1]
    tile = min(cols, TILE)
    tiles = cols // tile

    def left_spec(place):
        return pl.BlockSpec((1, tokens, rows), lambda i, j, base, _: (place(base[0]), 0, 0))

    def weight_spec(k):
        return pl.BlockSpec((rows, tile), lambda i, j, _, blocks: (row_at(k, blocks[i]), j))

    return pl.pallas_call(
        functools.partial(product_kernel, parts),
        grid_spec=pltpu.PrefetchScalarGridSpec(
            num_scalar_prefetch=2,
            grid=(count, tiles),
            in_specs=[left_spec(place) for _, place in lefts]
            + [weight_spec(k) for k in range(parts)],
            out_specs=pl.BlockSpec((tokens, tile), lambda i, j, *_: (0, i * tiles + j)),
            scratch_shapes=[pltpu.VMEM((parts, tokens, rows), jnp.bfloat16)],
        ),
        out_shape=jax.ShapeDtypeStruct((tokens, count * cols), jnp.bfloat16),
        compiler_params=pltpu.CompilerParams(vmem_limit_bytes=VMEM),
        cost_estimate=pl.CostEstimate(
            flops=2 * tokens * parts * rows * cols * count,
            bytes_accessed=2 * (tokens * parts * rows + parts * rows * cols * count),
            transcendentals=0,
        ),
        name="product",
    )(
        base.reshape(1).astype(jnp.int32),
        blocks.astype(jnp.int32),
        *[left for left, _ in lefts],
        *[gathered] * parts,
    )


def shards(
    head_input,
    gate_input,
    state_in_proj,
    state_out_proj,
    step_raw,
    head_step_bias,
    decay_log,
    skip_gain,
    norm_gain,
    out_weight,
    pool_states,
    slot_map,
    span_lengths,
):
    turns = lax.axis_size("ctx")
    turn = lax.axis_index("ctx")
    lanes = lax.axis_size("groups")
    lane = lax.axis_index("groups")
    cores = lax.axis_size("sess")
    core = lax.axis_index("sess")
    head_count = lax.axis_size("head")
    head_index = lax.axis_index("head")
    sessions, tokens, inner = head_input.shape
    heads = step_raw.shape[2]
    head_dim = inner // heads
    slots = pool_states.shape[0]
    state_cols = pool_states.shape[3]
    groups = heads // GROUP_HEADS
    width = inner // groups
    bf16 = jnp.bfloat16

    carriers = lanes * cores
    rows = inner // carriers
    mine = lax.dynamic_slice_in_dim(out_weight, (lane * cores + core) * rows, rows, 0)
    gathered = lax.all_gather(mine, ("groups", "ctx", "sess"), axis=0, tiled=True)

    def row_at(k, q):
        return (k // cores * turns + q) * cores + k % cores

    def slots_of(which):
        return lax.dynamic_slice_in_dim(slot_map, which * sessions, sessions)

    own_slots = slots_of(core)
    asked = jnp.concatenate([slots_of((core - by) % cores) for by in range(cores)])
    picked = pick_part(asked % slots, pool_states.transpose(0, 1, 3, 2), groups)
    start = picked[:, :sessions]
    for by in range(1, cores):
        found = picked[:, by * sessions : (by + 1) * sessions]
        found = lax.ppermute(found, "sess", [(i, (i - by) % cores) for i in range(cores)])
        here = (own_slots // slots == (core + by) % cores)[None, :, None, None]
        start = jnp.where(here, found, start)
    entering = []
    for g in range(groups):
        part = start[g : g + 1]
        if g:
            part, entering[-1] = lax.optimization_barrier((part, entering[-1]))
        entering.append([part] + [lax.ppermute(part, "ctx", [(k, 0)]) for k in range(1, turns)])

    first_session = core * sessions
    own_lengths = lax.dynamic_slice_in_dim(span_lengths, first_session, sessions)
    limits = jnp.clip(own_lengths * SPAN - turn * tokens, 0, tokens)
    first_group = head_index * groups

    def grouped(proj):
        return lax.dynamic_slice_in_dim(proj, first_group, groups, 2).swapaxes(1, 2)

    b = grouped(state_in_proj)
    c = grouped(state_out_proj)
    raw = step_raw.swapaxes(1, 2).reshape(sessions, groups, GROUP_HEADS, tokens)
    skip = jnp.repeat(skip_gain, head_dim).reshape(groups, 1, width)
    gain = norm_gain.reshape(groups, 1, width)
    bias = head_step_bias.reshape(groups, GROUP_HEADS)
    rate = decay_log.reshape(groups, GROUP_HEADS)
    end, keep, grow = end_part(limits, head_input, b, raw, bias, rate)

    waves = groups + turns - 2
    normed = jnp.zeros((waves + 1, sessions, tokens, width), bf16)
    leavings = []
    coming = None
    for index in range(waves + 1):
        at = jnp.stack([jnp.clip(index - turn, 0, groups - 1), turn]).astype(jnp.int32)
        given = entering[index] if index < groups else None
        state, leaving = leave_part(at, coming, given, 0, keep, end)
        leavings.append(leaving)
        if index < waves:
            pairs = [(i, i + 1) for i in range(turns - 1) if 0 <= index - i < groups]
            coming = lax.ppermute(leaving, "ctx", pairs)
        if index == 0:
            x, state = lax.optimization_barrier((head_input, state))
            y = inside_part(limits, x, b, c, raw, bias, rate, skip)
        normed = normed_part(index, at, state, c, grow, y, gate_input, gain, normed)
        if index < waves:
            coming, normed = lax.optimization_barrier((coming, normed))

    final = jnp.stack(leavings[turns - 1 :])
    for step in range((turns - 1).bit_length()):
        by = turns // 2 ** (step + 1)
        half = final.shape[2] // 2
        pairs = [(z, z - by) for z in range(turns) if (turns - 1 - z) % (2 * by) == 0]
        got = lax.ppermute(final[:, :, :half], "ctx", pairs)
        final = jnp.where((turns - 1 - turn) % (2 * by) == by, got, final[:, :, half:])
    final = final_part(final, heads, head_dim)

    def at_place(k):
        return lambda base: base + k

    def at_fixed(k):
        return lambda base: k

    if groups == carriers:
        held = normed.reshape(waves + 1, sessions * tokens, width)
        left = [(held, at_place(k)) for k in range(carriers)]
    else:
        held = lax.dynamic_slice_in_dim(normed, turn, groups, 0)
        held = held.reshape(groups, sessions * tokens, width)
        held = held.transpose(1, 0, 2).reshape(sessions * tokens, carriers, rows)
        held = held.transpose(1, 0, 2)
        left = [(held, at_fixed(k)) for k in range(carriers)]
    live = (jnp.arange(tokens, dtype=jnp.int32)[None, :] < limits[:, None]).astype(jnp.float32)
    if head_count == 2:
        share = turns // 2
        theirs = []
        for m in range(share):
            block = product(turn, ((1 - head_index) * share + m).reshape(1), left, gathered, row_at)
            theirs.append(lax.ppermute(block, "head", [(0, 1), (1, 0)]))
        ours = product(turn, head_index * share + jnp.arange(share), left, gathered, row_at)
        theirs, ours, final = lax.optimization_barrier((theirs, ours, final))
        summed = ours.astype(jnp.float32) + jnp.concatenate(theirs, axis=1).astype(jnp.float32)
        summed = summed.reshape(sessions, tokens, -1)
    else:
        partial = product(turn, jnp.arange(turns), left, gathered, row_at)
        partial = partial.reshape(sessions, tokens, -1)
        summed = lax.psum_scatter(partial, "head", scatter_dimension=2, tiled=True).astype(
            jnp.float32
        )
    mixed = (summed * live[:, :, None]).astype(bf16)
    return (mixed, final.transpose(0, 1, 3, 2))


def solution(mesh):
    placed = (
        P(("groups", "sess"), "ctx", "head"),
        P(("groups", "sess"), "ctx", "head"),
        P(("groups", "sess"), "ctx", None, None),
        P(("groups", "sess"), "ctx", None, None),
        P(("groups", "sess"), "ctx", "head"),
        P("head"),
        P("head"),
        P("head"),
        P("head"),
        P("head", "ctx"),
        P(("groups", "sess"), "head", None, "ctx"),
        P("groups"),
        P("groups"),
    )
    return jax.shard_map(
        shards,
        mesh=mesh,
        in_specs=placed,
        out_specs=(
            P(("groups", "sess"), "ctx", "head"),
            P(("groups", "sess"), "head", None, "ctx"),
        ),
        check_vma=False,
    )
```

time: 941 us -> 285 us (0.30)
  waiting for transfers between devices: 713 us -> 118 us
  matrix products: 81.1 us -> 0 us
  Pallas kernels: 0 us -> 63.4 us
  other arithmetic: 55 us -> 6.51 us
  starting transfers between devices: 27.1 us -> 40 us
    ppermute x3 -> x23, waiting for transfers between devices: 398 us -> 118 us  [the longest x6 60.8 us: shards(): coming = lax.ppermute(leaving, 'ctx', pairs)]
    all_gather x3 -> x1, waiting for transfers between devices: 218 us -> 0.01 us  [shards(): lax.all_gather(mine, ('groups', 'ctx', 'sess'), axis=0, tiled=True)]
    dot_general x6 -> x0, matrix products: 81.1 us -> none  [the longest x1 22.6 us: shards(): jnp.einsum('sclhn,shpn->sclhp', c_heads, carried, precision=highest)]
    psum x1 -> x0, waiting for transfers between devices: 69.4 us -> none  [from_root(): return lax.psum(block, axis)]
    pallas_call x0 -> x21, Pallas kernels: none -> 63.4 us  [the longest x3 19.1 us: product(): pl.pallas_call(functools.partial(product_kernel, parts), grid_spec=pltpu....]
    reduce_scatter x1 -> x0, waiting for transfers between devices: 26.4 us -> none  [shards(): lax.psum_scatter(partial_out.astype(jnp.bfloat16), 'head', scatter_dimens...]
    convert_element_type x10 -> x2, other arithmetic: 26.8 us -> 1.22 us  [the longest x1 1.15 us: shards(): mixed = (summed * live[:, :, None]).astype(bf16)]
    unnamed x30 -> x114, local copies, waits for them, and re-layouts: 12.7 us -> 34.1 us
  transfers between devices with their start and end apart: 8 -> 24, of which waited for: 8 -> 9; matrix products, arithmetic and copies ran while one was open for 18% -> 3% of each run, Pallas kernels for 0% -> 22%
where the time goes in v3:
time: 285 us; the launch traced here: 284 us
  waiting for transfers between devices  118 us (41%)
  Pallas kernels  63.4 us (22%)
  local copies, waits for them, and re-layouts  40.6 us (14%)
  starting transfers between devices  40 us (14%)
  between operations  14.9 us (5%)
  other arithmetic  6.51 us (2%)
    ppermute x6, waiting for transfers between devices, shards(): coming = lax.ppermute(leaving, 'ctx', pairs)  60.8 us
    ppermute x2, waiting for transfers between devices, shards(): got = lax.ppermute(final[:, :, :half], 'ctx', pairs)  46.1 us
    unnamed x114, local copies, waits for them, and re-layouts  34.1 us
    ppermute x12, starting transfers between devices, shards(): lax.ppermute(part, 'ctx', [(k, 0)])  23.6 us
    pallas_call x3, Pallas kernels, product(): pl.pallas_call(functools.partial(product_kernel, parts), grid_spec=pltpu....  19.1 us
    pallas_call x7, Pallas kernels, normed_part(): pl.pallas_call(normed_kernel, grid_spec=pltpu.PrefetchScalarGridSpec(num_...  11.7 us
    pallas_call x7, Pallas kernels, leave_part(): pl.pallas_call(functools.partial(leave_kernel, 0 if first is None else le...  11 us
    ppermute x6, starting transfers between devices, shards(): coming = lax.ppermute(leaving, 'ctx', pairs)  10.7 us
  transfers between devices with their start and end apart: 24, of which 9 were waited for; matrix products, arithmetic and copies ran while one was open for 3% of the time, Pallas kernels for 22%

profile of v3, /device:TPU:12, one launch (start us, length us, event | category | flops | bytes accessed | tf_op | source)
XLA Modules:
  0.0 283.8 jit_solution(9187888847479566002)
XLA Ops:
  7.2 3.1 %constant_dynamic-slice_fusion = bf16[1024,1024]{1,0:T(8,128)(2,1)} fusion(bf16[4096,1024]{1,0:T(8,128)(2,1)} %param.22, s32[]{:T(128)S(6)} %select_n.81), kind=kLoop, calls=%fused_computation.16 | loop fusion | bytes 4194308 | tf_op jit(solution)/shard_map/dynamic_slice | solution.py:391
  11.2 2.2 copy-done.23
  16.9 2.4 collective-permute-start.1
  20.6 8.2 %end_part.1 = (f32[4,2,128,1024]{3,2,1,0:T(8,128)S(1)}, f32[4,2,8,1024]{3,2,1,0:T(8,128)S(1)}, f32[2,4,128,16]{3,2,1,0:T(8,128)S(1)}) custom-call(s32[2]{0:T(128)S(1)} %get-tuple-element.115.limit_ref, bf16[2,128,4096]{2,1,0:T(8,128)(2,1)S(1)} %copy-done.44, bf16[2,4,128,128]{3,2,1,0:T(8,128)(2,1)S(1)} %bitcast.59, f32[2,4,16,128]{3,2,1,0:T(8,128)S(1)} %bitcast.61, ...), custom_call_target="tpu_custom_call" | custom-call | flops 2000000000 | bytes 8388608 | tf_op jit(solution)/shard_map/end_part/pallas_call | solution.py:119
  31.4 2.4 copy-done.12
  37.8 5.3 %collective-permute-start.5 = (bf16[1,2,32,1024]{3,2,1,0:T(8,128)(2,1)S(1)}, bf16[1,2,32,1024]{3,2,1,0:T(8,128)(2,1)S(1)}, u32[]{:S(2)}, u32[]{:S(2)}) collective-permute-start(bf16[1,2,32,1024]{3,2,1,0:T(8,128)(2,1)S(1)} %get-tuple-element.65.refs_2_), channel_id=1, source_target_pairs={{4,0},{5,1},{6,2},{7,3},{20,16},{21,17},{22,18},{23,19}} | collective-permute-start | bytes 393224 | tf_op jit(solution)/shard_map/ppermute | solution.py:414
  46.2 8.9 %inside_part.1.y_ref = f32[2,128,4096]{2,1,0:T(8,128)S(1)} custom-call(s32[2]{0:T(128)S(1)} %get-tuple-element.115.limit_ref, bf16[2,128,4096]{2,1,0:T(8,128)(2,1)S(1)} %copy-done.45, bf16[2,4,128,128]{3,2,1,0:T(8,128)(2,1)S(1)} %bitcast.60, bf16[2,4,128,128]{3,2,1,0:T(8,128)(2,1)S(1)} %bitcast.40, f32[2,4,16,128]{3,2,1,0:T(8,128)S(1)} %bitcast.62, ...), custom_call_target="tpu_custom_call" | custom-call | flops 4000000000 | bytes 8388608 | tf_op jit(solution)/shard_map/inside_part/pallas_call | solution.py:148
  55.6 2.6 copy-done.22
  60.1 3.8 %collective-permute-done.4.refs_1_ = bf16[2,128,1024]{2,1,0:T(8,128)(2,1)} collective-permute-done((bf16[2,128,1024]{2,1,0:T(8,128)(2,1)}, bf16[2,128,1024]{2,1,0:T(8,128)(2,1)}, u32[]{:S(2)}, u32[]{:S(2)}) %collective-permute-start.4) | collective-permute-done | bytes 524320 | tf_op jit(solution)/shard_map/ppermute | solution.py:444
  63.9 2.5 leave_part.8
  71.1 6.0 %collective-permute-start.9 = (bf16[1,2,32,1024]{3,2,1,0:T(8,128)(2,1)S(1)}, bf16[1,2,32,1024]{3,2,1,0:T(8,128)(2,1)}, u32[]{:S(2)}, u32[]{:S(2)}) collective-permute-start(bf16[1,2,32,1024]{3,2,1,0:T(8,128)(2,1)S(1)} %get-tuple-element.74.refs_2_), channel_id=1, source_target_pairs={{4,0},{5,1},{6,2},{7,3},{20,16},{21,17},{22,18},{23,19}} | collective-permute-start | bytes 393224 | tf_op jit(solution)/shard_map/ppermute | solution.py:414
  77.1 9.3 %collective-permute-done.9.refs_3_ = bf16[1,2,32,1024]{3,2,1,0:T(8,128)(2,1)} collective-permute-done((bf16[1,2,32,1024]{3,2,1,0:T(8,128)(2,1)S(1)}, bf16[1,2,32,1024]{3,2,1,0:T(8,128)(2,1)}, u32[]{:S(2)}, u32[]{:S(2)}) %collective-permute-start.9) | collective-permute-done | bytes 131104 | tf_op jit(solution)/shard_map/ppermute | solution.py:414
  86.5 2.0 copy-done.3
  88.5 2.2 copy-done.17
  94.7 2.1 leave_part.9
  96.8 2.1 collective-permute-start.12
  98.9 4.0 %collective-permute-start.13 = (bf16[1,2,32,1024]{3,2,1,0:T(8,128)(2,1)S(1)}, bf16[1,2,32,1024]{3,2,1,0:T(8,128)(2,1)S(1)}, u32[]{:S(2)}, u32[]{:S(2)}) collective-permute-start(bf16[1,2,32,1024]{3,2,1,0:T(8,128)(2,1)S(1)} %get-tuple-element.82.refs_2_), channel_id=1, source_target_pairs={{4,0},{5,1},{6,2},{7,3},{20,16},{21,17},{22,18},{23,19}} | collective-permute-start | bytes 393224 | tf_op jit(solution)/shard_map/ppermute | solution.py:414
  106.0 18.5 %collective-permute-done.12.refs_1_ = bf16[2,128,1024]{2,1,0:T(8,128)(2,1)S(1)} collective-permute-done((bf16[2,128,1024]{2,1,0:T(8,128)(2,1)S(1)}, bf16[2,128,1024]{2,1,0:T(8,128)(2,1)S(1)}, u32[]{:S(2)}, u32[]{:S(2)}) %collective-permute-start.12) | collective-permute-done | bytes 524320 | tf_op jit(solution)/shard_map/ppermute | solution.py:444
  128.9 23.5 %collective-permute-done.16.refs_1_ = bf16[2,128,1024]{2,1,0:T(8,128)(2,1)S(1)} collective-permute-done((bf16[2,128,1024]{2,1,0:T(8,128)(2,1)S(1)}, bf16[2,128,1024]{2,1,0:T(8,128)(2,1)S(1)}, u32[]{:S(2)}, u32[]{:S(2)}) %collective-permute-start.16) | collective-permute-done | bytes 524320 | tf_op jit(solution)/shard_map/ppermute | solution.py:444
  154.7 2.8 collective-permute-start.17
  157.6 2.0 copy-done.5
  159.7 2.4 copy-done.19
  165.4 14.3 %collective-permute-done.17.refs_1_ = bf16[2,128,1024]{2,1,0:T(8,128)(2,1)} collective-permute-done((bf16[2,128,1024]{2,1,0:T(8,128)(2,1)}, bf16[2,128,1024]{2,1,0:T(8,128)(2,1)}, u32[]{:S(2)}, u32[]{:S(2)}) %collective-permute-start.17) | collective-permute-done | bytes 524320 | tf_op jit(solution)/shard_map/ppermute | solution.py:444
  179.7 2.0 leave_part.12
  190.5 46.1 %collective-permute-done.21 = bf16[4,2,64,1024]{3,2,1,0:T(8,128)(2,1)} collective-permute-done((bf16[4,2,64,1024]{3,2,1,0:T(8,128)(2,1)}, bf16[4,2,64,1024]{3,2,1,0:T(8,128)(2,1)}, u32[]{:S(2)}, u32[]{:S(2)}) %collective-permute-start.21) | collective-permute-done | bytes 1048608 | tf_op jit(solution)/shard_map/ppermute | solution.py:457
  239.1 2.1 collective-permute-start.22
  241.3 2.2 copy-done.21
  247.0 2.0 copy-done.9
  249.0 4.9 %product.4 = bf16[256,1024]{1,0:T(8,128)(2,1)S(1)} custom-call(s32[1]{0:T(128)} %bitcast.base_ref, s32[1]{0:T(128)} %bitcast.17.block_ref, bf16[7,256,1024]{2,1,0:T(8,128)(2,1)S(1)} %bitcast.28, bf16[7,256,1024]{2,1,0:T(8,128)(2,1)S(1)} %bitcast.29, bf16[7,256,1024]{2,1,0:T(8,128)(2,1)S(1)} %bitcast.30, bf16[7,256,1024]{2,1,0:T(8,128)(2,1)S(1)} %bitcast.31, ...), custom_call_target="tpu_custom_call" | custom-call | flops 2147483648 | bytes 10485760 | tf_op jit(solution)/shard_map/product/pallas_call | solution.py:331
  255.5 5.0 %product.3 = bf16[256,1024]{1,0:T(8,128)(2,1)S(1)} custom-call(s32[1]{0:T(128)} %bitcast.base_ref, s32[1]{0:T(128)} %bitcast.1.block_ref, bf16[7,256,1024]{2,1,0:T(8,128)(2,1)S(1)} %bitcast.32, bf16[7,256,1024]{2,1,0:T(8,128)(2,1)S(1)} %bitcast.33, bf16[7,256,1024]{2,1,0:T(8,128)(2,1)S(1)} %bitcast.34, bf16[7,256,1024]{2,1,0:T(8,128)(2,1)S(1)} %bitcast.35, ...), custom_call_target="tpu_custom_call" | custom-call | flops 2147483648 | bytes 10485760 | tf_op jit(solution)/shard_map/product/pallas_call | solution.py:331
  261.2 3.3 %final_part.1 = f32[2,64,32,64]{3,2,1,0:T(8,128)} custom-call(bf16[4,2,32,1024]{3,2,1,0:T(8,128)(2,1)S(1)} %slice_select_fusion.1.value_ref), custom_call_target="tpu_custom_call" | custom-call | tf_op jit(solution)/shard_map/final_part/pallas_call | solution.py:292
  264.5 9.2 %product.5 = bf16[256,2048]{1,0:T(8,128)(2,1)S(1)} custom-call(s32[1]{0:T(128)} %bitcast.base_ref, s32[2]{0:T(128)S(1)} %iota_add_fusion.block_ref, bf16[7,256,1024]{2,1,0:T(8,128)(2,1)S(1)} %bitcast.36, bf16[7,256,1024]{2,1,0:T(8,128)(2,1)S(1)} %bitcast.37, bf16[7,256,1024]{2,1,0:T(8,128)(2,1)S(1)} %bitcast.38, bf16[7,256,1024]{2,1,0:T(8,128)(2,1)S(1)} %bitcast.39, ...), custom_call_target="tpu_custom_call" | custom-call | flops 4294967296 | bytes 18874368 | tf_op jit(solution)/shard_map/product/pallas_call | solution.py:331
  (180 shorter events, 59.4 us)
Async XLA Ops:
  7.2 239.8 %all-gather.2.cloned.1.call-start = ((), (), s32[]{:S(2)}) async-start(), calls=%async_computation | async-start | bytes 35651584 | tf_op jit(solution)/shard_map/all_gather | solution.py:392
  14.7 2.0 collective-permute-start
  16.3 28.2 %copy-start.42 = (s32[2]{0:T(128)}, s32[2]{0:T(128)S(1)}, u32[]{:S(2)}) copy-start(s32[2]{0:T(128)S(1)} %get-tuple-element.115.limit_ref) | copy-start | bytes 28
  16.9 14.5 %collective-permute-start.1 = (bf16[1,2,32,1024]{3,2,1,0:T(8,128)(2,1)S(1)}, bf16[1,2,32,1024]{3,2,1,0:T(8,128)(2,1)S(1)}, u32[]{:S(2)}, u32[]{:S(2)}) collective-permute-start(bf16[1,2,32,1024]{3,2,1,0:T(8,128)(2,1)S(1)} %get-tuple-element.52.refs_1_), channel_id=1, source_target_pairs={{4,0},{5,1},{6,2},{7,3},{20,16},{21,17},{22,18},{23,19}} | collective-permute-start | bytes 393224 | tf_op jit(solution)/shard_map/ppermute | solution.py:414
  19.2 12.1 %collective-permute-start.2 = (bf16[1,2,32,1024]{3,2,1,0:T(8,128)(2,1)S(1)}, bf16[1,2,32,1024]{3,2,1,0:T(8,128)(2,1)S(1)}, u32[]{:S(2)}, u32[]{:S(2)}) collective-permute-start(bf16[1,2,32,1024]{3,2,1,0:T(8,128)(2,1)S(1)} %get-tuple-element.52.refs_1_), channel_id=1, source_target_pairs={{8,0},{9,1},{10,2},{11,3},{24,16},{25,17},{26,18},{27,19}} | collective-permute-start | bytes 393224 | tf_op jit(solution)/shard_map/ppermute | solution.py:414
  19.9 11.5 %collective-permute-start.3 = (bf16[1,2,32,1024]{3,2,1,0:T(8,128)(2,1)S(1)}, bf16[1,2,32,1024]{3,2,1,0:T(8,128)(2,1)S(1)}, u32[]{:S(2)}, u32[]{:S(2)}) collective-permute-start(bf16[1,2,32,1024]{3,2,1,0:T(8,128)(2,1)S(1)} %get-tuple-element.52.refs_1_), channel_id=1, source_target_pairs={{12,0},{13,1},{14,2},{15,3},{28,16},{29,17},{30,18},{31,19}} | collective-permute-start | bytes 393224 | tf_op jit(solution)/shard_map/ppermute | solution.py:414
  36.0 27.8 %collective-permute-start.4 = (bf16[2,128,1024]{2,1,0:T(8,128)(2,1)}, bf16[2,128,1024]{2,1,0:T(8,128)(2,1)}, u32[]{:S(2)}, u32[]{:S(2)}) collective-permute-start(bf16[2,128,1024]{2,1,0:T(8,128)(2,1)} %get-tuple-element.58), channel_id=1, source_target_pairs={{0,4},{1,5},{2,6},{3,7},{16,20},{17,21},{18,22},{19,23}} | collective-permute-start | bytes 1572872 | tf_op jit(solution)/shard_map/ppermute | solution.py:444
  37.8 22.2 %collective-permute-start.5 = (bf16[1,2,32,1024]{3,2,1,0:T(8,128)(2,1)S(1)}, bf16[1,2,32,1024]{3,2,1,0:T(8,128)(2,1)S(1)}, u32[]{:S(2)}, u32[]{:S(2)}) collective-permute-start(bf16[1,2,32,1024]{3,2,1,0:T(8,128)(2,1)S(1)} %get-tuple-element.65.refs_2_), channel_id=1, source_target_pairs={{4,0},{5,1},{6,2},{7,3},{20,16},{21,17},{22,18},{23,19}} | collective-permute-start | bytes 393224 | tf_op jit(solution)/shard_map/ppermute | solution.py:414
  43.2 16.9 %collective-permute-start.6 = (bf16[1,2,32,1024]{3,2,1,0:T(8,128)(2,1)S(1)}, bf16[1,2,32,1024]{3,2,1,0:T(8,128)(2,1)S(1)}, u32[]{:S(2)}, u32[]{:S(2)}) collective-permute-start(bf16[1,2,32,1024]{3,2,1,0:T(8,128)(2,1)S(1)} %get-tuple-element.65.refs_2_), channel_id=1, source_target_pairs={{8,0},{9,1},{10,2},{11,3},{24,16},{25,17},{26,18},{27,19}} | collective-permute-start | bytes 393224 | tf_op jit(solution)/shard_map/ppermute | solution.py:414
  43.8 16.2 %collective-permute-start.7 = (bf16[1,2,32,1024]{3,2,1,0:T(8,128)(2,1)S(1)}, bf16[1,2,32,1024]{3,2,1,0:T(8,128)(2,1)S(1)}, u32[]{:S(2)}, u32[]{:S(2)}) collective-permute-start(bf16[1,2,32,1024]{3,2,1,0:T(8,128)(2,1)S(1)} %get-tuple-element.65.refs_2_), channel_id=1, source_target_pairs={{12,0},{13,1},{14,2},{15,3},{28,16},{29,17},{30,18},{31,19}} | collective-permute-start | bytes 393224 | tf_op jit(solution)/shard_map/ppermute | solution.py:414
  67.2 27.5 %collective-permute-start.8 = (bf16[2,128,1024]{2,1,0:T(8,128)(2,1)}, bf16[2,128,1024]{2,1,0:T(8,128)(2,1)}, u32[]{:S(2)}, u32[]{:S(2)}) collective-permute-start(bf16[2,128,1024]{2,1,0:T(8,128)(2,1)} %get-tuple-element.69), channel_id=1, source_target_pairs={{0,4},{4,8},{1,5},{5,9},{2,6},{6,10},{3,7},{7,11},{16,20},{20,24},... | collective-permute-start | bytes 1572872 | tf_op jit(solution)/shard_map/ppermute | solution.py:444
  69.1 8.0 %collective-permute-start.10 = (bf16[1,2,32,1024]{3,2,1,0:T(8,128)(2,1)S(1)}, bf16[1,2,32,1024]{3,2,1,0:T(8,128)(2,1)S(1)}, u32[]{:S(2)}, u32[]{:S(2)}) collective-permute-start(bf16[1,2,32,1024]{3,2,1,0:T(8,128)(2,1)S(1)} %get-tuple-element.74.refs_2_), channel_id=1, source_target_pairs={{8,0},{9,1},{10,2},{11,3},{24,16},{25,17},{26,18},{27,19}} | collective-permute-start | bytes 393224 | tf_op jit(solution)/shard_map/ppermute | solution.py:414
  69.8 7.4 %collective-permute-start.11 = (bf16[1,2,32,1024]{3,2,1,0:T(8,128)(2,1)S(1)}, bf16[1,2,32,1024]{3,2,1,0:T(8,128)(2,1)}, u32[]{:S(2)}, u32[]{:S(2)}) collective-permute-start(bf16[1,2,32,1024]{3,2,1,0:T(8,128)(2,1)S(1)} %get-tuple-element.74.refs_2_), channel_id=1, source_target_pairs={{12,0},{13,1},{14,2},{15,3},{28,16},{29,17},{30,18},{31,19}} | collective-permute-start | bytes 393224 | tf_op jit(solution)/shard_map/ppermute | solution.py:414
  71.1 15.4 %collective-permute-start.9 = (bf16[1,2,32,1024]{3,2,1,0:T(8,128)(2,1)S(1)}, bf16[1,2,32,1024]{3,2,1,0:T(8,128)(2,1)}, u32[]{:S(2)}, u32[]{:S(2)}) collective-permute-start(bf16[1,2,32,1024]{3,2,1,0:T(8,128)(2,1)S(1)} %get-tuple-element.74.refs_2_), channel_id=1, source_target_pairs={{4,0},{5,1},{6,2},{7,3},{20,16},{21,17},{22,18},{23,19}} | collective-permute-start | bytes 393224 | tf_op jit(solution)/shard_map/ppermute | solution.py:414
  77.1 75.4 %copy-start.38 = (s32[2]{0:T(128)}, s32[2]{0:T(128)S(1)}, u32[]{:S(2)}) copy-start(s32[2]{0:T(128)S(1)} %get-tuple-element.110.refs_0_.at_ref) | copy-start | bytes 28
  94.7 9.5 %copy-start.18 = (f32[2,128,4096]{2,1,0:T(8,128)S(1)}, f32[2,128,4096]{2,1,0:T(8,128)}, u32[]{:S(2)}) copy-start(f32[2,128,4096]{2,1,0:T(8,128)} %copy-done.16) | copy-start | bytes 12582916
  96.8 27.6 %collective-permute-start.12 = (bf16[2,128,1024]{2,1,0:T(8,128)(2,1)S(1)}, bf16[2,128,1024]{2,1,0:T(8,128)(2,1)S(1)}, u32[]{:S(2)}, u32[]{:S(2)}) collective-permute-start(bf16[2,128,1024]{2,1,0:T(8,128)(2,1)S(1)} %get-tuple-element.78), channel_id=1, source_target_pairs={{0,4},{4,8},{8,12},{1,5},{5,9},{9,13},{2,6},{6,10},{10,14},{3,7},{... | collective-permute-start | bytes 1572872 | tf_op jit(solution)/shard_map/ppermute | solution.py:444
  98.9 25.5 %collective-permute-start.13 = (bf16[1,2,32,1024]{3,2,1,0:T(8,128)(2,1)S(1)}, bf16[1,2,32,1024]{3,2,1,0:T(8,128)(2,1)S(1)}, u32[]{:S(2)}, u32[]{:S(2)}) collective-permute-start(bf16[1,2,32,1024]{3,2,1,0:T(8,128)(2,1)S(1)} %get-tuple-element.82.refs_2_), channel_id=1, source_target_pairs={{4,0},{5,1},{6,2},{7,3},{20,16},{21,17},{22,18},{23,19}} | collective-permute-start | bytes 393224 | tf_op jit(solution)/shard_map/ppermute | solution.py:414
  102.9 21.5 %collective-permute-start.14 = (bf16[1,2,32,1024]{3,2,1,0:T(8,128)(2,1)S(1)}, bf16[1,2,32,1024]{3,2,1,0:T(8,128)(2,1)S(1)}, u32[]{:S(2)}, u32[]{:S(2)}) collective-permute-start(bf16[1,2,32,1024]{3,2,1,0:T(8,128)(2,1)S(1)} %get-tuple-element.82.refs_2_), channel_id=1, source_target_pairs={{8,0},{9,1},{10,2},{11,3},{24,16},{25,17},{26,18},{27,19}} | collective-permute-start | bytes 393224 | tf_op jit(solution)/shard_map/ppermute | solution.py:414
  103.6 20.9 %collective-permute-start.15 = (bf16[1,2,32,1024]{3,2,1,0:T(8,128)(2,1)S(1)}, bf16[1,2,32,1024]{3,2,1,0:T(8,128)(2,1)S(1)}, u32[]{:S(2)}, u32[]{:S(2)}) collective-permute-start(bf16[1,2,32,1024]{3,2,1,0:T(8,128)(2,1)S(1)} %get-tuple-element.82.refs_2_), channel_id=1, source_target_pairs={{12,0},{13,1},{14,2},{15,3},{28,16},{29,17},{30,18},{31,19}} | collective-permute-start | bytes 393224 | tf_op jit(solution)/shard_map/ppermute | solution.py:414
  104.3 20.2 %copy-start.35 = (s32[2]{0:T(128)S(1)}, s32[2]{0:T(128)}, u32[]{:S(2)}) copy-start(s32[2]{0:T(128)} %get-tuple-element.114.refs_0_.at_ref) | copy-start | bytes 28
  125.3 27.2 %collective-permute-start.16 = (bf16[2,128,1024]{2,1,0:T(8,128)(2,1)S(1)}, bf16[2,128,1024]{2,1,0:T(8,128)(2,1)S(1)}, u32[]{:S(2)}, u32[]{:S(2)}) collective-permute-start(bf16[2,128,1024]{2,1,0:T(8,128)(2,1)S(1)} %get-tuple-element.83), channel_id=1, source_target_pairs={{0,4},{4,8},{8,12},{1,5},{5,9},{9,13},{2,6},{6,10},{10,14},{3,7},{... | collective-permute-start | bytes 1572872 | tf_op jit(solution)/shard_map/ppermute | solution.py:444
  128.9 25.0 %copy-start.4 = (bf16[7,2,128,1024]{3,2,1,0:T(8,128)(2,1)}, bf16[7,2,128,1024]{3,2,1,0:T(8,128)(2,1)S(1)}, u32[]{:S(2)}) copy-start(bf16[7,2,128,1024]{3,2,1,0:T(8,128)(2,1)S(1)} %normed_part.10._) | copy-start | bytes 11010052
  154.7 24.9 %collective-permute-start.17 = (bf16[2,128,1024]{2,1,0:T(8,128)(2,1)}, bf16[2,128,1024]{2,1,0:T(8,128)(2,1)}, u32[]{:S(2)}, u32[]{:S(2)}) collective-permute-start(bf16[2,128,1024]{2,1,0:T(8,128)(2,1)} %get-tuple-element.87), channel_id=1, source_target_pairs={{4,8},{8,12},{5,9},{9,13},{6,10},{10,14},{7,11},{11,15},{20,24},{2... | collective-permute-start | bytes 1572872 | tf_op jit(solution)/shard_map/ppermute | solution.py:444
  163.7 15.9 %copy-start.15 = (f32[4,2,128,1024]{3,2,1,0:T(8,128)S(1)}, f32[4,2,128,1024]{3,2,1,0:T(8,128)}, u32[]{:S(2)}) copy-start(f32[4,2,128,1024]{3,2,1,0:T(8,128)} %copy-done.11) | copy-start | bytes 12582916
  181.7 2.4 collective-permute-start.18
  189.1 47.5 %collective-permute-start.21 = (bf16[4,2,64,1024]{3,2,1,0:T(8,128)(2,1)}, bf16[4,2,64,1024]{3,2,1,0:T(8,128)(2,1)}, u32[]{:S(2)}, u32[]{:S(2)}) collective-permute-start(bf16[4,2,64,1024]{3,2,1,0:T(8,128)(2,1)} %slice.46), channel_id=1, source_target_pairs={{12,4},{13,5},{14,6},{15,7},{28,20},{29,21},{30,22},{31,23}} | collective-permute-start | bytes 3145736 | tf_op jit(solution)/shard_map/ppermute | solution.py:457
  190.5 50.8 %copy-start.7 = (bf16[7,2,128,1024]{3,2,1,0:T(8,128)(2,1)S(1)}, bf16[7,2,128,1024]{3,2,1,0:T(8,128)(2,1)}, u32[]{:S(2)}) copy-start(bf16[7,2,128,1024]{3,2,1,0:T(8,128)(2,1)} %copy-done.6) | copy-start | bytes 11010052
  190.5 50.8 %copy-start.28 = (bf16[2,128,1024]{2,1,0:T(8,128)(2,1)S(1)}, bf16[2,128,1024]{2,1,0:T(8,128)(2,1)}, u32[]{:S(2)}) copy-start(bf16[2,128,1024]{2,1,0:T(8,128)(2,1)} %copy-done.27) | copy-start | bytes 1572868
  239.1 22.0 %collective-permute-start.22 = (bf16[4,2,32,1024]{3,2,1,0:T(8,128)(2,1)}, bf16[4,2,32,1024]{3,2,1,0:T(8,128)(2,1)}, u32[]{:S(2)}, u32[]{:S(2)}) collective-permute-start(bf16[4,2,32,1024]{3,2,1,0:T(8,128)(2,1)} %slice.48), channel_id=1, source_target_pairs={{4,0},{12,8},{5,1},{13,9},{6,2},{14,10},{7,3},{15,11},{20,16},{28,... | collective-permute-start | bytes 1572872 | tf_op jit(solution)/shard_map/ppermute | solution.py:457
  253.9 19.7 %collective-permute-start.20 = (bf16[256,1024]{1,0:T(8,128)(2,1)S(1)}, bf16[256,1024]{1,0:T(8,128)(2,1)S(1)}, u32[]{:S(2)}, u32[]{:S(2)}) collective-permute-start(bf16[256,1024]{1,0:T(8,128)(2,1)S(1)} %product.4), channel_id=1, source_target_pairs={{0,2},{2,0},{1,3},{3,1},{4,6},{6,4},{5,7},{7,5},{8,10},{10,8},{9,1... | collective-permute-start | bytes 1572872 | tf_op jit(solution)/shard_map/ppermute | solution.py:482
  260.5 15.0 %collective-permute-start.19 = (bf16[256,1024]{1,0:T(8,128)(2,1)S(1)}, bf16[256,1024]{1,0:T(8,128)(2,1)S(1)}, u32[]{:S(2)}, u32[]{:S(2)}) collective-permute-start(bf16[256,1024]{1,0:T(8,128)(2,1)S(1)} %product.3), channel_id=1, source_target_pairs={{0,2},{2,0},{1,3},{3,1},{4,6},{6,4},{5,7},{7,5},{8,10},{10,8},{9,1... | collective-permute-start | bytes 1572872 | tf_op jit(solution)/shard_map/ppermute | solution.py:482
  (48 other events, 129.3 us)
Sparse Core Ops, SparseCore 0:
  10.5 213.2 all-gather.1

commit v4 on v3

--- a/solution.py
+++ b/solution.py
@@ -450,13 +450,19 @@
             coming, normed = lax.optimization_barrier((coming, normed))
 
     final = jnp.stack(leavings[turns - 1 :])
-    for step in range((turns - 1).bit_length()):
+
+    def moved(final, step):
         by = turns // 2 ** (step + 1)
         half = final.shape[2] // 2
         pairs = [(z, z - by) for z in range(turns) if (turns - 1 - z) % (2 * by) == 0]
-        got = lax.ppermute(final[:, :, :half], "ctx", pairs)
-        final = jnp.where((turns - 1 - turn) % (2 * by) == by, got, final[:, :, half:])
-    final = final_part(final, heads, head_dim)
+        return lax.ppermute(final[:, :, :half], "ctx", pairs)
+
+    def placed(final, got, step):
+        by = turns // 2 ** (step + 1)
+        half = final.shape[2] // 2
+        return jnp.where((turns - 1 - turn) % (2 * by) == by, got, final[:, :, half:])
+
+    steps = (turns - 1).bit_length()
 
     def at_place(k):
         return lambda base: base + k
@@ -477,14 +483,27 @@
     if head_count == 2:
         share = turns // 2
         theirs = []
+        got = moved(final, 0)
         for m in range(share):
             block = product(turn, ((1 - head_index) * share + m).reshape(1), left, gathered, row_at)
+            if m < steps:
+                got, block = lax.optimization_barrier((got, block))
+                final = placed(final, got, m)
+                if m + 1 < steps:
+                    got = moved(final, m + 1)
             theirs.append(lax.ppermute(block, "head", [(0, 1), (1, 0)]))
         ours = product(turn, head_index * share + jnp.arange(share), left, gathered, row_at)
+        for step in range(share, steps):
+            final = placed(final, moved(final, step), step)
+        final, ours = lax.optimization_barrier((final, ours))
+        final = final_part(final, heads, head_dim)
         theirs, ours, final = lax.optimization_barrier((theirs, ours, final))
         summed = ours.astype(jnp.float32) + jnp.concatenate(theirs, axis=1).astype(jnp.float32)
         summed = summed.reshape(sessions, tokens, -1)
     else:
+        for step in range(steps):
+            final = placed(final, moved(final, step), step)
+        final = final_part(final, heads, head_dim)
         partial = product(turn, jnp.arange(turns), left, gathered, row_at)
         partial = partial.reshape(sessions, tokens, -1)
         summed = lax.psum_scatter(partial, "head", scatter_dimension=2, tiled=True).astype(

time: 285 us -> 272 us (0.954); the launches traced: 284 us -> 268 us
  waiting for transfers between devices: 118 us -> 111 us
  local copies, waits for them, and re-layouts: 40.6 us -> 35.8 us
    ppermute x2, waiting for transfers between devices: 46.1 us -> 5.16 us  [moved(): return lax.ppermute(final[:, :, :half], 'ctx', pairs)]
    all_gather x1, waiting for transfers between devices: 0.01 us -> 28.5 us  [shards(): lax.all_gather(mine, ('groups', 'ctx', 'sess'), axis=0, tiled=True)]
    ppermute x6, waiting for transfers between devices: 60.8 us -> 66.3 us  [shards(): coming = lax.ppermute(leaving, 'ctx', pairs)]
    unnamed x114 -> x90, local copies, waits for them, and re-layouts: 34.1 us -> 30.1 us
  transfers between devices with their start and end apart: 24 -> 24, of which waited for: 9 -> 9; matrix products, arithmetic and copies ran while one was open for 3% -> 2% of each run, Pallas kernels for 22% -> 23%
where the time goes in v4:
time: 272 us; the launch traced here: 268 us
  waiting for transfers between devices  111 us (41%)
  Pallas kernels  61.5 us (23%)
  starting transfers between devices  39 us (14%)
  local copies, waits for them, and re-layouts  35.8 us (13%)
  between operations  15 us (6%)
  other arithmetic  6.12 us (2%)
    ppermute x6, waiting for transfers between devices, shards(): coming = lax.ppermute(leaving, 'ctx', pairs)  66.3 us
    unnamed x90, local copies, waits for them, and re-layouts  30.1 us
    all_gather x1, waiting for transfers between devices, shards(): lax.all_gather(mine, ('groups', 'ctx', 'sess'), axis=0, tiled=True)  28.5 us
    ppermute x12, starting transfers between devices, shards(): lax.ppermute(part, 'ctx', [(k, 0)])  22.1 us
    pallas_call x3, Pallas kernels, product(): pl.pallas_call(functools.partial(product_kernel, parts), grid_spec=pltpu....  19.2 us
    pallas_call x7, Pallas kernels, normed_part(): pl.pallas_call(normed_kernel, grid_spec=pltpu.PrefetchScalarGridSpec(num_...  11.7 us
    ppermute x6, starting transfers between devices, shards(): coming = lax.ppermute(leaving, 'ctx', pairs)  11 us
    ppermute x12, waiting for transfers between devices, shards(): lax.ppermute(part, 'ctx', [(k, 0)])  10.1 us
  transfers between devices with their start and end apart: 24, of which 9 were waited for; matrix products, arithmetic and copies ran while one was open for 2% of the time, Pallas kernels for 23%

profile of v4, /device:TPU:12, one launch (start us, length us, event | category | flops | bytes accessed | tf_op | source)
XLA Modules:
  0.0 267.9 jit_solution(7466400968380911625)
XLA Ops:
  7.2 3.1 %constant_dynamic-slice_fusion = bf16[1024,1024]{1,0:T(8,128)(2,1)} fusion(bf16[4096,1024]{1,0:T(8,128)(2,1)} %param.22, s32[]{:T(128)S(6)} %select_n.81), kind=kLoop, calls=%fused_computation.16 | loop fusion | bytes 4194308 | tf_op jit(solution)/shard_map/dynamic_slice | solution.py:391
  11.2 2.2 copy-done.17
  16.8 2.4 collective-permute-start.1
  20.6 8.2 %end_part.1 = (f32[4,2,128,1024]{3,2,1,0:T(8,128)S(1)}, f32[4,2,8,1024]{3,2,1,0:T(8,128)S(1)}, f32[2,4,128,16]{3,2,1,0:T(8,128)S(1)}) custom-call(s32[2]{0:T(128)S(1)} %get-tuple-element.121.limit_ref, bf16[2,128,4096]{2,1,0:T(8,128)(2,1)S(1)} %copy-done.33, bf16[2,4,128,128]{3,2,1,0:T(8,128)(2,1)S(1)} %bitcast.59, f32[2,4,16,128]{3,2,1,0:T(8,128)S(1)} %bitcast.61, ...), custom_call_target="tpu_custom_call" | custom-call | flops 2000000000 | bytes 8388608 | tf_op jit(solution)/shard_map/end_part/pallas_call | solution.py:119
  28.8 2.0 copy-done.8
  31.4 2.4 copy-done.9
  37.9 5.3 %collective-permute-start.5 = (bf16[1,2,32,1024]{3,2,1,0:T(8,128)(2,1)S(1)}, bf16[1,2,32,1024]{3,2,1,0:T(8,128)(2,1)S(1)}, u32[]{:S(2)}, u32[]{:S(2)}) collective-permute-start(bf16[1,2,32,1024]{3,2,1,0:T(8,128)(2,1)S(1)} %get-tuple-element.71.refs_2_), channel_id=1, source_target_pairs={{4,0},{5,1},{6,2},{7,3},{20,16},{21,17},{22,18},{23,19}} | collective-permute-start | bytes 393224 | tf_op jit(solution)/shard_map/ppermute | solution.py:414
  46.3 8.9 %inside_part.1.y_ref = f32[2,128,4096]{2,1,0:T(8,128)S(1)} custom-call(s32[2]{0:T(128)S(1)} %get-tuple-element.121.limit_ref, bf16[2,128,4096]{2,1,0:T(8,128)(2,1)S(1)} %copy-done.34, bf16[2,4,128,128]{3,2,1,0:T(8,128)(2,1)S(1)} %bitcast.60, bf16[2,4,128,128]{3,2,1,0:T(8,128)(2,1)S(1)} %bitcast.40, f32[2,4,16,128]{3,2,1,0:T(8,128)S(1)} %bitcast.62, ...), custom_call_target="tpu_custom_call" | custom-call | flops 4000000000 | bytes 8388608 | tf_op jit(solution)/shard_map/inside_part/pallas_call | solution.py:148
  55.7 2.6 copy-done.16
  60.1 3.8 %collective-permute-done.4.refs_1_ = bf16[2,128,1024]{2,1,0:T(8,128)(2,1)} collective-permute-done((bf16[2,128,1024]{2,1,0:T(8,128)(2,1)}, bf16[2,128,1024]{2,1,0:T(8,128)(2,1)}, u32[]{:S(2)}, u32[]{:S(2)}) %collective-permute-start.4) | collective-permute-done | bytes 524320 | tf_op jit(solution)/shard_map/ppermute | solution.py:444
  69.0 5.2 %collective-permute-start.9 = (bf16[1,2,32,1024]{3,2,1,0:T(8,128)(2,1)S(1)}, bf16[1,2,32,1024]{3,2,1,0:T(8,128)(2,1)S(1)}, u32[]{:S(2)}, u32[]{:S(2)}) collective-permute-start(bf16[1,2,32,1024]{3,2,1,0:T(8,128)(2,1)S(1)} %get-tuple-element.80.refs_2_), channel_id=1, source_target_pairs={{4,0},{5,1},{6,2},{7,3},{20,16},{21,17},{22,18},{23,19}} | collective-permute-start | bytes 393224 | tf_op jit(solution)/shard_map/ppermute | solution.py:414
  74.2 10.0 %collective-permute-done.9.refs_3_ = bf16[1,2,32,1024]{3,2,1,0:T(8,128)(2,1)S(1)} collective-permute-done((bf16[1,2,32,1024]{3,2,1,0:T(8,128)(2,1)S(1)}, bf16[1,2,32,1024]{3,2,1,0:T(8,128)(2,1)S(1)}, u32[]{:S(2)}, u32[]{:S(2)}) %collective-permute-start.9) | collective-permute-done | bytes 131104 | tf_op jit(solution)/shard_map/ppermute | solution.py:414
  85.9 7.0 %collective-permute-done.8.refs_1_ = bf16[2,128,1024]{2,1,0:T(8,128)(2,1)S(1)} collective-permute-done((bf16[2,128,1024]{2,1,0:T(8,128)(2,1)S(1)}, bf16[2,128,1024]{2,1,0:T(8,128)(2,1)S(1)}, u32[]{:S(2)}, u32[]{:S(2)}) %collective-permute-start.8) | collective-permute-done | bytes 524320 | tf_op jit(solution)/shard_map/ppermute | solution.py:444
  93.8 2.0 collective-permute-start.12
  95.8 3.9 %collective-permute-start.13 = (bf16[1,2,32,1024]{3,2,1,0:T(8,128)(2,1)S(1)}, bf16[1,2,32,1024]{3,2,1,0:T(8,128)(2,1)S(1)}, u32[]{:S(2)}, u32[]{:S(2)}) collective-permute-start(bf16[1,2,32,1024]{3,2,1,0:T(8,128)(2,1)S(1)} %get-tuple-element.88.refs_2_), channel_id=1, source_target_pairs={{4,0},{5,1},{6,2},{7,3},{20,16},{21,17},{22,18},{23,19}} | collective-permute-start | bytes 393224 | tf_op jit(solution)/shard_map/ppermute | solution.py:414
  102.7 18.0 %collective-permute-done.12.refs_1_ = bf16[2,128,1024]{2,1,0:T(8,128)(2,1)S(1)} collective-permute-done((bf16[2,128,1024]{2,1,0:T(8,128)(2,1)S(1)}, bf16[2,128,1024]{2,1,0:T(8,128)(2,1)S(1)}, u32[]{:S(2)}, u32[]{:S(2)}) %collective-permute-start.12) | collective-permute-done | bytes 524320 | tf_op jit(solution)/shard_map/ppermute | solution.py:444
  121.6 2.1 collective-permute-start.16
  125.5 22.9 %collective-permute-done.16.refs_1_ = bf16[2,128,1024]{2,1,0:T(8,128)(2,1)S(1)} collective-permute-done((bf16[2,128,1024]{2,1,0:T(8,128)(2,1)S(1)}, bf16[2,128,1024]{2,1,0:T(8,128)(2,1)S(1)}, u32[]{:S(2)}, u32[]{:S(2)}) %collective-permute-start.16) | collective-permute-done | bytes 524320 | tf_op jit(solution)/shard_map/ppermute | solution.py:444
  150.6 3.0 %collective-permute-start.17 = (bf16[2,128,1024]{2,1,0:T(8,128)(2,1)}, bf16[2,128,1024]{2,1,0:T(8,128)(2,1)}, u32[]{:S(2)}, u32[]{:S(2)}) collective-permute-start(bf16[2,128,1024]{2,1,0:T(8,128)(2,1)} %get-tuple-element.93), channel_id=1, source_target_pairs={{4,8},{8,12},{5,9},{9,13},{6,10},{10,14},{7,11},{11,15},{20,24},{2... | collective-permute-start | bytes 1572872 | tf_op jit(solution)/shard_map/ppermute | solution.py:444
  153.7 2.1 copy-done.3
  155.8 2.3 copy-done.13
  160.8 14.6 %collective-permute-done.17.refs_1_ = bf16[2,128,1024]{2,1,0:T(8,128)(2,1)} collective-permute-done((bf16[2,128,1024]{2,1,0:T(8,128)(2,1)}, bf16[2,128,1024]{2,1,0:T(8,128)(2,1)}, u32[]{:S(2)}, u32[]{:S(2)}) %collective-permute-start.17) | collective-permute-done | bytes 524320 | tf_op jit(solution)/shard_map/ppermute | solution.py:444
  175.3 2.0 leave_part.12
  186.1 2.0 copy-done.5
  188.2 2.4 copy-done.15
  195.2 28.5 %all-gather.2.cloned.1.call-done.refs_4_.refs_5_.refs_6_.refs_7_ = bf16[16384,1024]{1,0:T(8,128)(2,1)} async-done(((bf16[1024,1024]{1,0:T(8,128)(2,1)}), bf16[16384,1024]{1,0:T(8,128)(2,1)}) %all-gather.2.cloned.1.call-update) | async-done | bytes 33554448 | tf_op jit(solution)/shard_map/all_gather | solution.py:392
  223.8 2.0 copy-done.7
  225.8 5.1 %product.3 = bf16[256,1024]{1,0:T(8,128)(2,1)S(1)} custom-call(s32[1]{0:T(128)} %bitcast.1.base_ref, s32[1]{0:T(128)} %bitcast.19.block_ref, bf16[7,256,1024]{2,1,0:T(8,128)(2,1)S(1)} %bitcast.28, bf16[7,256,1024]{2,1,0:T(8,128)(2,1)S(1)} %bitcast.29, bf16[7,256,1024]{2,1,0:T(8,128)(2,1)S(1)} %bitcast.30, bf16[7,256,1024]{2,1,0:T(8,128)(2,1)S(1)} %bitcast.31, ...), custom_call_target="tpu_custom_call" | custom-call | flops 2147483648 | bytes 10485760 | tf_op jit(solution)/shard_map/product/pallas_call | solution.py:331
  235.4 4.9 %product.4 = bf16[256,1024]{1,0:T(8,128)(2,1)S(1)} custom-call(s32[1]{0:T(128)} %bitcast.1.base_ref, s32[1]{0:T(128)} %bitcast.21.block_ref, bf16[7,256,1024]{2,1,0:T(8,128)(2,1)S(1)} %bitcast.32, bf16[7,256,1024]{2,1,0:T(8,128)(2,1)S(1)} %bitcast.33, bf16[7,256,1024]{2,1,0:T(8,128)(2,1)S(1)} %bitcast.34, bf16[7,256,1024]{2,1,0:T(8,128)(2,1)S(1)} %bitcast.35, ...), custom_call_target="tpu_custom_call" | custom-call | flops 2147483648 | bytes 10485760 | tf_op jit(solution)/shard_map/product/pallas_call | solution.py:331
  240.3 5.2 %collective-permute-done.21 = bf16[4,2,32,1024]{3,2,1,0:T(8,128)(2,1)S(1)} collective-permute-done((bf16[4,2,32,1024]{3,2,1,0:T(8,128)(2,1)S(1)}, bf16[4,2,32,1024]{3,2,1,0:T(8,128)(2,1)S(1)}, u32[]{:S(2)}, u32[]{:S(2)}) %collective-permute-start.21) | collective-permute-done | bytes 524320 | tf_op jit(solution)/shard_map/ppermute | solution.py:458
  246.9 9.2 %product.5 = bf16[256,2048]{1,0:T(8,128)(2,1)S(1)} custom-call(s32[1]{0:T(128)} %bitcast.1.base_ref, s32[2]{0:T(128)S(1)} %iota_add_fusion.block_ref, bf16[7,256,1024]{2,1,0:T(8,128)(2,1)S(1)} %bitcast.36, bf16[7,256,1024]{2,1,0:T(8,128)(2,1)S(1)} %bitcast.37, bf16[7,256,1024]{2,1,0:T(8,128)(2,1)S(1)} %bitcast.38, bf16[7,256,1024]{2,1,0:T(8,128)(2,1)S(1)} %bitcast.39, ...), custom_call_target="tpu_custom_call" | custom-call | flops 4294967296 | bytes 18874368 | tf_op jit(solution)/shard_map/product/pallas_call | solution.py:331
  256.2 3.3 %final_part.1 = f32[2,64,32,64]{3,2,1,0:T(8,128)} custom-call(bf16[4,2,32,1024]{3,2,1,0:T(8,128)(2,1)S(1)} %slice_select_fusion.1.value_ref), custom_call_target="tpu_custom_call" | custom-call | tf_op jit(solution)/shard_map/final_part/pallas_call | solution.py:292
  (156 shorter events, 54.2 us)
Async XLA Ops:
  7.2 7.6 %copy-start = (bf16[2,128,8,128]{3,2,1,0:T(8,128)(2,1)S(1)}, bf16[2,128,8,128]{3,2,1,0:T(8,128)(2,1)}, u32[]{:S(2)}) copy-start(bf16[2,128,8,128]{3,2,1,0:T(8,128)(2,1)} %param.15) | copy-start | bytes 1572868
  7.2 216.6 %all-gather.2.cloned.1.call-start = ((), (), s32[]{:S(2)}) async-start(), calls=%async_computation | async-start | bytes 35651584 | tf_op jit(solution)/shard_map/all_gather | solution.py:392
  14.7 5.9 %copy-start.35 = (f32[2,128,64]{1,2,0:T(8,128)S(1)}, f32[2,128,64]{1,2,0:T(8,128)}, u32[]{:S(2)}) copy-start(f32[2,128,64]{1,2,0:T(8,128)} %param.17) | copy-start | bytes 196612
  14.7 2.0 collective-permute-start
  16.2 28.4 %copy-start.31 = (s32[2]{0:T(128)}, s32[2]{0:T(128)S(1)}, u32[]{:S(2)}) copy-start(s32[2]{0:T(128)S(1)} %get-tuple-element.121.limit_ref) | copy-start | bytes 28
  16.8 14.6 %collective-permute-start.1 = (bf16[1,2,32,1024]{3,2,1,0:T(8,128)(2,1)S(1)}, bf16[1,2,32,1024]{3,2,1,0:T(8,128)(2,1)S(1)}, u32[]{:S(2)}, u32[]{:S(2)}) collective-permute-start(bf16[1,2,32,1024]{3,2,1,0:T(8,128)(2,1)S(1)} %get-tuple-element.58.refs_1_), channel_id=1, source_target_pairs={{4,0},{5,1},{6,2},{7,3},{20,16},{21,17},{22,18},{23,19}} | collective-permute-start | bytes 393224 | tf_op jit(solution)/shard_map/ppermute | solution.py:414
  19.2 12.2 %collective-permute-start.2 = (bf16[1,2,32,1024]{3,2,1,0:T(8,128)(2,1)S(1)}, bf16[1,2,32,1024]{3,2,1,0:T(8,128)(2,1)S(1)}, u32[]{:S(2)}, u32[]{:S(2)}) collective-permute-start(bf16[1,2,32,1024]{3,2,1,0:T(8,128)(2,1)S(1)} %get-tuple-element.58.refs_1_), channel_id=1, source_target_pairs={{8,0},{9,1},{10,2},{11,3},{24,16},{25,17},{26,18},{27,19}} | collective-permute-start | bytes 393224 | tf_op jit(solution)/shard_map/ppermute | solution.py:414
  19.9 11.5 %collective-permute-start.3 = (bf16[1,2,32,1024]{3,2,1,0:T(8,128)(2,1)S(1)}, bf16[1,2,32,1024]{3,2,1,0:T(8,128)(2,1)S(1)}, u32[]{:S(2)}, u32[]{:S(2)}) collective-permute-start(bf16[1,2,32,1024]{3,2,1,0:T(8,128)(2,1)S(1)} %get-tuple-element.58.refs_1_), channel_id=1, source_target_pairs={{12,0},{13,1},{14,2},{15,3},{28,16},{29,17},{30,18},{31,19}} | collective-permute-start | bytes 393224 | tf_op jit(solution)/shard_map/ppermute | solution.py:414
  36.1 27.8 %collective-permute-start.4 = (bf16[2,128,1024]{2,1,0:T(8,128)(2,1)}, bf16[2,128,1024]{2,1,0:T(8,128)(2,1)}, u32[]{:S(2)}, u32[]{:S(2)}) collective-permute-start(bf16[2,128,1024]{2,1,0:T(8,128)(2,1)} %get-tuple-element.64), channel_id=1, source_target_pairs={{0,4},{1,5},{2,6},{3,7},{16,20},{17,21},{18,22},{19,23}} | collective-permute-start | bytes 1572872 | tf_op jit(solution)/shard_map/ppermute | solution.py:444
  37.9 22.2 %collective-permute-start.5 = (bf16[1,2,32,1024]{3,2,1,0:T(8,128)(2,1)S(1)}, bf16[1,2,32,1024]{3,2,1,0:T(8,128)(2,1)S(1)}, u32[]{:S(2)}, u32[]{:S(2)}) collective-permute-start(bf16[1,2,32,1024]{3,2,1,0:T(8,128)(2,1)S(1)} %get-tuple-element.71.refs_2_), channel_id=1, source_target_pairs={{4,0},{5,1},{6,2},{7,3},{20,16},{21,17},{22,18},{23,19}} | collective-permute-start | bytes 393224 | tf_op jit(solution)/shard_map/ppermute | solution.py:414
  43.3 16.8 %collective-permute-start.6 = (bf16[1,2,32,1024]{3,2,1,0:T(8,128)(2,1)S(1)}, bf16[1,2,32,1024]{3,2,1,0:T(8,128)(2,1)S(1)}, u32[]{:S(2)}, u32[]{:S(2)}) collective-permute-start(bf16[1,2,32,1024]{3,2,1,0:T(8,128)(2,1)S(1)} %get-tuple-element.71.refs_2_), channel_id=1, source_target_pairs={{8,0},{9,1},{10,2},{11,3},{24,16},{25,17},{26,18},{27,19}} | collective-permute-start | bytes 393224 | tf_op jit(solution)/shard_map/ppermute | solution.py:414
  44.0 16.2 %collective-permute-start.7 = (bf16[1,2,32,1024]{3,2,1,0:T(8,128)(2,1)S(1)}, bf16[1,2,32,1024]{3,2,1,0:T(8,128)(2,1)S(1)}, u32[]{:S(2)}, u32[]{:S(2)}) collective-permute-start(bf16[1,2,32,1024]{3,2,1,0:T(8,128)(2,1)S(1)} %get-tuple-element.71.refs_2_), channel_id=1, source_target_pairs={{12,0},{13,1},{14,2},{15,3},{28,16},{29,17},{30,18},{31,19}} | collective-permute-start | bytes 393224 | tf_op jit(solution)/shard_map/ppermute | solution.py:414
  55.2 68.5 %copy-start.12 = (f32[2,128,4096]{2,1,0:T(8,128)}, f32[2,128,4096]{2,1,0:T(8,128)S(1)}, u32[]{:S(2)}) copy-start(f32[2,128,4096]{2,1,0:T(8,128)S(1)} %inside_part.1.y_ref) | copy-start | bytes 12582916
  65.7 27.2 %collective-permute-start.8 = (bf16[2,128,1024]{2,1,0:T(8,128)(2,1)S(1)}, bf16[2,128,1024]{2,1,0:T(8,128)(2,1)S(1)}, u32[]{:S(2)}, u32[]{:S(2)}) collective-permute-start(bf16[2,128,1024]{2,1,0:T(8,128)(2,1)S(1)} %get-tuple-element.75), channel_id=1, source_target_pairs={{0,4},{4,8},{1,5},{5,9},{2,6},{6,10},{3,7},{7,11},{16,20},{20,24},... | collective-permute-start | bytes 1572872 | tf_op jit(solution)/shard_map/ppermute | solution.py:444
  67.6 6.6 %collective-permute-start.10 = (bf16[1,2,32,1024]{3,2,1,0:T(8,128)(2,1)S(1)}, bf16[1,2,32,1024]{3,2,1,0:T(8,128)(2,1)S(1)}, u32[]{:S(2)}, u32[]{:S(2)}) collective-permute-start(bf16[1,2,32,1024]{3,2,1,0:T(8,128)(2,1)S(1)} %get-tuple-element.80.refs_2_), channel_id=1, source_target_pairs={{8,0},{9,1},{10,2},{11,3},{24,16},{25,17},{26,18},{27,19}} | collective-permute-start | bytes 393224 | tf_op jit(solution)/shard_map/ppermute | solution.py:414
  68.3 5.9 %collective-permute-start.11 = (bf16[1,2,32,1024]{3,2,1,0:T(8,128)(2,1)S(1)}, bf16[1,2,32,1024]{3,2,1,0:T(8,128)(2,1)S(1)}, u32[]{:S(2)}, u32[]{:S(2)}) collective-permute-start(bf16[1,2,32,1024]{3,2,1,0:T(8,128)(2,1)S(1)} %get-tuple-element.80.refs_2_), channel_id=1, source_target_pairs={{12,0},{13,1},{14,2},{15,3},{28,16},{29,17},{30,18},{31,19}} | collective-permute-start | bytes 393224 | tf_op jit(solution)/shard_map/ppermute | solution.py:414
  69.0 15.3 %collective-permute-start.9 = (bf16[1,2,32,1024]{3,2,1,0:T(8,128)(2,1)S(1)}, bf16[1,2,32,1024]{3,2,1,0:T(8,128)(2,1)S(1)}, u32[]{:S(2)}, u32[]{:S(2)}) collective-permute-start(bf16[1,2,32,1024]{3,2,1,0:T(8,128)(2,1)S(1)} %get-tuple-element.80.refs_2_), channel_id=1, source_target_pairs={{4,0},{5,1},{6,2},{7,3},{20,16},{21,17},{22,18},{23,19}} | collective-permute-start | bytes 393224 | tf_op jit(solution)/shard_map/ppermute | solution.py:414
  93.8 27.0 %collective-permute-start.12 = (bf16[2,128,1024]{2,1,0:T(8,128)(2,1)S(1)}, bf16[2,128,1024]{2,1,0:T(8,128)(2,1)S(1)}, u32[]{:S(2)}, u32[]{:S(2)}) collective-permute-start(bf16[2,128,1024]{2,1,0:T(8,128)(2,1)S(1)} %get-tuple-element.84), channel_id=1, source_target_pairs={{0,4},{4,8},{8,12},{1,5},{5,9},{9,13},{2,6},{6,10},{10,14},{3,7},{... | collective-permute-start | bytes 1572872 | tf_op jit(solution)/shard_map/ppermute | solution.py:444
  95.8 25.0 %collective-permute-start.13 = (bf16[1,2,32,1024]{3,2,1,0:T(8,128)(2,1)S(1)}, bf16[1,2,32,1024]{3,2,1,0:T(8,128)(2,1)S(1)}, u32[]{:S(2)}, u32[]{:S(2)}) collective-permute-start(bf16[1,2,32,1024]{3,2,1,0:T(8,128)(2,1)S(1)} %get-tuple-element.88.refs_2_), channel_id=1, source_target_pairs={{4,0},{5,1},{6,2},{7,3},{20,16},{21,17},{22,18},{23,19}} | collective-permute-start | bytes 393224 | tf_op jit(solution)/shard_map/ppermute | solution.py:414
  99.7 21.1 %collective-permute-start.14 = (bf16[1,2,32,1024]{3,2,1,0:T(8,128)(2,1)S(1)}, bf16[1,2,32,1024]{3,2,1,0:T(8,128)(2,1)S(1)}, u32[]{:S(2)}, u32[]{:S(2)}) collective-permute-start(bf16[1,2,32,1024]{3,2,1,0:T(8,128)(2,1)S(1)} %get-tuple-element.88.refs_2_), channel_id=1, source_target_pairs={{8,0},{9,1},{10,2},{11,3},{24,16},{25,17},{26,18},{27,19}} | collective-permute-start | bytes 393224 | tf_op jit(solution)/shard_map/ppermute | solution.py:414
  100.3 20.4 %collective-permute-start.15 = (bf16[1,2,32,1024]{3,2,1,0:T(8,128)(2,1)S(1)}, bf16[1,2,32,1024]{3,2,1,0:T(8,128)(2,1)S(1)}, u32[]{:S(2)}, u32[]{:S(2)}) collective-permute-start(bf16[1,2,32,1024]{3,2,1,0:T(8,128)(2,1)S(1)} %get-tuple-element.88.refs_2_), channel_id=1, source_target_pairs={{12,0},{13,1},{14,2},{15,3},{28,16},{29,17},{30,18},{31,19}} | collective-permute-start | bytes 393224 | tf_op jit(solution)/shard_map/ppermute | solution.py:414
  101.0 19.8 %copy-start.27 = (s32[2]{0:T(128)S(1)}, s32[2]{0:T(128)}, u32[]{:S(2)}) copy-start(s32[2]{0:T(128)} %get-tuple-element.120.refs_0_.at_ref) | copy-start | bytes 28
  121.6 26.8 %collective-permute-start.16 = (bf16[2,128,1024]{2,1,0:T(8,128)(2,1)S(1)}, bf16[2,128,1024]{2,1,0:T(8,128)(2,1)S(1)}, u32[]{:S(2)}, u32[]{:S(2)}) collective-permute-start(bf16[2,128,1024]{2,1,0:T(8,128)(2,1)S(1)} %get-tuple-element.89), channel_id=1, source_target_pairs={{0,4},{4,8},{8,12},{1,5},{5,9},{9,13},{2,6},{6,10},{10,14},{3,7},{... | collective-permute-start | bytes 1572872 | tf_op jit(solution)/shard_map/ppermute | solution.py:444
  123.8 24.6 %copy-start.28 = (s32[2]{0:T(128)S(1)}, s32[2]{0:T(128)}, u32[]{:S(2)}) copy-start(s32[2]{0:T(128)} %get-tuple-element.125.refs_0_.at_ref) | copy-start | bytes 28
  125.5 24.4 %copy-start.2 = (bf16[7,2,128,1024]{3,2,1,0:T(8,128)(2,1)}, bf16[7,2,128,1024]{3,2,1,0:T(8,128)(2,1)S(1)}, u32[]{:S(2)}) copy-start(bf16[7,2,128,1024]{3,2,1,0:T(8,128)(2,1)S(1)} %normed_part.10._) | copy-start | bytes 11010052
  150.6 24.7 %collective-permute-start.17 = (bf16[2,128,1024]{2,1,0:T(8,128)(2,1)}, bf16[2,128,1024]{2,1,0:T(8,128)(2,1)}, u32[]{:S(2)}, u32[]{:S(2)}) collective-permute-start(bf16[2,128,1024]{2,1,0:T(8,128)(2,1)} %get-tuple-element.93), channel_id=1, source_target_pairs={{4,8},{8,12},{5,9},{9,13},{6,10},{10,14},{7,11},{11,15},{20,24},{2... | collective-permute-start | bytes 1572872 | tf_op jit(solution)/shard_map/ppermute | solution.py:444
  159.1 16.2 %copy-start.11 = (f32[4,2,128,1024]{3,2,1,0:T(8,128)S(1)}, f32[4,2,128,1024]{3,2,1,0:T(8,128)}, u32[]{:S(2)}) copy-start(f32[4,2,128,1024]{3,2,1,0:T(8,128)} %copy-done.8) | copy-start | bytes 12582916
  177.3 2.4 collective-permute-start.18
  184.8 46.1 %collective-permute-start.19 = (bf16[4,2,64,1024]{3,2,1,0:T(8,128)(2,1)}, bf16[4,2,64,1024]{3,2,1,0:T(8,128)(2,1)}, u32[]{:S(2)}, u32[]{:S(2)}) collective-permute-start(bf16[4,2,64,1024]{3,2,1,0:T(8,128)(2,1)} %slice.46), channel_id=1, source_target_pairs={{12,4},{13,5},{14,6},{15,7},{28,20},{29,21},{30,22},{31,23}} | collective-permute-start | bytes 3145736 | tf_op jit(solution)/shard_map/ppermute | solution.py:458
  232.3 13.2 %collective-permute-start.21 = (bf16[4,2,32,1024]{3,2,1,0:T(8,128)(2,1)S(1)}, bf16[4,2,32,1024]{3,2,1,0:T(8,128)(2,1)S(1)}, u32[]{:S(2)}, u32[]{:S(2)}) collective-permute-start(bf16[4,2,32,1024]{3,2,1,0:T(8,128)(2,1)S(1)} %slice.48), channel_id=1, source_target_pairs={{4,0},{12,8},{5,1},{13,9},{6,2},{14,10},{7,3},{15,11},{20,16},{28,... | collective-permute-start | bytes 1572872 | tf_op jit(solution)/shard_map/ppermute | solution.py:458
  233.9 25.6 %collective-permute-start.20 = (bf16[256,1024]{1,0:T(8,128)(2,1)S(1)}, bf16[256,1024]{1,0:T(8,128)(2,1)S(1)}, u32[]{:S(2)}, u32[]{:S(2)}) collective-permute-start(bf16[256,1024]{1,0:T(8,128)(2,1)S(1)} %product.3), channel_id=1, source_target_pairs={{0,2},{2,0},{1,3},{3,1},{4,6},{6,4},{5,7},{7,5},{8,10},{10,8},{9,1... | collective-permute-start | bytes 1572872 | tf_op jit(solution)/shard_map/ppermute | solution.py:494
  245.5 14.0 %collective-permute-start.22 = (bf16[256,1024]{1,0:T(8,128)(2,1)S(1)}, bf16[256,1024]{1,0:T(8,128)(2,1)S(1)}, u32[]{:S(2)}, u32[]{:S(2)}) collective-permute-start(bf16[256,1024]{1,0:T(8,128)(2,1)S(1)} %product.4), channel_id=1, source_target_pairs={{0,2},{2,0},{1,3},{3,1},{4,6},{6,4},{5,7},{7,5},{8,10},{10,8},{9,1... | collective-permute-start | bytes 1572872 | tf_op jit(solution)/shard_map/ppermute | solution.py:494
  (36 other events, 85.2 us)
Sparse Core Ops, SparseCore 0:
  10.5 213.2 all-gather.1

commit v5 on v4

--- a/solution.py
+++ b/solution.py
@@ -486,16 +486,15 @@
         got = moved(final, 0)
         for m in range(share):
             block = product(turn, ((1 - head_index) * share + m).reshape(1), left, gathered, row_at)
-            if m < steps:
-                got, block = lax.optimization_barrier((got, block))
-                final = placed(final, got, m)
-                if m + 1 < steps:
-                    got = moved(final, m + 1)
             theirs.append(lax.ppermute(block, "head", [(0, 1), (1, 0)]))
+            if m == 0:
+                got, _ = lax.optimization_barrier((got, block))
+                final = placed(final, got, 0)
         ours = product(turn, head_index * share + jnp.arange(share), left, gathered, row_at)
-        for step in range(share, steps):
-            final = placed(final, moved(final, step), step)
-        final, ours = lax.optimization_barrier((final, ours))
+        for step in range(1, steps):
+            got = moved(final, step)
+            got, ours = lax.optimization_barrier((got, ours))
+            final = placed(final, got, step)
         final = final_part(final, heads, head_dim)
         theirs, ours, final = lax.optimization_barrier((theirs, ours, final))
         summed = ours.astype(jnp.float32) + jnp.concatenate(theirs, axis=1).astype(jnp.float32)

time: 272 us -> 268 us (0.985); the launches traced: 268 us -> 267 us
  waiting for transfers between devices: 111 us -> 99.1 us
  local copies, waits for them, and re-layouts: 35.8 us -> 42.9 us
    unnamed x90 -> x110, local copies, waits for them, and re-layouts: 30.1 us -> 37.2 us
    ppermute x6, waiting for transfers between devices: 66.3 us -> 60.8 us  [shards(): coming = lax.ppermute(leaving, 'ctx', pairs)]
    all_gather x1, waiting for transfers between devices: 28.5 us -> 24.3 us  [shards(): lax.all_gather(mine, ('groups', 'ctx', 'sess'), axis=0, tiled=True)]
  transfers between devices with their start and end apart: 24 -> 24, of which waited for: 9 -> 9; matrix products, arithmetic and copies ran while one was open for 2% -> 3% of each run, Pallas kernels for 23% -> 24%
where the time goes in v5:
time: 268 us; the launch traced here: 267 us
  waiting for transfers between devices  99.1 us (37%)
  Pallas kernels  63.5 us (24%)
  local copies, waits for them, and re-layouts  42.9 us (16%)
  starting transfers between devices  40.4 us (15%)
  between operations  14.9 us (6%)
  other arithmetic  6.18 us (2%)
    ppermute x6, waiting for transfers between devices, shards(): coming = lax.ppermute(leaving, 'ctx', pairs)  60.8 us
    unnamed x110, local copies, waits for them, and re-layouts  37.2 us
    all_gather x1, waiting for transfers between devices, shards(): lax.all_gather(mine, ('groups', 'ctx', 'sess'), axis=0, tiled=True)  24.3 us
    ppermute x12, starting transfers between devices, shards(): lax.ppermute(part, 'ctx', [(k, 0)])  23.7 us
    pallas_call x3, Pallas kernels, product(): pl.pallas_call(functools.partial(product_kernel, parts), grid_spec=pltpu....  19.2 us
    pallas_call x7, Pallas kernels, normed_part(): pl.pallas_call(normed_kernel, grid_spec=pltpu.PrefetchScalarGridSpec(num_...  11.6 us
    pallas_call x7, Pallas kernels, leave_part(): pl.pallas_call(functools.partial(leave_kernel, 0 if first is None else le...  11 us
    ppermute x6, starting transfers between devices, shards(): coming = lax.ppermute(leaving, 'ctx', pairs)  10.7 us
  transfers between devices with their start and end apart: 24, of which 9 were waited for; matrix products, arithmetic and copies ran while one was open for 3% of the time, Pallas kernels for 24%

profile of v5, /device:TPU:12, one launch (start us, length us, event | category | flops | bytes accessed | tf_op | source)
XLA Modules:
  0.0 267.0 jit_solution(3051074880012781773)
XLA Ops:
  7.2 3.1 %constant_dynamic-slice_fusion = bf16[1024,1024]{1,0:T(8,128)(2,1)} fusion(bf16[4096,1024]{1,0:T(8,128)(2,1)} %param.22, s32[]{:T(128)S(6)} %select_n.81), kind=kLoop, calls=%fused_computation.16 | loop fusion | bytes 4194308 | tf_op jit(solution)/shard_map/dynamic_slice | solution.py:391
  11.2 2.2 copy-done.22
  16.9 2.4 collective-permute-start.1
  20.6 8.2 %end_part.1 = (f32[4,2,128,1024]{3,2,1,0:T(8,128)S(1)}, f32[4,2,8,1024]{3,2,1,0:T(8,128)S(1)}, f32[2,4,128,16]{3,2,1,0:T(8,128)S(1)}) custom-call(s32[2]{0:T(128)S(1)} %get-tuple-element.121.limit_ref, bf16[2,128,4096]{2,1,0:T(8,128)(2,1)S(1)} %copy-done.43, bf16[2,4,128,128]{3,2,1,0:T(8,128)(2,1)S(1)} %bitcast.59, f32[2,4,16,128]{3,2,1,0:T(8,128)S(1)} %bitcast.61, ...), custom_call_target="tpu_custom_call" | custom-call | flops 2000000000 | bytes 8388608 | tf_op jit(solution)/shard_map/end_part/pallas_call | solution.py:119
  31.4 2.4 copy-done.11
  37.8 5.3 %collective-permute-start.5 = (bf16[1,2,32,1024]{3,2,1,0:T(8,128)(2,1)S(1)}, bf16[1,2,32,1024]{3,2,1,0:T(8,128)(2,1)S(1)}, u32[]{:S(2)}, u32[]{:S(2)}) collective-permute-start(bf16[1,2,32,1024]{3,2,1,0:T(8,128)(2,1)S(1)} %get-tuple-element.68.refs_2_), channel_id=1, source_target_pairs={{4,0},{5,1},{6,2},{7,3},{20,16},{21,17},{22,18},{23,19}} | collective-permute-start | bytes 393224 | tf_op jit(solution)/shard_map/ppermute | solution.py:414
  46.2 8.9 %inside_part.1.y_ref = f32[2,128,4096]{2,1,0:T(8,128)S(1)} custom-call(s32[2]{0:T(128)S(1)} %get-tuple-element.121.limit_ref, bf16[2,128,4096]{2,1,0:T(8,128)(2,1)S(1)} %copy-done.44, bf16[2,4,128,128]{3,2,1,0:T(8,128)(2,1)S(1)} %bitcast.60, bf16[2,4,128,128]{3,2,1,0:T(8,128)(2,1)S(1)} %bitcast.40, f32[2,4,16,128]{3,2,1,0:T(8,128)S(1)} %bitcast.62, ...), custom_call_target="tpu_custom_call" | custom-call | flops 4000000000 | bytes 8388608 | tf_op jit(solution)/shard_map/inside_part/pallas_call | solution.py:148
  55.7 2.6 copy-done.21
  60.1 3.8 %collective-permute-done.4.refs_1_ = bf16[2,128,1024]{2,1,0:T(8,128)(2,1)} collective-permute-done((bf16[2,128,1024]{2,1,0:T(8,128)(2,1)}, bf16[2,128,1024]{2,1,0:T(8,128)(2,1)}, u32[]{:S(2)}, u32[]{:S(2)}) %collective-permute-start.4) | collective-permute-done | bytes 524320 | tf_op jit(solution)/shard_map/ppermute | solution.py:444
  63.9 2.5 leave_part.8
  71.1 6.0 %collective-permute-start.9 = (bf16[1,2,32,1024]{3,2,1,0:T(8,128)(2,1)S(1)}, bf16[1,2,32,1024]{3,2,1,0:T(8,128)(2,1)}, u32[]{:S(2)}, u32[]{:S(2)}) collective-permute-start(bf16[1,2,32,1024]{3,2,1,0:T(8,128)(2,1)S(1)} %get-tuple-element.77.refs_2_), channel_id=1, source_target_pairs={{4,0},{5,1},{6,2},{7,3},{20,16},{21,17},{22,18},{23,19}} | collective-permute-start | bytes 393224 | tf_op jit(solution)/shard_map/ppermute | solution.py:414
  77.2 9.3 %collective-permute-done.9.refs_3_ = bf16[1,2,32,1024]{3,2,1,0:T(8,128)(2,1)} collective-permute-done((bf16[1,2,32,1024]{3,2,1,0:T(8,128)(2,1)S(1)}, bf16[1,2,32,1024]{3,2,1,0:T(8,128)(2,1)}, u32[]{:S(2)}, u32[]{:S(2)}) %collective-permute-start.9) | collective-permute-done | bytes 131104 | tf_op jit(solution)/shard_map/ppermute | solution.py:414
  86.5 2.0 copy-done.3
  88.6 2.2 copy-done.16
  94.8 2.1 leave_part.9
  96.9 2.1 collective-permute-start.12
  99.0 4.0 %collective-permute-start.13 = (bf16[1,2,32,1024]{3,2,1,0:T(8,128)(2,1)S(1)}, bf16[1,2,32,1024]{3,2,1,0:T(8,128)(2,1)S(1)}, u32[]{:S(2)}, u32[]{:S(2)}) collective-permute-start(bf16[1,2,32,1024]{3,2,1,0:T(8,128)(2,1)S(1)} %get-tuple-element.85.refs_2_), channel_id=1, source_target_pairs={{4,0},{5,1},{6,2},{7,3},{20,16},{21,17},{22,18},{23,19}} | collective-permute-start | bytes 393224 | tf_op jit(solution)/shard_map/ppermute | solution.py:414
  106.0 18.5 %collective-permute-done.12.refs_1_ = bf16[2,128,1024]{2,1,0:T(8,128)(2,1)S(1)} collective-permute-done((bf16[2,128,1024]{2,1,0:T(8,128)(2,1)S(1)}, bf16[2,128,1024]{2,1,0:T(8,128)(2,1)S(1)}, u32[]{:S(2)}, u32[]{:S(2)}) %collective-permute-start.12) | collective-permute-done | bytes 524320 | tf_op jit(solution)/shard_map/ppermute | solution.py:444
  129.0 23.6 %collective-permute-done.16.refs_1_ = bf16[2,128,1024]{2,1,0:T(8,128)(2,1)S(1)} collective-permute-done((bf16[2,128,1024]{2,1,0:T(8,128)(2,1)S(1)}, bf16[2,128,1024]{2,1,0:T(8,128)(2,1)S(1)}, u32[]{:S(2)}, u32[]{:S(2)}) %collective-permute-start.16) | collective-permute-done | bytes 524320 | tf_op jit(solution)/shard_map/ppermute | solution.py:444
  154.8 2.8 %collective-permute-start.17 = (bf16[2,128,1024]{2,1,0:T(8,128)(2,1)}, bf16[2,128,1024]{2,1,0:T(8,128)(2,1)}, u32[]{:S(2)}, u32[]{:S(2)}) collective-permute-start(bf16[2,128,1024]{2,1,0:T(8,128)(2,1)} %get-tuple-element.90), channel_id=1, source_target_pairs={{4,8},{8,12},{5,9},{9,13},{6,10},{10,14},{7,11},{11,15},{20,24},{2... | collective-permute-start | bytes 1572872 | tf_op jit(solution)/shard_map/ppermute | solution.py:444
  157.7 2.0 copy-done.5
  159.7 2.4 copy-done.18
  165.5 14.3 %collective-permute-done.17.refs_1_ = bf16[2,128,1024]{2,1,0:T(8,128)(2,1)} collective-permute-done((bf16[2,128,1024]{2,1,0:T(8,128)(2,1)}, bf16[2,128,1024]{2,1,0:T(8,128)(2,1)}, u32[]{:S(2)}, u32[]{:S(2)}) %collective-permute-start.17) | collective-permute-done | bytes 524320 | tf_op jit(solution)/shard_map/ppermute | solution.py:444
  190.6 2.1 copy-done.7
  192.7 2.2 copy-done.20
  199.4 24.3 %all-gather.2.cloned.1.call-done.refs_4_.refs_5_.refs_6_.refs_7_ = bf16[16384,1024]{1,0:T(8,128)(2,1)} async-done(((bf16[1024,1024]{1,0:T(8,128)(2,1)}), bf16[16384,1024]{1,0:T(8,128)(2,1)}) %all-gather.2.cloned.1.call-update) | async-done | bytes 33554448 | tf_op jit(solution)/shard_map/all_gather | solution.py:392
  223.8 2.0 copy-done.9
  225.8 5.1 %product.3 = bf16[256,1024]{1,0:T(8,128)(2,1)S(1)} custom-call(s32[1]{0:T(128)} %bitcast.base_ref, s32[1]{0:T(128)} %bitcast.1.block_ref, bf16[7,256,1024]{2,1,0:T(8,128)(2,1)S(1)} %bitcast.28, bf16[7,256,1024]{2,1,0:T(8,128)(2,1)S(1)} %bitcast.29, bf16[7,256,1024]{2,1,0:T(8,128)(2,1)S(1)} %bitcast.30, bf16[7,256,1024]{2,1,0:T(8,128)(2,1)S(1)} %bitcast.31, ...), custom_call_target="tpu_custom_call" | custom-call | flops 2147483648 | bytes 10485760 | tf_op jit(solution)/shard_map/product/pallas_call | solution.py:331
  232.4 4.2 %collective-permute-done.21 = bf16[4,2,64,1024]{3,2,1,0:T(8,128)(2,1)} collective-permute-done((bf16[4,2,64,1024]{3,2,1,0:T(8,128)(2,1)}, bf16[4,2,64,1024]{3,2,1,0:T(8,128)(2,1)}, u32[]{:S(2)}, u32[]{:S(2)}) %collective-permute-start.21) | collective-permute-done | bytes 1048608 | tf_op jit(solution)/shard_map/ppermute | solution.py:458
  239.5 5.0 %product.4 = bf16[256,1024]{1,0:T(8,128)(2,1)S(1)} custom-call(s32[1]{0:T(128)} %bitcast.base_ref, s32[1]{0:T(128)} %bitcast.17.block_ref, bf16[7,256,1024]{2,1,0:T(8,128)(2,1)S(1)} %bitcast.32, bf16[7,256,1024]{2,1,0:T(8,128)(2,1)S(1)} %bitcast.33, bf16[7,256,1024]{2,1,0:T(8,128)(2,1)S(1)} %bitcast.34, bf16[7,256,1024]{2,1,0:T(8,128)(2,1)S(1)} %bitcast.35, ...), custom_call_target="tpu_custom_call" | custom-call | flops 2147483648 | bytes 10485760 | tf_op jit(solution)/shard_map/product/pallas_call | solution.py:331
  246.1 9.2 %product.5 = bf16[256,2048]{1,0:T(8,128)(2,1)S(1)} custom-call(s32[1]{0:T(128)} %bitcast.base_ref, s32[2]{0:T(128)S(1)} %iota_add_fusion.block_ref, bf16[7,256,1024]{2,1,0:T(8,128)(2,1)S(1)} %bitcast.36, bf16[7,256,1024]{2,1,0:T(8,128)(2,1)S(1)} %bitcast.37, bf16[7,256,1024]{2,1,0:T(8,128)(2,1)S(1)} %bitcast.38, bf16[7,256,1024]{2,1,0:T(8,128)(2,1)S(1)} %bitcast.39, ...), custom_call_target="tpu_custom_call" | custom-call | flops 4294967296 | bytes 18874368 | tf_op jit(solution)/shard_map/product/pallas_call | solution.py:331
  255.3 3.3 %final_part.1 = f32[2,64,32,64]{3,2,1,0:T(8,128)} custom-call(bf16[4,2,32,1024]{3,2,1,0:T(8,128)(2,1)S(1)} %slice_select_fusion.1.value_ref), custom_call_target="tpu_custom_call" | custom-call | tf_op jit(solution)/shard_map/final_part/pallas_call | solution.py:292
  (176 shorter events, 62.0 us)
Async XLA Ops:
  7.2 7.6 %copy-start = (bf16[2,128,8,128]{3,2,1,0:T(8,128)(2,1)S(1)}, bf16[2,128,8,128]{3,2,1,0:T(8,128)(2,1)}, u32[]{:S(2)}) copy-start(bf16[2,128,8,128]{3,2,1,0:T(8,128)(2,1)} %param.15) | copy-start | bytes 1572868
  7.2 216.6 %all-gather.2.cloned.1.call-start = ((), (), s32[]{:S(2)}) async-start(), calls=%async_computation | async-start | bytes 35651584 | tf_op jit(solution)/shard_map/all_gather | solution.py:392
  14.7 2.0 collective-permute-start
  16.2 28.3 %copy-start.41 = (s32[2]{0:T(128)}, s32[2]{0:T(128)S(1)}, u32[]{:S(2)}) copy-start(s32[2]{0:T(128)S(1)} %get-tuple-element.121.limit_ref) | copy-start | bytes 28
  16.9 14.5 %collective-permute-start.1 = (bf16[1,2,32,1024]{3,2,1,0:T(8,128)(2,1)S(1)}, bf16[1,2,32,1024]{3,2,1,0:T(8,128)(2,1)S(1)}, u32[]{:S(2)}, u32[]{:S(2)}) collective-permute-start(bf16[1,2,32,1024]{3,2,1,0:T(8,128)(2,1)S(1)} %get-tuple-element.55.refs_1_), channel_id=1, source_target_pairs={{4,0},{5,1},{6,2},{7,3},{20,16},{21,17},{22,18},{23,19}} | collective-permute-start | bytes 393224 | tf_op jit(solution)/shard_map/ppermute | solution.py:414
  19.2 12.2 %collective-permute-start.2 = (bf16[1,2,32,1024]{3,2,1,0:T(8,128)(2,1)S(1)}, bf16[1,2,32,1024]{3,2,1,0:T(8,128)(2,1)S(1)}, u32[]{:S(2)}, u32[]{:S(2)}) collective-permute-start(bf16[1,2,32,1024]{3,2,1,0:T(8,128)(2,1)S(1)} %get-tuple-element.55.refs_1_), channel_id=1, source_target_pairs={{8,0},{9,1},{10,2},{11,3},{24,16},{25,17},{26,18},{27,19}} | collective-permute-start | bytes 393224 | tf_op jit(solution)/shard_map/ppermute | solution.py:414
  19.9 11.5 %collective-permute-start.3 = (bf16[1,2,32,1024]{3,2,1,0:T(8,128)(2,1)S(1)}, bf16[1,2,32,1024]{3,2,1,0:T(8,128)(2,1)S(1)}, u32[]{:S(2)}, u32[]{:S(2)}) collective-permute-start(bf16[1,2,32,1024]{3,2,1,0:T(8,128)(2,1)S(1)} %get-tuple-element.55.refs_1_), channel_id=1, source_target_pairs={{12,0},{13,1},{14,2},{15,3},{28,16},{29,17},{30,18},{31,19}} | collective-permute-start | bytes 393224 | tf_op jit(solution)/shard_map/ppermute | solution.py:414
  36.1 27.8 %collective-permute-start.4 = (bf16[2,128,1024]{2,1,0:T(8,128)(2,1)}, bf16[2,128,1024]{2,1,0:T(8,128)(2,1)}, u32[]{:S(2)}, u32[]{:S(2)}) collective-permute-start(bf16[2,128,1024]{2,1,0:T(8,128)(2,1)} %get-tuple-element.61), channel_id=1, source_target_pairs={{0,4},{1,5},{2,6},{3,7},{16,20},{17,21},{18,22},{19,23}} | collective-permute-start | bytes 1572872 | tf_op jit(solution)/shard_map/ppermute | solution.py:444
  37.8 22.2 %collective-permute-start.5 = (bf16[1,2,32,1024]{3,2,1,0:T(8,128)(2,1)S(1)}, bf16[1,2,32,1024]{3,2,1,0:T(8,128)(2,1)S(1)}, u32[]{:S(2)}, u32[]{:S(2)}) collective-permute-start(bf16[1,2,32,1024]{3,2,1,0:T(8,128)(2,1)S(1)} %get-tuple-element.68.refs_2_), channel_id=1, source_target_pairs={{4,0},{5,1},{6,2},{7,3},{20,16},{21,17},{22,18},{23,19}} | collective-permute-start | bytes 393224 | tf_op jit(solution)/shard_map/ppermute | solution.py:414
  43.2 16.9 %collective-permute-start.6 = (bf16[1,2,32,1024]{3,2,1,0:T(8,128)(2,1)S(1)}, bf16[1,2,32,1024]{3,2,1,0:T(8,128)(2,1)S(1)}, u32[]{:S(2)}, u32[]{:S(2)}) collective-permute-start(bf16[1,2,32,1024]{3,2,1,0:T(8,128)(2,1)S(1)} %get-tuple-element.68.refs_2_), channel_id=1, source_target_pairs={{8,0},{9,1},{10,2},{11,3},{24,16},{25,17},{26,18},{27,19}} | collective-permute-start | bytes 393224 | tf_op jit(solution)/shard_map/ppermute | solution.py:414
  43.9 16.2 %collective-permute-start.7 = (bf16[1,2,32,1024]{3,2,1,0:T(8,128)(2,1)S(1)}, bf16[1,2,32,1024]{3,2,1,0:T(8,128)(2,1)S(1)}, u32[]{:S(2)}, u32[]{:S(2)}) collective-permute-start(bf16[1,2,32,1024]{3,2,1,0:T(8,128)(2,1)S(1)} %get-tuple-element.68.refs_2_), channel_id=1, source_target_pairs={{12,0},{13,1},{14,2},{15,3},{28,16},{29,17},{30,18},{31,19}} | collective-permute-start | bytes 393224 | tf_op jit(solution)/shard_map/ppermute | solution.py:414
  67.2 27.6 %collective-permute-start.8 = (bf16[2,128,1024]{2,1,0:T(8,128)(2,1)}, bf16[2,128,1024]{2,1,0:T(8,128)(2,1)}, u32[]{:S(2)}, u32[]{:S(2)}) collective-permute-start(bf16[2,128,1024]{2,1,0:T(8,128)(2,1)} %get-tuple-element.72), channel_id=1, source_target_pairs={{0,4},{4,8},{1,5},{5,9},{2,6},{6,10},{3,7},{7,11},{16,20},{20,24},... | collective-permute-start | bytes 1572872 | tf_op jit(solution)/shard_map/ppermute | solution.py:444
  69.1 8.0 %collective-permute-start.10 = (bf16[1,2,32,1024]{3,2,1,0:T(8,128)(2,1)S(1)}, bf16[1,2,32,1024]{3,2,1,0:T(8,128)(2,1)S(1)}, u32[]{:S(2)}, u32[]{:S(2)}) collective-permute-start(bf16[1,2,32,1024]{3,2,1,0:T(8,128)(2,1)S(1)} %get-tuple-element.77.refs_2_), channel_id=1, source_target_pairs={{8,0},{9,1},{10,2},{11,3},{24,16},{25,17},{26,18},{27,19}} | collective-permute-start | bytes 393224 | tf_op jit(solution)/shard_map/ppermute | solution.py:414
  69.8 7.4 %collective-permute-start.11 = (bf16[1,2,32,1024]{3,2,1,0:T(8,128)(2,1)S(1)}, bf16[1,2,32,1024]{3,2,1,0:T(8,128)(2,1)}, u32[]{:S(2)}, u32[]{:S(2)}) collective-permute-start(bf16[1,2,32,1024]{3,2,1,0:T(8,128)(2,1)S(1)} %get-tuple-element.77.refs_2_), channel_id=1, source_target_pairs={{12,0},{13,1},{14,2},{15,3},{28,16},{29,17},{30,18},{31,19}} | collective-permute-start | bytes 393224 | tf_op jit(solution)/shard_map/ppermute | solution.py:414
  71.1 15.4 %collective-permute-start.9 = (bf16[1,2,32,1024]{3,2,1,0:T(8,128)(2,1)S(1)}, bf16[1,2,32,1024]{3,2,1,0:T(8,128)(2,1)}, u32[]{:S(2)}, u32[]{:S(2)}) collective-permute-start(bf16[1,2,32,1024]{3,2,1,0:T(8,128)(2,1)S(1)} %get-tuple-element.77.refs_2_), channel_id=1, source_target_pairs={{4,0},{5,1},{6,2},{7,3},{20,16},{21,17},{22,18},{23,19}} | collective-permute-start | bytes 393224 | tf_op jit(solution)/shard_map/ppermute | solution.py:414
  77.2 75.4 %copy-start.37 = (s32[2]{0:T(128)}, s32[2]{0:T(128)S(1)}, u32[]{:S(2)}) copy-start(s32[2]{0:T(128)S(1)} %get-tuple-element.116.refs_0_.at_ref) | copy-start | bytes 28
  94.8 9.6 %copy-start.17 = (f32[2,128,4096]{2,1,0:T(8,128)S(1)}, f32[2,128,4096]{2,1,0:T(8,128)}, u32[]{:S(2)}) copy-start(f32[2,128,4096]{2,1,0:T(8,128)} %copy-done.15) | copy-start | bytes 12582916
  96.9 27.6 %collective-permute-start.12 = (bf16[2,128,1024]{2,1,0:T(8,128)(2,1)S(1)}, bf16[2,128,1024]{2,1,0:T(8,128)(2,1)S(1)}, u32[]{:S(2)}, u32[]{:S(2)}) collective-permute-start(bf16[2,128,1024]{2,1,0:T(8,128)(2,1)S(1)} %get-tuple-element.81), channel_id=1, source_target_pairs={{0,4},{4,8},{8,12},{1,5},{5,9},{9,13},{2,6},{6,10},{10,14},{3,7},{... | collective-permute-start | bytes 1572872 | tf_op jit(solution)/shard_map/ppermute | solution.py:444
  99.0 25.6 %collective-permute-start.13 = (bf16[1,2,32,1024]{3,2,1,0:T(8,128)(2,1)S(1)}, bf16[1,2,32,1024]{3,2,1,0:T(8,128)(2,1)S(1)}, u32[]{:S(2)}, u32[]{:S(2)}) collective-permute-start(bf16[1,2,32,1024]{3,2,1,0:T(8,128)(2,1)S(1)} %get-tuple-element.85.refs_2_), channel_id=1, source_target_pairs={{4,0},{5,1},{6,2},{7,3},{20,16},{21,17},{22,18},{23,19}} | collective-permute-start | bytes 393224 | tf_op jit(solution)/shard_map/ppermute | solution.py:414
  103.0 21.5 %collective-permute-start.14 = (bf16[1,2,32,1024]{3,2,1,0:T(8,128)(2,1)S(1)}, bf16[1,2,32,1024]{3,2,1,0:T(8,128)(2,1)S(1)}, u32[]{:S(2)}, u32[]{:S(2)}) collective-permute-start(bf16[1,2,32,1024]{3,2,1,0:T(8,128)(2,1)S(1)} %get-tuple-element.85.refs_2_), channel_id=1, source_target_pairs={{8,0},{9,1},{10,2},{11,3},{24,16},{25,17},{26,18},{27,19}} | collective-permute-start | bytes 393224 | tf_op jit(solution)/shard_map/ppermute | solution.py:414
  103.6 20.9 %collective-permute-start.15 = (bf16[1,2,32,1024]{3,2,1,0:T(8,128)(2,1)S(1)}, bf16[1,2,32,1024]{3,2,1,0:T(8,128)(2,1)S(1)}, u32[]{:S(2)}, u32[]{:S(2)}) collective-permute-start(bf16[1,2,32,1024]{3,2,1,0:T(8,128)(2,1)S(1)} %get-tuple-element.85.refs_2_), channel_id=1, source_target_pairs={{12,0},{13,1},{14,2},{15,3},{28,16},{29,17},{30,18},{31,19}} | collective-permute-start | bytes 393224 | tf_op jit(solution)/shard_map/ppermute | solution.py:414
  104.3 20.2 %copy-start.34 = (s32[2]{0:T(128)S(1)}, s32[2]{0:T(128)}, u32[]{:S(2)}) copy-start(s32[2]{0:T(128)} %get-tuple-element.120.refs_0_.at_ref) | copy-start | bytes 28
  125.4 27.2 %collective-permute-start.16 = (bf16[2,128,1024]{2,1,0:T(8,128)(2,1)S(1)}, bf16[2,128,1024]{2,1,0:T(8,128)(2,1)S(1)}, u32[]{:S(2)}, u32[]{:S(2)}) collective-permute-start(bf16[2,128,1024]{2,1,0:T(8,128)(2,1)S(1)} %get-tuple-element.86), channel_id=1, source_target_pairs={{0,4},{4,8},{8,12},{1,5},{5,9},{9,13},{2,6},{6,10},{10,14},{3,7},{... | collective-permute-start | bytes 1572872 | tf_op jit(solution)/shard_map/ppermute | solution.py:444
  129.0 25.0 %copy-start.4 = (bf16[7,2,128,1024]{3,2,1,0:T(8,128)(2,1)}, bf16[7,2,128,1024]{3,2,1,0:T(8,128)(2,1)S(1)}, u32[]{:S(2)}) copy-start(bf16[7,2,128,1024]{3,2,1,0:T(8,128)(2,1)S(1)} %normed_part.10._) | copy-start | bytes 11010052
  154.8 25.0 %collective-permute-start.17 = (bf16[2,128,1024]{2,1,0:T(8,128)(2,1)}, bf16[2,128,1024]{2,1,0:T(8,128)(2,1)}, u32[]{:S(2)}, u32[]{:S(2)}) collective-permute-start(bf16[2,128,1024]{2,1,0:T(8,128)(2,1)} %get-tuple-element.90), channel_id=1, source_target_pairs={{4,8},{8,12},{5,9},{9,13},{6,10},{10,14},{7,11},{11,15},{20,24},{2... | collective-permute-start | bytes 1572872 | tf_op jit(solution)/shard_map/ppermute | solution.py:444
  163.8 15.9 %copy-start.14 = (f32[4,2,128,1024]{3,2,1,0:T(8,128)S(1)}, f32[4,2,128,1024]{3,2,1,0:T(8,128)}, u32[]{:S(2)}) copy-start(f32[4,2,128,1024]{3,2,1,0:T(8,128)} %copy-done.10) | copy-start | bytes 12582916
  181.8 2.4 collective-permute-start.18
  189.2 47.5 %collective-permute-start.21 = (bf16[4,2,64,1024]{3,2,1,0:T(8,128)(2,1)}, bf16[4,2,64,1024]{3,2,1,0:T(8,128)(2,1)}, u32[]{:S(2)}, u32[]{:S(2)}) collective-permute-start(bf16[4,2,64,1024]{3,2,1,0:T(8,128)(2,1)} %slice.46), channel_id=1, source_target_pairs={{12,4},{13,5},{14,6},{15,7},{28,20},{29,21},{30,22},{31,23}} | collective-permute-start | bytes 3145736 | tf_op jit(solution)/shard_map/ppermute | solution.py:458
  225.8 10.9 %copy-start.47 = (bf16[4,2,128,1024]{3,2,1,0:T(8,128)(2,1)S(1)}, bf16[4,2,128,1024]{3,2,1,0:T(8,128)(2,1)}, u32[]{:S(2)}) copy-start(bf16[4,2,128,1024]{3,2,1,0:T(8,128)(2,1)} %copy-done.46) | copy-start | bytes 6291460
  230.9 27.8 %collective-permute-start.19 = (bf16[256,1024]{1,0:T(8,128)(2,1)S(1)}, bf16[256,1024]{1,0:T(8,128)(2,1)S(1)}, u32[]{:S(2)}, u32[]{:S(2)}) collective-permute-start(bf16[256,1024]{1,0:T(8,128)(2,1)S(1)} %product.3), channel_id=1, source_target_pairs={{0,2},{2,0},{1,3},{3,1},{4,6},{6,4},{5,7},{7,5},{8,10},{10,8},{9,1... | collective-permute-start | bytes 1572872 | tf_op jit(solution)/shard_map/ppermute | solution.py:489
  238.0 17.2 %collective-permute-start.22 = (bf16[4,2,32,1024]{3,2,1,0:T(8,128)(2,1)S(1)}, bf16[4,2,32,1024]{3,2,1,0:T(8,128)(2,1)S(1)}, u32[]{:S(2)}, u32[]{:S(2)}) collective-permute-start(bf16[4,2,32,1024]{3,2,1,0:T(8,128)(2,1)S(1)} %slice.48), channel_id=1, source_target_pairs={{4,0},{12,8},{5,1},{13,9},{6,2},{14,10},{7,3},{15,11},{20,16},{28,... | collective-permute-start | bytes 1572872 | tf_op jit(solution)/shard_map/ppermute | solution.py:458
  244.5 14.1 %collective-permute-start.20 = (bf16[256,1024]{1,0:T(8,128)(2,1)S(1)}, bf16[256,1024]{1,0:T(8,128)(2,1)S(1)}, u32[]{:S(2)}, u32[]{:S(2)}) collective-permute-start(bf16[256,1024]{1,0:T(8,128)(2,1)S(1)} %product.4), channel_id=1, source_target_pairs={{0,2},{2,0},{1,3},{3,1},{4,6},{6,4},{5,7},{7,5},{8,10},{10,8},{9,1... | collective-permute-start | bytes 1572872 | tf_op jit(solution)/shard_map/ppermute | solution.py:489
  (46 other events, 112.1 us)
Sparse Core Ops, SparseCore 0:
  10.5 213.2 all-gather.1

commit v6 on v5

--- a/solution.py
+++ b/solution.py
@@ -300,43 +300,33 @@
     )(value)
 
 
-def product_kernel(parts, base_ref, block_ref, *refs):
-    lefts, weights, out_ref, held = refs[:parts], refs[parts:-2], refs[-2], refs[-1]
-
-    @pl.when((pl.program_id(0) == 0) & (pl.program_id(1) == 0))
-    def _():
-        for k in range(parts):
-            held[k] = lefts[k][0]
-
+def product_kernel(block_ref, left_ref, *refs):
+    weights, out_ref = refs[:-1], refs[-1]
     total = jnp.zeros(out_ref.shape, jnp.float32)
-    for k in range(parts):
-        total += jnp.dot(held[k], weights[k][...], preferred_element_type=jnp.float32)
+    for k, weight in enumerate(weights):
+        total += jnp.dot(left_ref[k], weight[...], preferred_element_type=jnp.float32)
     out_ref[...] = total.astype(out_ref.dtype)
 
 
-def product(base, blocks, lefts, gathered, row_at):
-    parts = len(lefts)
-    tokens, rows = lefts[0][0].shape[1:]
+def product(blocks, left, gathered, row_at, part=(0, 1)):
+    parts, tokens, rows = left.shape
     count = blocks.shape[0]
-    cols = gathered.shape[1]
+    cols = gathered.shape[1] // part[1]
     tile = min(cols, TILE)
     tiles = cols // tile
-
-    def left_spec(place):
-        return pl.BlockSpec((1, tokens, rows), lambda i, j, base, _: (place(base[0]), 0, 0))
+    ahead = part[0] * tiles
 
     def weight_spec(k):
-        return pl.BlockSpec((rows, tile), lambda i, j, _, blocks: (row_at(k, blocks[i]), j))
-
-    return pl.pallas_call(
-        functools.partial(product_kernel, parts),
+        return pl.BlockSpec((rows, tile), lambda i, j, blocks: (row_at(k, blocks[i]), ahead + j))
+
+    return pl.pallas_call(
+        product_kernel,
         grid_spec=pltpu.PrefetchScalarGridSpec(
-            num_scalar_prefetch=2,
+            num_scalar_prefetch=1,
             grid=(count, tiles),
-            in_specs=[left_spec(place) for _, place in lefts]
+            in_specs=[pl.BlockSpec((parts, tokens, rows), lambda i, j, _: (0, 0, 0))]
             + [weight_spec(k) for k in range(parts)],
-            out_specs=pl.BlockSpec((tokens, tile), lambda i, j, *_: (0, i * tiles + j)),
-            scratch_shapes=[pltpu.VMEM((parts, tokens, rows), jnp.bfloat16)],
+            out_specs=pl.BlockSpec((tokens, tile), lambda i, j, _: (0, i * tiles + j)),
         ),
         out_shape=jax.ShapeDtypeStruct((tokens, count * cols), jnp.bfloat16),
         compiler_params=pltpu.CompilerParams(vmem_limit_bytes=VMEM),
@@ -346,12 +336,7 @@
             transcendentals=0,
         ),
         name="product",
-    )(
-        base.reshape(1).astype(jnp.int32),
-        blocks.astype(jnp.int32),
-        *[left for left, _ in lefts],
-        *[gathered] * parts,
-    )
+    )(blocks.astype(jnp.int32), left, *[gathered] * parts)
 
 
 def shards(
@@ -464,33 +449,27 @@
 
     steps = (turns - 1).bit_length()
 
-    def at_place(k):
-        return lambda base: base + k
-
-    def at_fixed(k):
-        return lambda base: k
-
-    if groups == carriers:
-        held = normed.reshape(waves + 1, sessions * tokens, width)
-        left = [(held, at_place(k)) for k in range(carriers)]
-    else:
-        held = lax.dynamic_slice_in_dim(normed, turn, groups, 0)
-        held = held.reshape(groups, sessions * tokens, width)
-        held = held.transpose(1, 0, 2).reshape(sessions * tokens, carriers, rows)
-        held = held.transpose(1, 0, 2)
-        left = [(held, at_fixed(k)) for k in range(carriers)]
+    left = lax.dynamic_slice_in_dim(normed, turn, groups, 0)
+    left = left.reshape(groups, sessions * tokens, width)
+    if groups != carriers:
+        left = left.transpose(1, 0, 2).reshape(sessions * tokens, carriers, rows)
+        left = left.transpose(1, 0, 2)
+    left, gathered = lax.optimization_barrier((left, gathered))
     live = (jnp.arange(tokens, dtype=jnp.int32)[None, :] < limits[:, None]).astype(jnp.float32)
     if head_count == 2:
         share = turns // 2
         theirs = []
         got = moved(final, 0)
-        for m in range(share):
-            block = product(turn, ((1 - head_index) * share + m).reshape(1), left, gathered, row_at)
+        block = jnp.int32(0)
+        for m, part in [(0, (0, 2)), (0, (1, 2))] + [(m, (0, 1)) for m in range(1, share)]:
+            which = ((1 - head_index) * share + m).reshape(1)
+            which, block = lax.optimization_barrier((which, block))
+            block = product(which, left, gathered, row_at, part)
             theirs.append(lax.ppermute(block, "head", [(0, 1), (1, 0)]))
-            if m == 0:
-                got, _ = lax.optimization_barrier((got, block))
+            if part == (1, 2):
+                got, block = lax.optimization_barrier((got, block))
                 final = placed(final, got, 0)
-        ours = product(turn, head_index * share + jnp.arange(share), left, gathered, row_at)
+        ours = product(head_index * share + jnp.arange(share), left, gathered, row_at)
         for step in range(1, steps):
             got = moved(final, step)
             got, ours = lax.optimization_barrier((got, ours))
@@ -498,17 +477,17 @@
         final = final_part(final, heads, head_dim)
         theirs, ours, final = lax.optimization_barrier((theirs, ours, final))
         summed = ours.astype(jnp.float32) + jnp.concatenate(theirs, axis=1).astype(jnp.float32)
-        summed = summed.reshape(sessions, tokens, -1)
+        mixed = (summed * live.reshape(-1, 1)).astype(bf16).reshape(sessions, tokens, -1)
     else:
         for step in range(steps):
             final = placed(final, moved(final, step), step)
         final = final_part(final, heads, head_dim)
-        partial = product(turn, jnp.arange(turns), left, gathered, row_at)
+        partial = product(jnp.arange(turns), left, gathered, row_at)
         partial = partial.reshape(sessions, tokens, -1)
         summed = lax.psum_scatter(partial, "head", scatter_dimension=2, tiled=True).astype(
             jnp.float32
         )
-    mixed = (summed * live[:, :, None]).astype(bf16)
+        mixed = (summed * live[:, :, None]).astype(bf16)
     return (mixed, final.transpose(0, 1, 3, 2))
 
 

time: 268 us -> 265 us (0.989)
  local copies, waits for them, and re-layouts: 42.9 us -> 39 us
    unnamed x110 -> x108, local copies, waits for them, and re-layouts: 37.2 us -> 33.2 us
    ppermute x2, waiting for transfers between devices: 4.23 us -> 1.46 us  [moved(): return lax.ppermute(final[:, :, :half], 'ctx', pairs)]
    pallas_call x3 -> x4, Pallas kernels: 19.2 us -> 20.7 us  [product(): pl.pallas_call(product_kernel, grid_spec=pltpu.PrefetchScalarGridSpec(num...]
  transfers between devices with their start and end apart: 24 -> 25, of which waited for: 9 -> 9; matrix products, arithmetic and copies ran while one was open for 3% -> 3% of each run, Pallas kernels for 24% -> 25%
where the time goes in v6:
time: 265 us; the launch traced here: 264 us
  waiting for transfers between devices  97.6 us (37%)
  Pallas kernels  65 us (25%)
  starting transfers between devices  40.8 us (15%)
  local copies, waits for them, and re-layouts  39 us (15%)
  between operations  14.9 us (6%)
  other arithmetic  6.49 us (2%)
    ppermute x6, waiting for transfers between devices, shards(): coming = lax.ppermute(leaving, 'ctx', pairs)  60.8 us
    unnamed x108, local copies, waits for them, and re-layouts  33.2 us
    all_gather x1, waiting for transfers between devices, shards(): lax.all_gather(mine, ('groups', 'ctx', 'sess'), axis=0, tiled=True)  26.4 us
    ppermute x12, starting transfers between devices, shards(): lax.ppermute(part, 'ctx', [(k, 0)])  22.9 us
    pallas_call x4, Pallas kernels, product(): pl.pallas_call(product_kernel, grid_spec=pltpu.PrefetchScalarGridSpec(num...  20.7 us
    pallas_call x7, Pallas kernels, normed_part(): pl.pallas_call(normed_kernel, grid_spec=pltpu.PrefetchScalarGridSpec(num_...  11.7 us
    ppermute x6, starting transfers between devices, shards(): coming = lax.ppermute(leaving, 'ctx', pairs)  11.4 us
    pallas_call x7, Pallas kernels, leave_part(): pl.pallas_call(functools.partial(leave_kernel, 0 if first is None else le...  11.1 us
  transfers between devices with their start and end apart: 25, of which 9 were waited for; matrix products, arithmetic and copies ran while one was open for 3% of the time, Pallas kernels for 25%

profile of v6, /device:TPU:12, one launch (start us, length us, event | category | flops | bytes accessed | tf_op | source)
XLA Modules:
  0.0 263.9 jit_solution(1269471051718241584)
XLA Ops:
  7.2 3.1 %constant_dynamic-slice_fusion = bf16[1024,1024]{1,0:T(8,128)(2,1)} fusion(bf16[4096,1024]{1,0:T(8,128)(2,1)} %param.22, s32[]{:T(128)S(6)} %select_n.85), kind=kLoop, calls=%fused_computation.16 | loop fusion | bytes 4194308 | tf_op jit(solution)/shard_map/dynamic_slice | solution.py:376
  11.2 2.2 copy-done.20
  16.9 2.4 collective-permute-start.1
  20.6 8.2 %end_part.1 = (f32[4,2,128,1024]{3,2,1,0:T(8,128)S(1)}, f32[4,2,8,1024]{3,2,1,0:T(8,128)S(1)}, f32[2,4,128,16]{3,2,1,0:T(8,128)S(1)}) custom-call(s32[2]{0:T(128)S(1)} %get-tuple-element.129.limit_ref, bf16[2,128,4096]{2,1,0:T(8,128)(2,1)S(1)} %copy-done.41, bf16[2,4,128,128]{3,2,1,0:T(8,128)(2,1)S(1)} %bitcast.53, f32[2,4,16,128]{3,2,1,0:T(8,128)S(1)} %bitcast.55, ...), custom_call_target="tpu_custom_call" | custom-call | flops 2000000000 | bytes 8388608 | tf_op jit(solution)/shard_map/end_part/pallas_call | solution.py:119
  31.4 2.4 copy-done.9
  37.8 5.3 %collective-permute-start.5 = (bf16[1,2,32,1024]{3,2,1,0:T(8,128)(2,1)S(1)}, bf16[1,2,32,1024]{3,2,1,0:T(8,128)(2,1)S(1)}, u32[]{:S(2)}, u32[]{:S(2)}) collective-permute-start(bf16[1,2,32,1024]{3,2,1,0:T(8,128)(2,1)S(1)} %get-tuple-element.74.refs_2_), channel_id=1, source_target_pairs={{4,0},{5,1},{6,2},{7,3},{20,16},{21,17},{22,18},{23,19}} | collective-permute-start | bytes 393224 | tf_op jit(solution)/shard_map/ppermute | solution.py:399
  46.2 8.9 %inside_part.1.y_ref = f32[2,128,4096]{2,1,0:T(8,128)S(1)} custom-call(s32[2]{0:T(128)S(1)} %get-tuple-element.129.limit_ref, bf16[2,128,4096]{2,1,0:T(8,128)(2,1)S(1)} %copy-done.42, bf16[2,4,128,128]{3,2,1,0:T(8,128)(2,1)S(1)} %bitcast.54, bf16[2,4,128,128]{3,2,1,0:T(8,128)(2,1)S(1)} %bitcast.34, f32[2,4,16,128]{3,2,1,0:T(8,128)S(1)} %bitcast.56, ...), custom_call_target="tpu_custom_call" | custom-call | flops 4000000000 | bytes 8388608 | tf_op jit(solution)/shard_map/inside_part/pallas_call | solution.py:148
  55.7 2.6 copy-done.19
  60.1 3.8 %collective-permute-done.4.refs_1_ = bf16[2,128,1024]{2,1,0:T(8,128)(2,1)} collective-permute-done((bf16[2,128,1024]{2,1,0:T(8,128)(2,1)}, bf16[2,128,1024]{2,1,0:T(8,128)(2,1)}, u32[]{:S(2)}, u32[]{:S(2)}) %collective-permute-start.4) | collective-permute-done | bytes 524320 | tf_op jit(solution)/shard_map/ppermute | solution.py:429
  63.9 2.5 leave_part.8
  69.1 4.7 %collective-permute-start.9 = (bf16[1,2,32,1024]{3,2,1,0:T(8,128)(2,1)S(1)}, bf16[1,2,32,1024]{3,2,1,0:T(8,128)(2,1)S(1)}, u32[]{:S(2)}, u32[]{:S(2)}) collective-permute-start(bf16[1,2,32,1024]{3,2,1,0:T(8,128)(2,1)S(1)} %get-tuple-element.83.refs_2_), channel_id=1, source_target_pairs={{4,0},{5,1},{6,2},{7,3},{20,16},{21,17},{22,18},{23,19}} | collective-permute-start | bytes 393224 | tf_op jit(solution)/shard_map/ppermute | solution.py:399
  76.5 8.5 %collective-permute-done.9.refs_3_ = bf16[1,2,32,1024]{3,2,1,0:T(8,128)(2,1)S(1)} collective-permute-done((bf16[1,2,32,1024]{3,2,1,0:T(8,128)(2,1)S(1)}, bf16[1,2,32,1024]{3,2,1,0:T(8,128)(2,1)S(1)}, u32[]{:S(2)}, u32[]{:S(2)}) %collective-permute-start.9) | collective-permute-done | bytes 131104 | tf_op jit(solution)/shard_map/ppermute | solution.py:399
  87.1 2.2 copy-done.14
  92.7 2.1 collective-permute-done.8.refs_1_
  94.8 2.1 leave_part.9
  96.9 2.1 collective-permute-start.12
  99.0 3.8 %collective-permute-start.13 = (bf16[1,2,32,1024]{3,2,1,0:T(8,128)(2,1)S(1)}, bf16[1,2,32,1024]{3,2,1,0:T(8,128)(2,1)S(1)}, u32[]{:S(2)}, u32[]{:S(2)}) collective-permute-start(bf16[1,2,32,1024]{3,2,1,0:T(8,128)(2,1)S(1)} %get-tuple-element.91.refs_2_), channel_id=1, source_target_pairs={{4,0},{5,1},{6,2},{7,3},{20,16},{21,17},{22,18},{23,19}} | collective-permute-start | bytes 393224 | tf_op jit(solution)/shard_map/ppermute | solution.py:399
  105.8 18.0 %collective-permute-done.12.refs_1_ = bf16[2,128,1024]{2,1,0:T(8,128)(2,1)S(1)} collective-permute-done((bf16[2,128,1024]{2,1,0:T(8,128)(2,1)S(1)}, bf16[2,128,1024]{2,1,0:T(8,128)(2,1)S(1)}, u32[]{:S(2)}, u32[]{:S(2)}) %collective-permute-start.12) | collective-permute-done | bytes 524320 | tf_op jit(solution)/shard_map/ppermute | solution.py:429
  124.7 2.2 collective-permute-start.16
  128.6 22.8 %collective-permute-done.16.refs_1_ = bf16[2,128,1024]{2,1,0:T(8,128)(2,1)S(1)} collective-permute-done((bf16[2,128,1024]{2,1,0:T(8,128)(2,1)S(1)}, bf16[2,128,1024]{2,1,0:T(8,128)(2,1)S(1)}, u32[]{:S(2)}, u32[]{:S(2)}) %collective-permute-start.16) | collective-permute-done | bytes 524320 | tf_op jit(solution)/shard_map/ppermute | solution.py:429
  153.7 3.2 %collective-permute-start.17 = (bf16[2,128,1024]{2,1,0:T(8,128)(2,1)}, bf16[2,128,1024]{2,1,0:T(8,128)(2,1)}, u32[]{:S(2)}, u32[]{:S(2)}) collective-permute-start(bf16[2,128,1024]{2,1,0:T(8,128)(2,1)} %get-tuple-element.96), channel_id=1, source_target_pairs={{4,8},{8,12},{5,9},{9,13},{6,10},{10,14},{7,11},{11,15},{20,24},{2... | collective-permute-start | bytes 1572872 | tf_op jit(solution)/shard_map/ppermute | solution.py:429
  156.9 2.1 copy-done.5
  159.0 2.2 copy-done.16
  164.5 14.1 %collective-permute-done.17.refs_1_ = bf16[2,128,1024]{2,1,0:T(8,128)(2,1)} collective-permute-done((bf16[2,128,1024]{2,1,0:T(8,128)(2,1)}, bf16[2,128,1024]{2,1,0:T(8,128)(2,1)}, u32[]{:S(2)}, u32[]{:S(2)}) %collective-permute-start.17) | collective-permute-done | bytes 524320 | tf_op jit(solution)/shard_map/ppermute | solution.py:429
  190.2 2.1 copy-done.7
  192.3 2.2 copy-done.18
  197.4 26.4 %all-gather.2.cloned.1.call-done.refs_0_.refs_1_.refs_2_.refs_3_ = bf16[16384,1024]{1,0:T(8,128)(2,1)} async-done(((bf16[1024,1024]{1,0:T(8,128)(2,1)}), bf16[16384,1024]{1,0:T(8,128)(2,1)}) %all-gather.2.cloned.1.call-update) | async-done | bytes 33554448 | tf_op jit(solution)/shard_map/all_gather | solution.py:377
  223.8 3.4 %product.4 = bf16[256,512]{1,0:T(8,128)(2,1)S(1)} custom-call(s32[1]{0:T(128)} %bitcast.block_ref, bf16[4,256,1024]{2,1,0:T(8,128)(2,1)S(1)} %bitcast.30, bf16[16384,1024]{1,0:T(8,128)(2,1)} %all-gather.2.cloned.1.call-done.refs_0_.refs_1_.refs_2_.refs_3_, bf16[16384,1024]{1,0:T(8,128)(2,1)} %all-gather.2.cloned.1.call-done.refs_0_.refs_1_.refs_2_.refs_3_, ...), custom_call_target="tpu_custom_call" | custom-call | flops 1073741824 | bytes 6291456 | tf_op jit(solution)/shard_map/product/pallas_call | solution.py:322
  228.7 3.4 %product.5 = bf16[256,512]{1,0:T(8,128)(2,1)S(1)} custom-call(s32[1]{0:T(128)} %bitcast.block_ref, bf16[4,256,1024]{2,1,0:T(8,128)(2,1)S(1)} %bitcast.31, bf16[16384,1024]{1,0:T(8,128)(2,1)} %all-gather.2.cloned.1.call-done.refs_0_.refs_1_.refs_2_.refs_3_, bf16[16384,1024]{1,0:T(8,128)(2,1)} %all-gather.2.cloned.1.call-done.refs_0_.refs_1_.refs_2_.refs_3_, ...), custom_call_target="tpu_custom_call" | custom-call | flops 1073741824 | bytes 6291456 | tf_op jit(solution)/shard_map/product/pallas_call | solution.py:322
  237.0 4.8 %product.6 = bf16[256,1024]{1,0:T(8,128)(2,1)S(1)} custom-call(s32[1]{0:T(128)} %bitcast.17.block_ref, bf16[4,256,1024]{2,1,0:T(8,128)(2,1)S(1)} %bitcast.32, bf16[16384,1024]{1,0:T(8,128)(2,1)} %all-gather.2.cloned.1.call-done.refs_0_.refs_1_.refs_2_.refs_3_, bf16[16384,1024]{1,0:T(8,128)(2,1)} %all-gather.2.cloned.1.call-done.refs_0_.refs_1_.refs_2_.refs_3_, ...), custom_call_target="tpu_custom_call" | custom-call | flops 2147483648 | bytes 10485760 | tf_op jit(solution)/shard_map/product/pallas_call | solution.py:322
  243.3 9.0 %product.7 = bf16[256,2048]{1,0:T(8,128)(2,1)S(1)} custom-call(s32[2]{0:T(128)S(1)} %iota_add_fusion.block_ref, bf16[4,256,1024]{2,1,0:T(8,128)(2,1)S(1)} %bitcast.33, bf16[16384,1024]{1,0:T(8,128)(2,1)} %all-gather.2.cloned.1.call-done.refs_0_.refs_1_.refs_2_.refs_3_, bf16[16384,1024]{1,0:T(8,128)(2,1)} %all-gather.2.cloned.1.call-done.refs_0_.refs_1_.refs_2_.refs_3_, ...), custom_call_target="tpu_custom_call" | custom-call | flops 4294967296 | bytes 18874368 | tf_op jit(solution)/shard_map/product/pallas_call | solution.py:322
  252.4 3.3 %final_part.1 = f32[2,64,32,64]{3,2,1,0:T(8,128)} custom-call(bf16[4,2,32,1024]{3,2,1,0:T(8,128)(2,1)S(1)} %slice_select_fusion.1.value_ref), custom_call_target="tpu_custom_call" | custom-call | tf_op jit(solution)/shard_map/final_part/pallas_call | solution.py:292
  (177 shorter events, 62.9 us)
Async XLA Ops:
  7.2 7.6 %copy-start = (bf16[2,128,8,128]{3,2,1,0:T(8,128)(2,1)S(1)}, bf16[2,128,8,128]{3,2,1,0:T(8,128)(2,1)}, u32[]{:S(2)}) copy-start(bf16[2,128,8,128]{3,2,1,0:T(8,128)(2,1)} %param.15) | copy-start | bytes 1572868
  7.2 216.6 %all-gather.2.cloned.1.call-start = ((), (), s32[]{:S(2)}) async-start(), calls=%async_computation | async-start | bytes 35651584 | tf_op jit(solution)/shard_map/all_gather | solution.py:377
  14.7 2.0 collective-permute-start
  16.2 28.3 %copy-start.39 = (s32[2]{0:T(128)}, s32[2]{0:T(128)S(1)}, u32[]{:S(2)}) copy-start(s32[2]{0:T(128)S(1)} %get-tuple-element.129.limit_ref) | copy-start | bytes 28
  16.9 14.5 %collective-permute-start.1 = (bf16[1,2,32,1024]{3,2,1,0:T(8,128)(2,1)S(1)}, bf16[1,2,32,1024]{3,2,1,0:T(8,128)(2,1)S(1)}, u32[]{:S(2)}, u32[]{:S(2)}) collective-permute-start(bf16[1,2,32,1024]{3,2,1,0:T(8,128)(2,1)S(1)} %get-tuple-element.61.refs_1_), channel_id=1, source_target_pairs={{4,0},{5,1},{6,2},{7,3},{20,16},{21,17},{22,18},{23,19}} | collective-permute-start | bytes 393224 | tf_op jit(solution)/shard_map/ppermute | solution.py:399
  19.2 12.2 %collective-permute-start.2 = (bf16[1,2,32,1024]{3,2,1,0:T(8,128)(2,1)S(1)}, bf16[1,2,32,1024]{3,2,1,0:T(8,128)(2,1)S(1)}, u32[]{:S(2)}, u32[]{:S(2)}) collective-permute-start(bf16[1,2,32,1024]{3,2,1,0:T(8,128)(2,1)S(1)} %get-tuple-element.61.refs_1_), channel_id=1, source_target_pairs={{8,0},{9,1},{10,2},{11,3},{24,16},{25,17},{26,18},{27,19}} | collective-permute-start | bytes 393224 | tf_op jit(solution)/shard_map/ppermute | solution.py:399
  19.9 11.5 %collective-permute-start.3 = (bf16[1,2,32,1024]{3,2,1,0:T(8,128)(2,1)S(1)}, bf16[1,2,32,1024]{3,2,1,0:T(8,128)(2,1)S(1)}, u32[]{:S(2)}, u32[]{:S(2)}) collective-permute-start(bf16[1,2,32,1024]{3,2,1,0:T(8,128)(2,1)S(1)} %get-tuple-element.61.refs_1_), channel_id=1, source_target_pairs={{12,0},{13,1},{14,2},{15,3},{28,16},{29,17},{30,18},{31,19}} | collective-permute-start | bytes 393224 | tf_op jit(solution)/shard_map/ppermute | solution.py:399
  36.1 27.8 %collective-permute-start.4 = (bf16[2,128,1024]{2,1,0:T(8,128)(2,1)}, bf16[2,128,1024]{2,1,0:T(8,128)(2,1)}, u32[]{:S(2)}, u32[]{:S(2)}) collective-permute-start(bf16[2,128,1024]{2,1,0:T(8,128)(2,1)} %get-tuple-element.67), channel_id=1, source_target_pairs={{0,4},{1,5},{2,6},{3,7},{16,20},{17,21},{18,22},{19,23}} | collective-permute-start | bytes 1572872 | tf_op jit(solution)/shard_map/ppermute | solution.py:429
  37.8 22.2 %collective-permute-start.5 = (bf16[1,2,32,1024]{3,2,1,0:T(8,128)(2,1)S(1)}, bf16[1,2,32,1024]{3,2,1,0:T(8,128)(2,1)S(1)}, u32[]{:S(2)}, u32[]{:S(2)}) collective-permute-start(bf16[1,2,32,1024]{3,2,1,0:T(8,128)(2,1)S(1)} %get-tuple-element.74.refs_2_), channel_id=1, source_target_pairs={{4,0},{5,1},{6,2},{7,3},{20,16},{21,17},{22,18},{23,19}} | collective-permute-start | bytes 393224 | tf_op jit(solution)/shard_map/ppermute | solution.py:399
  43.2 16.9 %collective-permute-start.6 = (bf16[1,2,32,1024]{3,2,1,0:T(8,128)(2,1)S(1)}, bf16[1,2,32,1024]{3,2,1,0:T(8,128)(2,1)S(1)}, u32[]{:S(2)}, u32[]{:S(2)}) collective-permute-start(bf16[1,2,32,1024]{3,2,1,0:T(8,128)(2,1)S(1)} %get-tuple-element.74.refs_2_), channel_id=1, source_target_pairs={{8,0},{9,1},{10,2},{11,3},{24,16},{25,17},{26,18},{27,19}} | collective-permute-start | bytes 393224 | tf_op jit(solution)/shard_map/ppermute | solution.py:399
  43.9 16.2 %collective-permute-start.7 = (bf16[1,2,32,1024]{3,2,1,0:T(8,128)(2,1)S(1)}, bf16[1,2,32,1024]{3,2,1,0:T(8,128)(2,1)S(1)}, u32[]{:S(2)}, u32[]{:S(2)}) collective-permute-start(bf16[1,2,32,1024]{3,2,1,0:T(8,128)(2,1)S(1)} %get-tuple-element.74.refs_2_), channel_id=1, source_target_pairs={{12,0},{13,1},{14,2},{15,3},{28,16},{29,17},{30,18},{31,19}} | collective-permute-start | bytes 393224 | tf_op jit(solution)/shard_map/ppermute | solution.py:399
  67.2 27.6 %collective-permute-start.8 = (bf16[2,128,1024]{2,1,0:T(8,128)(2,1)}, bf16[2,128,1024]{2,1,0:T(8,128)(2,1)}, u32[]{:S(2)}, u32[]{:S(2)}) collective-permute-start(bf16[2,128,1024]{2,1,0:T(8,128)(2,1)} %get-tuple-element.78), channel_id=1, source_target_pairs={{0,4},{4,8},{1,5},{5,9},{2,6},{6,10},{3,7},{7,11},{16,20},{20,24},... | collective-permute-start | bytes 1572872 | tf_op jit(solution)/shard_map/ppermute | solution.py:429
  69.1 15.9 %collective-permute-start.9 = (bf16[1,2,32,1024]{3,2,1,0:T(8,128)(2,1)S(1)}, bf16[1,2,32,1024]{3,2,1,0:T(8,128)(2,1)S(1)}, u32[]{:S(2)}, u32[]{:S(2)}) collective-permute-start(bf16[1,2,32,1024]{3,2,1,0:T(8,128)(2,1)S(1)} %get-tuple-element.83.refs_2_), channel_id=1, source_target_pairs={{4,0},{5,1},{6,2},{7,3},{20,16},{21,17},{22,18},{23,19}} | collective-permute-start | bytes 393224 | tf_op jit(solution)/shard_map/ppermute | solution.py:399
  73.9 11.2 %collective-permute-start.10 = (bf16[1,2,32,1024]{3,2,1,0:T(8,128)(2,1)S(1)}, bf16[1,2,32,1024]{3,2,1,0:T(8,128)(2,1)}, u32[]{:S(2)}, u32[]{:S(2)}) collective-permute-start(bf16[1,2,32,1024]{3,2,1,0:T(8,128)(2,1)S(1)} %get-tuple-element.83.refs_2_), channel_id=1, source_target_pairs={{8,0},{9,1},{10,2},{11,3},{24,16},{25,17},{26,18},{27,19}} | collective-permute-start | bytes 393224 | tf_op jit(solution)/shard_map/ppermute | solution.py:399
  75.2 9.9 %collective-permute-start.11 = (bf16[1,2,32,1024]{3,2,1,0:T(8,128)(2,1)S(1)}, bf16[1,2,32,1024]{3,2,1,0:T(8,128)(2,1)}, u32[]{:S(2)}, u32[]{:S(2)}) collective-permute-start(bf16[1,2,32,1024]{3,2,1,0:T(8,128)(2,1)S(1)} %get-tuple-element.83.refs_2_), channel_id=1, source_target_pairs={{12,0},{13,1},{14,2},{15,3},{28,16},{29,17},{30,18},{31,19}} | collective-permute-start | bytes 393224 | tf_op jit(solution)/shard_map/ppermute | solution.py:399
  76.5 74.9 %copy-start.35 = (s32[2]{0:T(128)}, s32[2]{0:T(128)S(1)}, u32[]{:S(2)}) copy-start(s32[2]{0:T(128)S(1)} %get-tuple-element.126.refs_0_.at_ref) | copy-start | bytes 28
  94.8 9.4 %copy-start.15 = (f32[2,128,4096]{2,1,0:T(8,128)S(1)}, f32[2,128,4096]{2,1,0:T(8,128)}, u32[]{:S(2)}) copy-start(f32[2,128,4096]{2,1,0:T(8,128)} %copy-done.13) | copy-start | bytes 12582916
  96.9 27.0 %collective-permute-start.12 = (bf16[2,128,1024]{2,1,0:T(8,128)(2,1)S(1)}, bf16[2,128,1024]{2,1,0:T(8,128)(2,1)S(1)}, u32[]{:S(2)}, u32[]{:S(2)}) collective-permute-start(bf16[2,128,1024]{2,1,0:T(8,128)(2,1)S(1)} %get-tuple-element.87), channel_id=1, source_target_pairs={{0,4},{4,8},{8,12},{1,5},{5,9},{9,13},{2,6},{6,10},{10,14},{3,7},{... | collective-permute-start | bytes 1572872 | tf_op jit(solution)/shard_map/ppermute | solution.py:429
  99.0 24.9 %collective-permute-start.13 = (bf16[1,2,32,1024]{3,2,1,0:T(8,128)(2,1)S(1)}, bf16[1,2,32,1024]{3,2,1,0:T(8,128)(2,1)S(1)}, u32[]{:S(2)}, u32[]{:S(2)}) collective-permute-start(bf16[1,2,32,1024]{3,2,1,0:T(8,128)(2,1)S(1)} %get-tuple-element.91.refs_2_), channel_id=1, source_target_pairs={{4,0},{5,1},{6,2},{7,3},{20,16},{21,17},{22,18},{23,19}} | collective-permute-start | bytes 393224 | tf_op jit(solution)/shard_map/ppermute | solution.py:399
  102.8 21.1 %collective-permute-start.14 = (bf16[1,2,32,1024]{3,2,1,0:T(8,128)(2,1)S(1)}, bf16[1,2,32,1024]{3,2,1,0:T(8,128)(2,1)S(1)}, u32[]{:S(2)}, u32[]{:S(2)}) collective-permute-start(bf16[1,2,32,1024]{3,2,1,0:T(8,128)(2,1)S(1)} %get-tuple-element.91.refs_2_), channel_id=1, source_target_pairs={{8,0},{9,1},{10,2},{11,3},{24,16},{25,17},{26,18},{27,19}} | collective-permute-start | bytes 393224 | tf_op jit(solution)/shard_map/ppermute | solution.py:399
  103.4 20.4 %collective-permute-start.15 = (bf16[1,2,32,1024]{3,2,1,0:T(8,128)(2,1)S(1)}, bf16[1,2,32,1024]{3,2,1,0:T(8,128)(2,1)S(1)}, u32[]{:S(2)}, u32[]{:S(2)}) collective-permute-start(bf16[1,2,32,1024]{3,2,1,0:T(8,128)(2,1)S(1)} %get-tuple-element.91.refs_2_), channel_id=1, source_target_pairs={{12,0},{13,1},{14,2},{15,3},{28,16},{29,17},{30,18},{31,19}} | collective-permute-start | bytes 393224 | tf_op jit(solution)/shard_map/ppermute | solution.py:399
  104.1 19.7 %copy-start.32 = (s32[2]{0:T(128)S(1)}, s32[2]{0:T(128)}, u32[]{:S(2)}) copy-start(s32[2]{0:T(128)} %get-tuple-element.128.refs_0_.at_ref) | copy-start | bytes 28
  124.7 26.7 %collective-permute-start.16 = (bf16[2,128,1024]{2,1,0:T(8,128)(2,1)S(1)}, bf16[2,128,1024]{2,1,0:T(8,128)(2,1)S(1)}, u32[]{:S(2)}, u32[]{:S(2)}) collective-permute-start(bf16[2,128,1024]{2,1,0:T(8,128)(2,1)S(1)} %get-tuple-element.92), channel_id=1, source_target_pairs={{0,4},{4,8},{8,12},{1,5},{5,9},{9,13},{2,6},{6,10},{10,14},{3,7},{... | collective-permute-start | bytes 1572872 | tf_op jit(solution)/shard_map/ppermute | solution.py:429
  128.6 24.2 %copy-start.4 = (bf16[7,2,128,1024]{3,2,1,0:T(8,128)(2,1)}, bf16[7,2,128,1024]{3,2,1,0:T(8,128)(2,1)S(1)}, u32[]{:S(2)}) copy-start(bf16[7,2,128,1024]{3,2,1,0:T(8,128)(2,1)S(1)} %normed_part.10._) | copy-start | bytes 11010052
  153.7 24.9 %collective-permute-start.17 = (bf16[2,128,1024]{2,1,0:T(8,128)(2,1)}, bf16[2,128,1024]{2,1,0:T(8,128)(2,1)}, u32[]{:S(2)}, u32[]{:S(2)}) collective-permute-start(bf16[2,128,1024]{2,1,0:T(8,128)(2,1)} %get-tuple-element.96), channel_id=1, source_target_pairs={{4,8},{8,12},{5,9},{9,13},{6,10},{10,14},{7,11},{11,15},{20,24},{2... | collective-permute-start | bytes 1572872 | tf_op jit(solution)/shard_map/ppermute | solution.py:429
  162.9 15.7 %copy-start.12 = (f32[4,2,128,1024]{3,2,1,0:T(8,128)S(1)}, f32[4,2,128,1024]{3,2,1,0:T(8,128)}, u32[]{:S(2)}) copy-start(f32[4,2,128,1024]{3,2,1,0:T(8,128)} %copy-done.8) | copy-start | bytes 12582916
  180.7 2.4 collective-permute-start.18
  188.0 46.2 %collective-permute-start.22 = (bf16[4,2,64,1024]{3,2,1,0:T(8,128)(2,1)}, bf16[4,2,64,1024]{3,2,1,0:T(8,128)(2,1)}, u32[]{:S(2)}, u32[]{:S(2)}) collective-permute-start(bf16[4,2,64,1024]{3,2,1,0:T(8,128)(2,1)} %slice.46), channel_id=1, source_target_pairs={{12,4},{13,5},{14,6},{15,7},{28,20},{29,21},{30,22},{31,23}} | collective-permute-start | bytes 3145736 | tf_op jit(solution)/shard_map/ppermute | solution.py:443
  227.2 28.5 %collective-permute-start.19 = (bf16[256,512]{1,0:T(8,128)(2,1)S(1)}, bf16[256,512]{1,0:T(8,128)(2,1)S(1)}, u32[]{:S(2)}, u32[]{:S(2)}) collective-permute-start(bf16[256,512]{1,0:T(8,128)(2,1)S(1)} %product.4), channel_id=1, source_target_pairs={{0,2},{2,0},{1,3},{3,1},{4,6},{6,4},{5,7},{7,5},{8,10},{10,8},{9,1... | collective-permute-start | bytes 786440 | tf_op jit(solution)/shard_map/ppermute | solution.py:468
  232.1 23.6 %collective-permute-start.20 = (bf16[256,512]{1,0:T(8,128)(2,1)S(1)}, bf16[256,512]{1,0:T(8,128)(2,1)S(1)}, u32[]{:S(2)}, u32[]{:S(2)}) collective-permute-start(bf16[256,512]{1,0:T(8,128)(2,1)S(1)} %product.5), channel_id=1, source_target_pairs={{0,2},{2,0},{1,3},{3,1},{4,6},{6,4},{5,7},{7,5},{8,10},{10,8},{9,1... | collective-permute-start | bytes 786440 | tf_op jit(solution)/shard_map/ppermute | solution.py:468
  235.6 16.7 %collective-permute-start.23 = (bf16[4,2,32,1024]{3,2,1,0:T(8,128)(2,1)S(1)}, bf16[4,2,32,1024]{3,2,1,0:T(8,128)(2,1)S(1)}, u32[]{:S(2)}, u32[]{:S(2)}) collective-permute-start(bf16[4,2,32,1024]{3,2,1,0:T(8,128)(2,1)S(1)} %slice.48), channel_id=1, source_target_pairs={{4,0},{12,8},{5,1},{13,9},{6,2},{14,10},{7,3},{15,11},{20,16},{28,... | collective-permute-start | bytes 1572872 | tf_op jit(solution)/shard_map/ppermute | solution.py:443
  241.8 14.0 %collective-permute-start.21 = (bf16[256,1024]{1,0:T(8,128)(2,1)S(1)}, bf16[256,1024]{1,0:T(8,128)(2,1)S(1)}, u32[]{:S(2)}, u32[]{:S(2)}) collective-permute-start(bf16[256,1024]{1,0:T(8,128)(2,1)S(1)} %product.6), channel_id=1, source_target_pairs={{0,2},{2,0},{1,3},{3,1},{4,6},{6,4},{5,7},{7,5},{8,10},{10,8},{9,1... | collective-permute-start | bytes 1572872 | tf_op jit(solution)/shard_map/ppermute | solution.py:468
  (46 other events, 123.6 us)
Sparse Core Ops, SparseCore 0:
  10.5 213.2 all-gather.1

commit v7 on v6

--- a/solution.py
+++ b/solution.py
@@ -54,7 +54,7 @@
     tail = spread((jnp.exp(last - cum) * size).T, head_dim)
     weighted = (tail * x_ref[0].astype(f32)).astype(jnp.bfloat16)
     b_t = b_ref[0, 0].astype(f32).T.astype(jnp.bfloat16)
-    end_ref[0, 0] = jnp.dot(b_t, weighted, preferred_element_type=f32)
+    end_ref[0, 0] = jnp.dot(b_t, weighted, preferred_element_type=f32).astype(jnp.bfloat16)
     grow = jnp.exp(cum.T)
     keep_ref[0, 0] = spread(jnp.broadcast_to(grow[tokens - 1 :], (8, heads)), head_dim)
     grow_ref[0, 0] = grow
@@ -129,7 +129,7 @@
             ],
         ),
         out_shape=[
-            jax.ShapeDtypeStruct((groups, sessions, state, width), f32),
+            jax.ShapeDtypeStruct((groups, sessions, state, width), jnp.bfloat16),
             jax.ShapeDtypeStruct((groups, sessions, 8, width), f32),
             jax.ShapeDtypeStruct((sessions, groups, tokens, heads), f32),
         ],
@@ -173,7 +173,7 @@
         first = jnp.concatenate([r[0, 0].astype(jnp.float32) for r in refs[:count]], axis=0)
         state = first if state is None else jnp.where(at_ref[1] == 0, first, state)
     state_ref[0] = state.astype(jnp.bfloat16)
-    leaving_ref[0] = (keep_ref[0, 0, :1] * state + end_ref[0, 0]).astype(jnp.bfloat16)
+    leaving_ref[0] = (keep_ref[0, 0, :1] * state + end_ref[0, 0].astype(jnp.float32)).astype(jnp.bfloat16)
 
 
 def leave_part(at, coming, first, inside, keep, end):
@@ -461,7 +461,7 @@
         theirs = []
         got = moved(final, 0)
         block = jnp.int32(0)
-        for m, part in [(0, (0, 2)), (0, (1, 2))] + [(m, (0, 1)) for m in range(1, share)]:
+        for m, part in [(0, (0, 4)), (0, (1, 4)), (0, (1, 2))] + [(m, (0, 1)) for m in range(1, share)]:
             which = ((1 - head_index) * share + m).reshape(1)
             which, block = lax.optimization_barrier((which, block))
             block = product(which, left, gathered, row_at, part)

time: 265 us -> 273 us (1.030)
  waiting for transfers between devices: 97.6 us -> 85 us
  local copies, waits for them, and re-layouts: 39 us -> 49.6 us
  starting transfers between devices: 40.8 us -> 46.8 us
    ppermute x6, waiting for transfers between devices: 60.8 us -> 50.6 us  [shards(): coming = lax.ppermute(leaving, 'ctx', pairs)]
    unnamed x108 -> x120, local copies, waits for them, and re-layouts: 33.2 us -> 41.2 us
    ppermute x6, starting transfers between devices: 11.4 us -> 18.3 us  [shards(): coming = lax.ppermute(leaving, 'ctx', pairs)]
    all_gather x1, waiting for transfers between devices: 26.4 us -> 21.2 us  [shards(): lax.all_gather(mine, ('groups', 'ctx', 'sess'), axis=0, tiled=True)]
    ppermute x2, waiting for transfers between devices: 1.46 us -> 4.25 us  [moved(): return lax.ppermute(final[:, :, :half], 'ctx', pairs)]
    pallas_call x4 -> x5, Pallas kernels: 20.7 us -> 22.4 us  [product(): pl.pallas_call(product_kernel, grid_spec=pltpu.PrefetchScalarGridSpec(num...]
  transfers between devices with their start and end apart: 25 -> 26, of which waited for: 9 -> 7; matrix products, arithmetic and copies ran while one was open for 3% -> 4% of each run, Pallas kernels for 25% -> 25%
where the time goes in v7:
time: 273 us; the launch traced here: 271 us
  waiting for transfers between devices  85 us (31%)
  Pallas kernels  67.2 us (25%)
  local copies, waits for them, and re-layouts  49.6 us (18%)
  starting transfers between devices  46.8 us (17%)
  between operations  14.9 us (5%)
  other arithmetic  7.23 us (3%)
    ppermute x6, waiting for transfers between devices, shards(): coming = lax.ppermute(leaving, 'ctx', pairs)  50.6 us
    unnamed x120, local copies, waits for them, and re-layouts  41.2 us
    pallas_call x5, Pallas kernels, product(): pl.pallas_call(product_kernel, grid_spec=pltpu.PrefetchScalarGridSpec(num...  22.4 us
    all_gather x1, waiting for transfers between devices, shards(): lax.all_gather(mine, ('groups', 'ctx', 'sess'), axis=0, tiled=True)  21.2 us
    ppermute x12, starting transfers between devices, shards(): lax.ppermute(part, 'ctx', [(k, 0)])  20.3 us
    ppermute x6, starting transfers between devices, shards(): coming = lax.ppermute(leaving, 'ctx', pairs)  18.3 us
    pallas_call x7, Pallas kernels, normed_part(): pl.pallas_call(normed_kernel, grid_spec=pltpu.PrefetchScalarGridSpec(num_...  11.6 us
    pallas_call x7, Pallas kernels, leave_part(): pl.pallas_call(functools.partial(leave_kernel, 0 if first is None else le...  11.5 us
  transfers between devices with their start and end apart: 26, of which 7 were waited for; matrix products, arithmetic and copies ran while one was open for 4% of the time, Pallas kernels for 25%

profile of v7, /device:TPU:12, one launch (start us, length us, event | category | flops | bytes accessed | tf_op | source)
XLA Modules:
  0.0 270.8 jit_solution(10308585125344761701)
XLA Ops:
  7.2 3.1 %constant_dynamic-slice_fusion = bf16[1024,1024]{1,0:T(8,128)(2,1)} fusion(bf16[4096,1024]{1,0:T(8,128)(2,1)} %param.22, s32[]{:T(128)S(6)} %select_n.85), kind=kLoop, calls=%fused_computation.16 | loop fusion | bytes 4194308 | tf_op jit(solution)/shard_map/dynamic_slice | solution.py:376
  11.2 2.2 copy-done.18
  18.1 2.4 collective-permute-start.1
  24.0 8.2 %end_part.1 = (bf16[4,2,128,1024]{3,2,1,0:T(8,128)(2,1)S(1)}, f32[4,2,8,1024]{3,2,1,0:T(8,128)S(1)}, f32[2,4,128,16]{3,2,1,0:T(8,128)S(1)}) custom-call(s32[2]{0:T(128)S(1)} %get-tuple-element.133.limit_ref, bf16[2,128,4096]{2,1,0:T(8,128)(2,1)S(1)} %copy-done.46, bf16[2,4,128,128]{3,2,1,0:T(8,128)(2,1)S(1)} %bitcast.54, f32[2,4,16,128]{3,2,1,0:T(8,128)S(1)} %bitcast.56, ...), custom_call_target="tpu_custom_call" | custom-call | flops 2000000000 | bytes 8388608 | tf_op jit(solution)/shard_map/end_part/pallas_call | solution.py:119
  32.8 2.3 leave_part.7
  39.1 5.4 %collective-permute-start.5 = (bf16[1,2,32,1024]{3,2,1,0:T(8,128)(2,1)S(1)}, bf16[1,2,32,1024]{3,2,1,0:T(8,128)(2,1)S(1)}, u32[]{:S(2)}, u32[]{:S(2)}) collective-permute-start(bf16[1,2,32,1024]{3,2,1,0:T(8,128)(2,1)S(1)} %get-tuple-element.76.refs_2_), channel_id=1, source_target_pairs={{4,0},{5,1},{6,2},{7,3},{20,16},{21,17},{22,18},{23,19}} | collective-permute-start | bytes 393224 | tf_op jit(solution)/shard_map/ppermute | solution.py:399
  51.4 8.9 %inside_part.1.y_ref = f32[2,128,4096]{2,1,0:T(8,128)S(1)} custom-call(s32[2]{0:T(128)S(1)} %copy-done.44, bf16[2,128,4096]{2,1,0:T(8,128)(2,1)S(1)} %copy-done.47, bf16[2,4,128,128]{3,2,1,0:T(8,128)(2,1)S(1)} %bitcast.55, bf16[2,4,128,128]{3,2,1,0:T(8,128)(2,1)S(1)} %bitcast.35, f32[2,4,16,128]{3,2,1,0:T(8,128)S(1)} %bitcast.57, ...), custom_call_target="tpu_custom_call" | custom-call | flops 4000000000 | bytes 8388608 | tf_op jit(solution)/shard_map/inside_part/pallas_call | solution.py:148
  60.9 2.6 copy-done.14
  67.1 2.5 leave_part.8
  70.4 4.0 %collective-permute-start.8 = (bf16[2,128,1024]{2,1,0:T(8,128)(2,1)}, bf16[2,128,1024]{2,1,0:T(8,128)(2,1)}, u32[]{:S(2)}, u32[]{:S(2)}) collective-permute-start(bf16[2,128,1024]{2,1,0:T(8,128)(2,1)} %get-tuple-element.80), channel_id=1, source_target_pairs={{0,4},{4,8},{1,5},{5,9},{2,6},{6,10},{3,7},{7,11},{16,20},{20,24},... | collective-permute-start | bytes 1572872 | tf_op jit(solution)/shard_map/ppermute | solution.py:429
  74.4 2.7 collective-permute-start.9
  79.8 8.9 %collective-permute-done.9.refs_3_ = bf16[1,2,32,1024]{3,2,1,0:T(8,128)(2,1)S(1)} collective-permute-done((bf16[1,2,32,1024]{3,2,1,0:T(8,128)(2,1)S(1)}, bf16[1,2,32,1024]{3,2,1,0:T(8,128)(2,1)S(1)}, u32[]{:S(2)}, u32[]{:S(2)}) %collective-permute-start.9) | collective-permute-done | bytes 131104 | tf_op jit(solution)/shard_map/ppermute | solution.py:399
  88.7 2.1 copy-done.3
  90.8 2.2 copy-done.9
  100.2 3.9 %collective-permute-start.12 = (bf16[2,128,1024]{2,1,0:T(8,128)(2,1)S(1)}, bf16[2,128,1024]{2,1,0:T(8,128)(2,1)S(1)}, u32[]{:S(2)}, u32[]{:S(2)}) collective-permute-start(bf16[2,128,1024]{2,1,0:T(8,128)(2,1)S(1)} %get-tuple-element.89), channel_id=1, source_target_pairs={{0,4},{4,8},{8,12},{1,5},{5,9},{9,13},{2,6},{6,10},{10,14},{3,7},{... | collective-permute-start | bytes 1572872 | tf_op jit(solution)/shard_map/ppermute | solution.py:429
  109.1 18.3 %collective-permute-done.12.refs_1_ = bf16[2,128,1024]{2,1,0:T(8,128)(2,1)S(1)} collective-permute-done((bf16[2,128,1024]{2,1,0:T(8,128)(2,1)S(1)}, bf16[2,128,1024]{2,1,0:T(8,128)(2,1)S(1)}, u32[]{:S(2)}, u32[]{:S(2)}) %collective-permute-start.12) | collective-permute-done | bytes 524320 | tf_op jit(solution)/shard_map/ppermute | solution.py:429
  128.3 3.9 %collective-permute-start.16 = (bf16[2,128,1024]{2,1,0:T(8,128)(2,1)S(1)}, bf16[2,128,1024]{2,1,0:T(8,128)(2,1)S(1)}, u32[]{:S(2)}, u32[]{:S(2)}) collective-permute-start(bf16[2,128,1024]{2,1,0:T(8,128)(2,1)S(1)} %get-tuple-element.94), channel_id=1, source_target_pairs={{0,4},{4,8},{8,12},{1,5},{5,9},{9,13},{2,6},{6,10},{10,14},{3,7},{... | collective-permute-start | bytes 1572872 | tf_op jit(solution)/shard_map/ppermute | solution.py:429
  135.6 19.6 %collective-permute-done.16.refs_1_ = bf16[2,128,1024]{2,1,0:T(8,128)(2,1)S(1)} collective-permute-done((bf16[2,128,1024]{2,1,0:T(8,128)(2,1)S(1)}, bf16[2,128,1024]{2,1,0:T(8,128)(2,1)S(1)}, u32[]{:S(2)}, u32[]{:S(2)}) %collective-permute-start.16) | collective-permute-done | bytes 524320 | tf_op jit(solution)/shard_map/ppermute | solution.py:429
  157.5 4.7 %collective-permute-start.17 = (bf16[2,128,1024]{2,1,0:T(8,128)(2,1)}, bf16[2,128,1024]{2,1,0:T(8,128)(2,1)}, u32[]{:S(2)}, u32[]{:S(2)}) collective-permute-start(bf16[2,128,1024]{2,1,0:T(8,128)(2,1)} %get-tuple-element.98), channel_id=1, source_target_pairs={{4,8},{8,12},{5,9},{9,13},{6,10},{10,14},{7,11},{11,15},{20,24},{2... | collective-permute-start | bytes 1572872 | tf_op jit(solution)/shard_map/ppermute | solution.py:429
  164.3 2.2 copy-done.11
  171.5 12.4 %collective-permute-done.17.refs_1_ = bf16[2,128,1024]{2,1,0:T(8,128)(2,1)} collective-permute-done((bf16[2,128,1024]{2,1,0:T(8,128)(2,1)}, bf16[2,128,1024]{2,1,0:T(8,128)(2,1)}, u32[]{:S(2)}, u32[]{:S(2)}) %collective-permute-start.17) | collective-permute-done | bytes 524320 | tf_op jit(solution)/shard_map/ppermute | solution.py:429
  195.3 2.1 copy-done.7
  197.4 2.2 copy-done.13
  202.6 21.2 %all-gather.2.cloned.1.call-done.refs_0_.refs_1_.refs_2_.refs_3_ = bf16[16384,1024]{1,0:T(8,128)(2,1)} async-done(((bf16[1024,1024]{1,0:T(8,128)(2,1)}), bf16[16384,1024]{1,0:T(8,128)(2,1)}) %all-gather.2.cloned.1.call-update) | async-done | bytes 33554448 | tf_op jit(solution)/shard_map/all_gather | solution.py:377
  223.8 2.9 %product.5 = bf16[256,256]{1,0:T(8,128)(2,1)} custom-call(s32[1]{0:T(128)} %bitcast.block_ref, bf16[4,256,1024]{2,1,0:T(8,128)(2,1)S(1)} %bitcast.30, bf16[16384,1024]{1,0:T(8,128)(2,1)} %all-gather.2.cloned.1.call-done.refs_0_.refs_1_.refs_2_.refs_3_, bf16[16384,1024]{1,0:T(8,128)(2,1)} %all-gather.2.cloned.1.call-done.refs_0_.refs_1_.refs_2_.refs_3_, ...), custom_call_target="tpu_custom_call" | custom-call | flops 536870912 | bytes 4194304 | tf_op jit(solution)/shard_map/product/pallas_call | solution.py:322
  228.1 2.2 product.6
  231.0 3.4 %product.7 = bf16[256,512]{1,0:T(8,128)(2,1)S(1)} custom-call(s32[1]{0:T(128)} %bitcast.block_ref, bf16[4,256,1024]{2,1,0:T(8,128)(2,1)S(1)} %bitcast.32, bf16[16384,1024]{1,0:T(8,128)(2,1)} %all-gather.2.cloned.1.call-done.refs_0_.refs_1_.refs_2_.refs_3_, bf16[16384,1024]{1,0:T(8,128)(2,1)} %all-gather.2.cloned.1.call-done.refs_0_.refs_1_.refs_2_.refs_3_, ...), custom_call_target="tpu_custom_call" | custom-call | flops 1073741824 | bytes 6291456 | tf_op jit(solution)/shard_map/product/pallas_call | solution.py:322
  236.0 4.2 %collective-permute-done.23 = bf16[4,2,64,1024]{3,2,1,0:T(8,128)(2,1)} collective-permute-done((bf16[4,2,64,1024]{3,2,1,0:T(8,128)(2,1)}, bf16[4,2,64,1024]{3,2,1,0:T(8,128)(2,1)}, u32[]{:S(2)}, u32[]{:S(2)}) %collective-permute-start.23) | collective-permute-done | bytes 1048608 | tf_op jit(solution)/shard_map/ppermute | solution.py:443
  242.9 4.8 %product.8 = bf16[256,1024]{1,0:T(8,128)(2,1)S(1)} custom-call(s32[1]{0:T(128)} %bitcast.17.block_ref, bf16[4,256,1024]{2,1,0:T(8,128)(2,1)S(1)} %bitcast.33, bf16[16384,1024]{1,0:T(8,128)(2,1)} %all-gather.2.cloned.1.call-done.refs_0_.refs_1_.refs_2_.refs_3_, bf16[16384,1024]{1,0:T(8,128)(2,1)} %all-gather.2.cloned.1.call-done.refs_0_.refs_1_.refs_2_.refs_3_, ...), custom_call_target="tpu_custom_call" | custom-call | flops 2147483648 | bytes 10485760 | tf_op jit(solution)/shard_map/product/pallas_call | solution.py:322
  249.3 9.0 %product.9 = bf16[256,2048]{1,0:T(8,128)(2,1)S(1)} custom-call(s32[2]{0:T(128)S(1)} %iota_add_fusion.block_ref, bf16[4,256,1024]{2,1,0:T(8,128)(2,1)S(1)} %bitcast.34, bf16[16384,1024]{1,0:T(8,128)(2,1)} %all-gather.2.cloned.1.call-done.refs_0_.refs_1_.refs_2_.refs_3_, bf16[16384,1024]{1,0:T(8,128)(2,1)} %all-gather.2.cloned.1.call-done.refs_0_.refs_1_.refs_2_.refs_3_, ...), custom_call_target="tpu_custom_call" | custom-call | flops 4294967296 | bytes 18874368 | tf_op jit(solution)/shard_map/product/pallas_call | solution.py:322
  258.4 3.3 %final_part.1 = f32[2,64,32,64]{3,2,1,0:T(8,128)} custom-call(bf16[4,2,32,1024]{3,2,1,0:T(8,128)(2,1)S(1)} %slice_select_fusion.1.value_ref), custom_call_target="tpu_custom_call" | custom-call | tf_op jit(solution)/shard_map/final_part/pallas_call | solution.py:292
  261.8 2.2 multiply_convert_fusion
  (192 shorter events, 76.0 us)
Async XLA Ops:
  7.2 7.6 %copy-start = (bf16[2,128,8,128]{3,2,1,0:T(8,128)(2,1)S(1)}, bf16[2,128,8,128]{3,2,1,0:T(8,128)(2,1)}, u32[]{:S(2)}) copy-start(bf16[2,128,8,128]{3,2,1,0:T(8,128)(2,1)} %param.15) | copy-start | bytes 1572868
  7.2 216.6 %all-gather.2.cloned.1.call-start = ((), (), s32[]{:S(2)}) async-start(), calls=%async_computation | async-start | bytes 35651584 | tf_op jit(solution)/shard_map/all_gather | solution.py:377
  14.7 3.3 %collective-permute-start = (bf16[4,2,32,1024]{3,2,1,0:T(8,128)(2,1)S(1)}, bf16[4,2,32,1024]{3,2,1,0:T(8,128)(2,1)S(1)}, u32[]{:S(2)}, u32[]{:S(2)}) collective-permute-start(bf16[4,2,32,1024]{3,2,1,0:T(8,128)(2,1)S(1)} %slice.40), channel_id=1, source_target_pairs={{0,1},{1,0},{2,3},{3,2},{4,5},{5,4},{6,7},{7,6},{8,9},{9,8},{10,11... | collective-permute-start | bytes 1572872 | tf_op jit(solution)/shard_map/ppermute | solution.py:391
  18.1 14.7 %collective-permute-start.1 = (bf16[1,2,32,1024]{3,2,1,0:T(8,128)(2,1)S(1)}, bf16[1,2,32,1024]{3,2,1,0:T(8,128)(2,1)S(1)}, u32[]{:S(2)}, u32[]{:S(2)}) collective-permute-start(bf16[1,2,32,1024]{3,2,1,0:T(8,128)(2,1)S(1)} %get-tuple-element.63.refs_1_), channel_id=1, source_target_pairs={{4,0},{5,1},{6,2},{7,3},{20,16},{21,17},{22,18},{23,19}} | collective-permute-start | bytes 393224 | tf_op jit(solution)/shard_map/ppermute | solution.py:399
  20.5 12.3 %collective-permute-start.2 = (bf16[1,2,32,1024]{3,2,1,0:T(8,128)(2,1)S(1)}, bf16[1,2,32,1024]{3,2,1,0:T(8,128)(2,1)}, u32[]{:S(2)}, u32[]{:S(2)}) collective-permute-start(bf16[1,2,32,1024]{3,2,1,0:T(8,128)(2,1)S(1)} %get-tuple-element.63.refs_1_), channel_id=1, source_target_pairs={{8,0},{9,1},{10,2},{11,3},{24,16},{25,17},{26,18},{27,19}} | collective-permute-start | bytes 393224 | tf_op jit(solution)/shard_map/ppermute | solution.py:399
  21.8 11.0 %collective-permute-start.3 = (bf16[1,2,32,1024]{3,2,1,0:T(8,128)(2,1)S(1)}, bf16[1,2,32,1024]{3,2,1,0:T(8,128)(2,1)}, u32[]{:S(2)}, u32[]{:S(2)}) collective-permute-start(bf16[1,2,32,1024]{3,2,1,0:T(8,128)(2,1)S(1)} %get-tuple-element.63.refs_1_), channel_id=1, source_target_pairs={{12,0},{13,1},{14,2},{15,3},{28,16},{29,17},{30,18},{31,19}} | collective-permute-start | bytes 393224 | tf_op jit(solution)/shard_map/ppermute | solution.py:399
  36.0 31.1 %collective-permute-start.4 = (bf16[2,128,1024]{2,1,0:T(8,128)(2,1)}, bf16[2,128,1024]{2,1,0:T(8,128)(2,1)}, u32[]{:S(2)}, u32[]{:S(2)}) collective-permute-start(bf16[2,128,1024]{2,1,0:T(8,128)(2,1)} %get-tuple-element.69), channel_id=1, source_target_pairs={{0,4},{1,5},{2,6},{3,7},{16,20},{17,21},{18,22},{19,23}} | collective-permute-start | bytes 1572872 | tf_op jit(solution)/shard_map/ppermute | solution.py:429
  39.1 28.0 %collective-permute-start.5 = (bf16[1,2,32,1024]{3,2,1,0:T(8,128)(2,1)S(1)}, bf16[1,2,32,1024]{3,2,1,0:T(8,128)(2,1)S(1)}, u32[]{:S(2)}, u32[]{:S(2)}) collective-permute-start(bf16[1,2,32,1024]{3,2,1,0:T(8,128)(2,1)S(1)} %get-tuple-element.76.refs_2_), channel_id=1, source_target_pairs={{4,0},{5,1},{6,2},{7,3},{20,16},{21,17},{22,18},{23,19}} | collective-permute-start | bytes 393224 | tf_op jit(solution)/shard_map/ppermute | solution.py:399
  44.4 22.7 %collective-permute-start.6 = (bf16[1,2,32,1024]{3,2,1,0:T(8,128)(2,1)S(1)}, bf16[1,2,32,1024]{3,2,1,0:T(8,128)(2,1)S(1)}, u32[]{:S(2)}, u32[]{:S(2)}) collective-permute-start(bf16[1,2,32,1024]{3,2,1,0:T(8,128)(2,1)S(1)} %get-tuple-element.76.refs_2_), channel_id=1, source_target_pairs={{8,0},{9,1},{10,2},{11,3},{24,16},{25,17},{26,18},{27,19}} | collective-permute-start | bytes 393224 | tf_op jit(solution)/shard_map/ppermute | solution.py:399
  45.1 22.0 %collective-permute-start.7 = (bf16[1,2,32,1024]{3,2,1,0:T(8,128)(2,1)S(1)}, bf16[1,2,32,1024]{3,2,1,0:T(8,128)(2,1)S(1)}, u32[]{:S(2)}, u32[]{:S(2)}) collective-permute-start(bf16[1,2,32,1024]{3,2,1,0:T(8,128)(2,1)S(1)} %get-tuple-element.76.refs_2_), channel_id=1, source_target_pairs={{12,0},{13,1},{14,2},{15,3},{28,16},{29,17},{30,18},{31,19}} | collective-permute-start | bytes 393224 | tf_op jit(solution)/shard_map/ppermute | solution.py:399
  70.4 27.8 %collective-permute-start.8 = (bf16[2,128,1024]{2,1,0:T(8,128)(2,1)}, bf16[2,128,1024]{2,1,0:T(8,128)(2,1)}, u32[]{:S(2)}, u32[]{:S(2)}) collective-permute-start(bf16[2,128,1024]{2,1,0:T(8,128)(2,1)} %get-tuple-element.80), channel_id=1, source_target_pairs={{0,4},{4,8},{1,5},{5,9},{2,6},{6,10},{3,7},{7,11},{16,20},{20,24},... | collective-permute-start | bytes 1572872 | tf_op jit(solution)/shard_map/ppermute | solution.py:429
  74.4 14.3 %collective-permute-start.9 = (bf16[1,2,32,1024]{3,2,1,0:T(8,128)(2,1)S(1)}, bf16[1,2,32,1024]{3,2,1,0:T(8,128)(2,1)S(1)}, u32[]{:S(2)}, u32[]{:S(2)}) collective-permute-start(bf16[1,2,32,1024]{3,2,1,0:T(8,128)(2,1)S(1)} %get-tuple-element.85.refs_2_), channel_id=1, source_target_pairs={{4,0},{5,1},{6,2},{7,3},{20,16},{21,17},{22,18},{23,19}} | collective-permute-start | bytes 393224 | tf_op jit(solution)/shard_map/ppermute | solution.py:399
  77.1 11.6 %collective-permute-start.10 = (bf16[1,2,32,1024]{3,2,1,0:T(8,128)(2,1)S(1)}, bf16[1,2,32,1024]{3,2,1,0:T(8,128)(2,1)}, u32[]{:S(2)}, u32[]{:S(2)}) collective-permute-start(bf16[1,2,32,1024]{3,2,1,0:T(8,128)(2,1)S(1)} %get-tuple-element.85.refs_2_), channel_id=1, source_target_pairs={{8,0},{9,1},{10,2},{11,3},{24,16},{25,17},{26,18},{27,19}} | collective-permute-start | bytes 393224 | tf_op jit(solution)/shard_map/ppermute | solution.py:399
  78.4 10.3 %collective-permute-start.11 = (bf16[1,2,32,1024]{3,2,1,0:T(8,128)(2,1)S(1)}, bf16[1,2,32,1024]{3,2,1,0:T(8,128)(2,1)}, u32[]{:S(2)}, u32[]{:S(2)}) collective-permute-start(bf16[1,2,32,1024]{3,2,1,0:T(8,128)(2,1)S(1)} %get-tuple-element.85.refs_2_), channel_id=1, source_target_pairs={{12,0},{13,1},{14,2},{15,3},{28,16},{29,17},{30,18},{31,19}} | collective-permute-start | bytes 393224 | tf_op jit(solution)/shard_map/ppermute | solution.py:399
  79.8 75.5 %copy-start.39 = (s32[2]{0:T(128)}, s32[2]{0:T(128)S(1)}, u32[]{:S(2)}) copy-start(s32[2]{0:T(128)S(1)} %get-tuple-element.130.refs_0_.at_ref) | copy-start | bytes 28
  96.3 11.2 %copy-start.10 = (f32[2,128,4096]{2,1,0:T(8,128)S(1)}, f32[2,128,4096]{2,1,0:T(8,128)}, u32[]{:S(2)}) copy-start(f32[2,128,4096]{2,1,0:T(8,128)} %copy-done.8) | copy-start | bytes 12582916
  100.2 27.2 %collective-permute-start.12 = (bf16[2,128,1024]{2,1,0:T(8,128)(2,1)S(1)}, bf16[2,128,1024]{2,1,0:T(8,128)(2,1)S(1)}, u32[]{:S(2)}, u32[]{:S(2)}) collective-permute-start(bf16[2,128,1024]{2,1,0:T(8,128)(2,1)S(1)} %get-tuple-element.89), channel_id=1, source_target_pairs={{0,4},{4,8},{8,12},{1,5},{5,9},{9,13},{2,6},{6,10},{10,14},{3,7},{... | collective-permute-start | bytes 1572872 | tf_op jit(solution)/shard_map/ppermute | solution.py:429
  104.0 23.3 %collective-permute-start.13 = (bf16[1,2,32,1024]{3,2,1,0:T(8,128)(2,1)S(1)}, bf16[1,2,32,1024]{3,2,1,0:T(8,128)(2,1)S(1)}, u32[]{:S(2)}, u32[]{:S(2)}) collective-permute-start(bf16[1,2,32,1024]{3,2,1,0:T(8,128)(2,1)S(1)} %get-tuple-element.93.refs_2_), channel_id=1, source_target_pairs={{4,0},{5,1},{6,2},{7,3},{20,16},{21,17},{22,18},{23,19}} | collective-permute-start | bytes 393224 | tf_op jit(solution)/shard_map/ppermute | solution.py:399
  106.1 21.3 %collective-permute-start.14 = (bf16[1,2,32,1024]{3,2,1,0:T(8,128)(2,1)S(1)}, bf16[1,2,32,1024]{3,2,1,0:T(8,128)(2,1)S(1)}, u32[]{:S(2)}, u32[]{:S(2)}) collective-permute-start(bf16[1,2,32,1024]{3,2,1,0:T(8,128)(2,1)S(1)} %get-tuple-element.93.refs_2_), channel_id=1, source_target_pairs={{8,0},{9,1},{10,2},{11,3},{24,16},{25,17},{26,18},{27,19}} | collective-permute-start | bytes 393224 | tf_op jit(solution)/shard_map/ppermute | solution.py:399
  106.7 20.7 %collective-permute-start.15 = (bf16[1,2,32,1024]{3,2,1,0:T(8,128)(2,1)S(1)}, bf16[1,2,32,1024]{3,2,1,0:T(8,128)(2,1)S(1)}, u32[]{:S(2)}, u32[]{:S(2)}) collective-permute-start(bf16[1,2,32,1024]{3,2,1,0:T(8,128)(2,1)S(1)} %get-tuple-element.93.refs_2_), channel_id=1, source_target_pairs={{12,0},{13,1},{14,2},{15,3},{28,16},{29,17},{30,18},{31,19}} | collective-permute-start | bytes 393224 | tf_op jit(solution)/shard_map/ppermute | solution.py:399
  107.4 20.0 %copy-start.36 = (s32[2]{0:T(128)S(1)}, s32[2]{0:T(128)}, u32[]{:S(2)}) copy-start(s32[2]{0:T(128)} %get-tuple-element.132.refs_0_.at_ref) | copy-start | bytes 28
  128.3 27.0 %collective-permute-start.16 = (bf16[2,128,1024]{2,1,0:T(8,128)(2,1)S(1)}, bf16[2,128,1024]{2,1,0:T(8,128)(2,1)S(1)}, u32[]{:S(2)}, u32[]{:S(2)}) collective-permute-start(bf16[2,128,1024]{2,1,0:T(8,128)(2,1)S(1)} %get-tuple-element.94), channel_id=1, source_target_pairs={{0,4},{4,8},{8,12},{1,5},{5,9},{9,13},{2,6},{6,10},{10,14},{3,7},{... | collective-permute-start | bytes 1572872 | tf_op jit(solution)/shard_map/ppermute | solution.py:429
  157.5 26.5 %collective-permute-start.17 = (bf16[2,128,1024]{2,1,0:T(8,128)(2,1)}, bf16[2,128,1024]{2,1,0:T(8,128)(2,1)}, u32[]{:S(2)}, u32[]{:S(2)}) collective-permute-start(bf16[2,128,1024]{2,1,0:T(8,128)(2,1)} %get-tuple-element.98), channel_id=1, source_target_pairs={{4,8},{8,12},{5,9},{9,13},{6,10},{10,14},{7,11},{11,15},{20,24},{2... | collective-permute-start | bytes 1572872 | tf_op jit(solution)/shard_map/ppermute | solution.py:429
  169.8 16.5 %copy-start.12 = (f32[2,128,4096]{2,1,0:T(8,128)S(1)}, f32[2,128,4096]{2,1,0:T(8,128)}, u32[]{:S(2)}) copy-start(f32[2,128,4096]{2,1,0:T(8,128)} %copy-done.8) | copy-start | bytes 12582916
  185.7 2.4 collective-permute-start.18
  193.0 47.2 %collective-permute-start.23 = (bf16[4,2,64,1024]{3,2,1,0:T(8,128)(2,1)}, bf16[4,2,64,1024]{3,2,1,0:T(8,128)(2,1)}, u32[]{:S(2)}, u32[]{:S(2)}) collective-permute-start(bf16[4,2,64,1024]{3,2,1,0:T(8,128)(2,1)} %slice.46), channel_id=1, source_target_pairs={{12,4},{13,5},{14,6},{15,7},{28,20},{29,21},{30,22},{31,23}} | collective-permute-start | bytes 3145736 | tf_op jit(solution)/shard_map/ppermute | solution.py:443
  226.7 35.1 %collective-permute-start.19 = (bf16[256,256]{1,0:T(8,128)(2,1)}, bf16[256,256]{1,0:T(8,128)(2,1)}, u32[]{:S(2)}, u32[]{:S(2)}) collective-permute-start(bf16[256,256]{1,0:T(8,128)(2,1)} %product.5), channel_id=1, source_target_pairs={{0,2},{2,0},{1,3},{3,1},{4,6},{6,4},{5,7},{7,5},{8,10},{10,8},{9,1... | collective-permute-start | bytes 393224 | tf_op jit(solution)/shard_map/ppermute | solution.py:468
  230.4 9.8 %copy-start.51 = (bf16[4,2,128,1024]{3,2,1,0:T(8,128)(2,1)S(1)}, bf16[4,2,128,1024]{3,2,1,0:T(8,128)(2,1)}, u32[]{:S(2)}) copy-start(bf16[4,2,128,1024]{3,2,1,0:T(8,128)(2,1)} %copy-done.50) | copy-start | bytes 6291460
  230.4 31.3 %collective-permute-start.20 = (bf16[256,256]{1,0:T(8,128)(2,1)S(1)}, bf16[256,256]{1,0:T(8,128)(2,1)S(1)}, u32[]{:S(2)}, u32[]{:S(2)}) collective-permute-start(bf16[256,256]{1,0:T(8,128)(2,1)S(1)} %product.6), channel_id=1, source_target_pairs={{0,2},{2,0},{1,3},{3,1},{4,6},{6,4},{5,7},{7,5},{8,10},{10,8},{9,1... | collective-permute-start | bytes 393224 | tf_op jit(solution)/shard_map/ppermute | solution.py:468
  234.4 27.3 %collective-permute-start.21 = (bf16[256,512]{1,0:T(8,128)(2,1)S(1)}, bf16[256,512]{1,0:T(8,128)(2,1)S(1)}, u32[]{:S(2)}, u32[]{:S(2)}) collective-permute-start(bf16[256,512]{1,0:T(8,128)(2,1)S(1)} %product.7), channel_id=1, source_target_pairs={{0,2},{2,0},{1,3},{3,1},{4,6},{6,4},{5,7},{7,5},{8,10},{10,8},{9,1... | collective-permute-start | bytes 786440 | tf_op jit(solution)/shard_map/ppermute | solution.py:468
  241.6 16.7 %collective-permute-start.24 = (bf16[4,2,32,1024]{3,2,1,0:T(8,128)(2,1)S(1)}, bf16[4,2,32,1024]{3,2,1,0:T(8,128)(2,1)S(1)}, u32[]{:S(2)}, u32[]{:S(2)}) collective-permute-start(bf16[4,2,32,1024]{3,2,1,0:T(8,128)(2,1)S(1)} %slice.48), channel_id=1, source_target_pairs={{4,0},{12,8},{5,1},{13,9},{6,2},{14,10},{7,3},{15,11},{20,16},{28,... | collective-permute-start | bytes 1572872 | tf_op jit(solution)/shard_map/ppermute | solution.py:443
  247.7 14.0 %collective-permute-start.22 = (bf16[256,1024]{1,0:T(8,128)(2,1)S(1)}, bf16[256,1024]{1,0:T(8,128)(2,1)S(1)}, u32[]{:S(2)}, u32[]{:S(2)}) collective-permute-start(bf16[256,1024]{1,0:T(8,128)(2,1)S(1)} %product.8), channel_id=1, source_target_pairs={{0,2},{2,0},{1,3},{3,1},{4,6},{6,4},{5,7},{7,5},{8,10},{10,8},{9,1... | collective-permute-start | bytes 1572872 | tf_op jit(solution)/shard_map/ppermute | solution.py:468
  (53 other events, 136.4 us)
Sparse Core Ops, SparseCore 0:
  10.5 213.2 all-gather.1

commit v8 on v7

--- a/solution.py
+++ b/solution.py
@@ -461,7 +461,7 @@
         theirs = []
         got = moved(final, 0)
         block = jnp.int32(0)
-        for m, part in [(0, (0, 4)), (0, (1, 4)), (0, (1, 2))] + [(m, (0, 1)) for m in range(1, share)]:
+        for m, part in [(0, (0, 2)), (0, (1, 2))] + [(m, (0, 1)) for m in range(1, share)]:
             which = ((1 - head_index) * share + m).reshape(1)
             which, block = lax.optimization_barrier((which, block))
             block = product(which, left, gathered, row_at, part)

time: 273 us -> 274 us (level)
  waiting for transfers between devices: 85 us -> 90 us
    ppermute x2, waiting for transfers between devices: 4.25 us -> 9.12 us  [moved(): return lax.ppermute(final[:, :, :half], 'ctx', pairs)]
    pallas_call x5 -> x4, Pallas kernels: 22.4 us -> 20.7 us  [product(): pl.pallas_call(product_kernel, grid_spec=pltpu.PrefetchScalarGridSpec(num...]
  transfers between devices with their start and end apart: 26 -> 25, of which waited for: 7 -> 7; matrix products, arithmetic and copies ran while one was open for 4% -> 4% of each run, Pallas kernels for 25% -> 24%
where the time goes in v8:
time: 274 us; the launch traced here: 272 us
  waiting for transfers between devices  90 us (33%)
  Pallas kernels  65.6 us (24%)
  local copies, waits for them, and re-layouts  49.5 us (18%)
  starting transfers between devices  45.6 us (17%)
  between operations  14.9 us (5%)
  other arithmetic  6.32 us (2%)
    ppermute x6, waiting for transfers between devices, shards(): coming = lax.ppermute(leaving, 'ctx', pairs)  50.7 us
    unnamed x120, local copies, waits for them, and re-layouts  41.1 us
    all_gather x1, waiting for transfers between devices, shards(): lax.all_gather(mine, ('groups', 'ctx', 'sess'), axis=0, tiled=True)  21.3 us
    pallas_call x4, Pallas kernels, product(): pl.pallas_call(product_kernel, grid_spec=pltpu.PrefetchScalarGridSpec(num...  20.7 us
    ppermute x12, starting transfers between devices, shards(): lax.ppermute(part, 'ctx', [(k, 0)])  20.2 us
    ppermute x6, starting transfers between devices, shards(): coming = lax.ppermute(leaving, 'ctx', pairs)  18.4 us
    pallas_call x7, Pallas kernels, normed_part(): pl.pallas_call(normed_kernel, grid_spec=pltpu.PrefetchScalarGridSpec(num_...  11.7 us
    pallas_call x7, Pallas kernels, leave_part(): pl.pallas_call(functools.partial(leave_kernel, 0 if first is None else le...  11.6 us
  transfers between devices with their start and end apart: 25, of which 7 were waited for; matrix products, arithmetic and copies ran while one was open for 4% of the time, Pallas kernels for 24%

profile of v8, /device:TPU:12, one launch (start us, length us, event | category | flops | bytes accessed | tf_op | source)
XLA Modules:
  0.0 271.9 jit_solution(6025739036323738783)
XLA Ops:
  7.2 3.1 %constant_dynamic-slice_fusion = bf16[1024,1024]{1,0:T(8,128)(2,1)} fusion(bf16[4096,1024]{1,0:T(8,128)(2,1)} %param.22, s32[]{:T(128)S(6)} %select_n.85), kind=kLoop, calls=%fused_computation.16 | loop fusion | bytes 4194308 | tf_op jit(solution)/shard_map/dynamic_slice | solution.py:376
  11.2 2.2 copy-done.18
  18.0 2.4 collective-permute-start.1
  23.9 8.2 %end_part.1 = (bf16[4,2,128,1024]{3,2,1,0:T(8,128)(2,1)S(1)}, f32[4,2,8,1024]{3,2,1,0:T(8,128)S(1)}, f32[2,4,128,16]{3,2,1,0:T(8,128)S(1)}) custom-call(s32[2]{0:T(128)S(1)} %get-tuple-element.129.limit_ref, bf16[2,128,4096]{2,1,0:T(8,128)(2,1)S(1)} %copy-done.46, bf16[2,4,128,128]{3,2,1,0:T(8,128)(2,1)S(1)} %bitcast.53, f32[2,4,16,128]{3,2,1,0:T(8,128)S(1)} %bitcast.55, ...), custom_call_target="tpu_custom_call" | custom-call | flops 2000000000 | bytes 8388608 | tf_op jit(solution)/shard_map/end_part/pallas_call | solution.py:119
  32.8 2.3 leave_part.7
  39.0 5.3 %collective-permute-start.5 = (bf16[1,2,32,1024]{3,2,1,0:T(8,128)(2,1)S(1)}, bf16[1,2,32,1024]{3,2,1,0:T(8,128)(2,1)S(1)}, u32[]{:S(2)}, u32[]{:S(2)}) collective-permute-start(bf16[1,2,32,1024]{3,2,1,0:T(8,128)(2,1)S(1)} %get-tuple-element.74.refs_2_), channel_id=1, source_target_pairs={{4,0},{5,1},{6,2},{7,3},{20,16},{21,17},{22,18},{23,19}} | collective-permute-start | bytes 393224 | tf_op jit(solution)/shard_map/ppermute | solution.py:399
  51.2 8.9 %inside_part.1.y_ref = f32[2,128,4096]{2,1,0:T(8,128)S(1)} custom-call(s32[2]{0:T(128)S(1)} %copy-done.44, bf16[2,128,4096]{2,1,0:T(8,128)(2,1)S(1)} %copy-done.47, bf16[2,4,128,128]{3,2,1,0:T(8,128)(2,1)S(1)} %bitcast.54, bf16[2,4,128,128]{3,2,1,0:T(8,128)(2,1)S(1)} %bitcast.34, f32[2,4,16,128]{3,2,1,0:T(8,128)S(1)} %bitcast.56, ...), custom_call_target="tpu_custom_call" | custom-call | flops 4000000000 | bytes 8388608 | tf_op jit(solution)/shard_map/inside_part/pallas_call | solution.py:148
  60.7 2.6 copy-done.14
  67.0 2.5 leave_part.8
  70.3 4.0 %collective-permute-start.8 = (bf16[2,128,1024]{2,1,0:T(8,128)(2,1)}, bf16[2,128,1024]{2,1,0:T(8,128)(2,1)}, u32[]{:S(2)}, u32[]{:S(2)}) collective-permute-start(bf16[2,128,1024]{2,1,0:T(8,128)(2,1)} %get-tuple-element.78), channel_id=1, source_target_pairs={{0,4},{4,8},{1,5},{5,9},{2,6},{6,10},{3,7},{7,11},{16,20},{20,24},... | collective-permute-start | bytes 1572872 | tf_op jit(solution)/shard_map/ppermute | solution.py:429
  74.3 2.6 collective-permute-start.9
  79.6 8.8 %collective-permute-done.9.refs_3_ = bf16[1,2,32,1024]{3,2,1,0:T(8,128)(2,1)S(1)} collective-permute-done((bf16[1,2,32,1024]{3,2,1,0:T(8,128)(2,1)S(1)}, bf16[1,2,32,1024]{3,2,1,0:T(8,128)(2,1)S(1)}, u32[]{:S(2)}, u32[]{:S(2)}) %collective-permute-start.9) | collective-permute-done | bytes 131104 | tf_op jit(solution)/shard_map/ppermute | solution.py:399
  88.4 2.1 copy-done.3
  90.5 2.2 copy-done.9
  100.1 3.9 %collective-permute-start.12 = (bf16[2,128,1024]{2,1,0:T(8,128)(2,1)S(1)}, bf16[2,128,1024]{2,1,0:T(8,128)(2,1)S(1)}, u32[]{:S(2)}, u32[]{:S(2)}) collective-permute-start(bf16[2,128,1024]{2,1,0:T(8,128)(2,1)S(1)} %get-tuple-element.87), channel_id=1, source_target_pairs={{0,4},{4,8},{8,12},{1,5},{5,9},{9,13},{2,6},{6,10},{10,14},{3,7},{... | collective-permute-start | bytes 1572872 | tf_op jit(solution)/shard_map/ppermute | solution.py:429
  104.0 2.0 collective-permute-start.13
  109.0 18.2 %collective-permute-done.12.refs_1_ = bf16[2,128,1024]{2,1,0:T(8,128)(2,1)S(1)} collective-permute-done((bf16[2,128,1024]{2,1,0:T(8,128)(2,1)S(1)}, bf16[2,128,1024]{2,1,0:T(8,128)(2,1)S(1)}, u32[]{:S(2)}, u32[]{:S(2)}) %collective-permute-start.12) | collective-permute-done | bytes 524320 | tf_op jit(solution)/shard_map/ppermute | solution.py:429
  128.2 3.9 %collective-permute-start.16 = (bf16[2,128,1024]{2,1,0:T(8,128)(2,1)S(1)}, bf16[2,128,1024]{2,1,0:T(8,128)(2,1)S(1)}, u32[]{:S(2)}, u32[]{:S(2)}) collective-permute-start(bf16[2,128,1024]{2,1,0:T(8,128)(2,1)S(1)} %get-tuple-element.92), channel_id=1, source_target_pairs={{0,4},{4,8},{8,12},{1,5},{5,9},{9,13},{2,6},{6,10},{10,14},{3,7},{... | collective-permute-start | bytes 1572872 | tf_op jit(solution)/shard_map/ppermute | solution.py:429
  135.6 19.5 %collective-permute-done.16.refs_1_ = bf16[2,128,1024]{2,1,0:T(8,128)(2,1)S(1)} collective-permute-done((bf16[2,128,1024]{2,1,0:T(8,128)(2,1)S(1)}, bf16[2,128,1024]{2,1,0:T(8,128)(2,1)S(1)}, u32[]{:S(2)}, u32[]{:S(2)}) %collective-permute-start.16) | collective-permute-done | bytes 524320 | tf_op jit(solution)/shard_map/ppermute | solution.py:429
  157.4 4.7 %collective-permute-start.17 = (bf16[2,128,1024]{2,1,0:T(8,128)(2,1)}, bf16[2,128,1024]{2,1,0:T(8,128)(2,1)}, u32[]{:S(2)}, u32[]{:S(2)}) collective-permute-start(bf16[2,128,1024]{2,1,0:T(8,128)(2,1)} %get-tuple-element.96), channel_id=1, source_target_pairs={{4,8},{8,12},{5,9},{9,13},{6,10},{10,14},{7,11},{11,15},{20,24},{2... | collective-permute-start | bytes 1572872 | tf_op jit(solution)/shard_map/ppermute | solution.py:429
  162.1 2.1 copy-done.5
  164.2 2.2 copy-done.11
  171.3 12.5 %collective-permute-done.17.refs_1_ = bf16[2,128,1024]{2,1,0:T(8,128)(2,1)} collective-permute-done((bf16[2,128,1024]{2,1,0:T(8,128)(2,1)}, bf16[2,128,1024]{2,1,0:T(8,128)(2,1)}, u32[]{:S(2)}, u32[]{:S(2)}) %collective-permute-start.17) | collective-permute-done | bytes 524320 | tf_op jit(solution)/shard_map/ppermute | solution.py:429
  195.3 2.1 copy-done.7
  197.4 2.2 copy-done.13
  202.5 21.3 %all-gather.2.cloned.1.call-done.refs_0_.refs_1_.refs_2_.refs_3_ = bf16[16384,1024]{1,0:T(8,128)(2,1)} async-done(((bf16[1024,1024]{1,0:T(8,128)(2,1)}), bf16[16384,1024]{1,0:T(8,128)(2,1)}) %all-gather.2.cloned.1.call-update) | async-done | bytes 33554448 | tf_op jit(solution)/shard_map/all_gather | solution.py:377
  223.8 3.4 %product.4 = bf16[256,512]{1,0:T(8,128)(2,1)S(1)} custom-call(s32[1]{0:T(128)} %bitcast.block_ref, bf16[4,256,1024]{2,1,0:T(8,128)(2,1)S(1)} %bitcast.30, bf16[16384,1024]{1,0:T(8,128)(2,1)} %all-gather.2.cloned.1.call-done.refs_0_.refs_1_.refs_2_.refs_3_, bf16[16384,1024]{1,0:T(8,128)(2,1)} %all-gather.2.cloned.1.call-done.refs_0_.refs_1_.refs_2_.refs_3_, ...), custom_call_target="tpu_custom_call" | custom-call | flops 1073741824 | bytes 6291456 | tf_op jit(solution)/shard_map/product/pallas_call | solution.py:322
  228.8 3.4 %product.5 = bf16[256,512]{1,0:T(8,128)(2,1)S(1)} custom-call(s32[1]{0:T(128)} %bitcast.block_ref, bf16[4,256,1024]{2,1,0:T(8,128)(2,1)S(1)} %bitcast.31, bf16[16384,1024]{1,0:T(8,128)(2,1)} %all-gather.2.cloned.1.call-done.refs_0_.refs_1_.refs_2_.refs_3_, bf16[16384,1024]{1,0:T(8,128)(2,1)} %all-gather.2.cloned.1.call-done.refs_0_.refs_1_.refs_2_.refs_3_, ...), custom_call_target="tpu_custom_call" | custom-call | flops 1073741824 | bytes 6291456 | tf_op jit(solution)/shard_map/product/pallas_call | solution.py:322
  232.9 9.1 %collective-permute-done.22 = bf16[4,2,64,1024]{3,2,1,0:T(8,128)(2,1)} collective-permute-done((bf16[4,2,64,1024]{3,2,1,0:T(8,128)(2,1)}, bf16[4,2,64,1024]{3,2,1,0:T(8,128)(2,1)}, u32[]{:S(2)}, u32[]{:S(2)}) %collective-permute-start.22) | collective-permute-done | bytes 1048608 | tf_op jit(solution)/shard_map/ppermute | solution.py:443
  244.7 4.8 %product.6 = bf16[256,1024]{1,0:T(8,128)(2,1)S(1)} custom-call(s32[1]{0:T(128)} %bitcast.17.block_ref, bf16[4,256,1024]{2,1,0:T(8,128)(2,1)S(1)} %bitcast.32, bf16[16384,1024]{1,0:T(8,128)(2,1)} %all-gather.2.cloned.1.call-done.refs_0_.refs_1_.refs_2_.refs_3_, bf16[16384,1024]{1,0:T(8,128)(2,1)} %all-gather.2.cloned.1.call-done.refs_0_.refs_1_.refs_2_.refs_3_, ...), custom_call_target="tpu_custom_call" | custom-call | flops 2147483648 | bytes 10485760 | tf_op jit(solution)/shard_map/product/pallas_call | solution.py:322
  251.3 9.0 %product.7 = bf16[256,2048]{1,0:T(8,128)(2,1)S(1)} custom-call(s32[2]{0:T(128)S(1)} %iota_add_fusion.block_ref, bf16[4,256,1024]{2,1,0:T(8,128)(2,1)S(1)} %bitcast.33, bf16[16384,1024]{1,0:T(8,128)(2,1)} %all-gather.2.cloned.1.call-done.refs_0_.refs_1_.refs_2_.refs_3_, bf16[16384,1024]{1,0:T(8,128)(2,1)} %all-gather.2.cloned.1.call-done.refs_0_.refs_1_.refs_2_.refs_3_, ...), custom_call_target="tpu_custom_call" | custom-call | flops 4294967296 | bytes 18874368 | tf_op jit(solution)/shard_map/product/pallas_call | solution.py:322
  260.4 3.3 %final_part.1 = f32[2,64,32,64]{3,2,1,0:T(8,128)} custom-call(bf16[4,2,32,1024]{3,2,1,0:T(8,128)(2,1)S(1)} %slice_select_fusion.1.value_ref), custom_call_target="tpu_custom_call" | custom-call | tf_op jit(solution)/shard_map/final_part/pallas_call | solution.py:292
  (189 shorter events, 72.0 us)
Async XLA Ops:
  7.2 7.6 %copy-start = (bf16[2,128,8,128]{3,2,1,0:T(8,128)(2,1)S(1)}, bf16[2,128,8,128]{3,2,1,0:T(8,128)(2,1)}, u32[]{:S(2)}) copy-start(bf16[2,128,8,128]{3,2,1,0:T(8,128)(2,1)} %param.15) | copy-start | bytes 1572868
  7.2 216.6 %all-gather.2.cloned.1.call-start = ((), (), s32[]{:S(2)}) async-start(), calls=%async_computation | async-start | bytes 35651584 | tf_op jit(solution)/shard_map/all_gather | solution.py:377
  14.7 3.2 %collective-permute-start = (bf16[4,2,32,1024]{3,2,1,0:T(8,128)(2,1)S(1)}, bf16[4,2,32,1024]{3,2,1,0:T(8,128)(2,1)S(1)}, u32[]{:S(2)}, u32[]{:S(2)}) collective-permute-start(bf16[4,2,32,1024]{3,2,1,0:T(8,128)(2,1)S(1)} %slice.40), channel_id=1, source_target_pairs={{0,1},{1,0},{2,3},{3,2},{4,5},{5,4},{6,7},{7,6},{8,9},{9,8},{10,11... | collective-permute-start | bytes 1572872 | tf_op jit(solution)/shard_map/ppermute | solution.py:391
  17.2 5.9 %copy-start.46 = (bf16[2,128,4096]{2,1,0:T(8,128)(2,1)S(1)}, bf16[2,128,4096]{2,1,0:T(8,128)(2,1)}, u32[]{:S(2)}) copy-start(bf16[2,128,4096]{2,1,0:T(8,128)(2,1)} %x_ref.2) | copy-start | bytes 6291460
  18.0 14.7 %collective-permute-start.1 = (bf16[1,2,32,1024]{3,2,1,0:T(8,128)(2,1)S(1)}, bf16[1,2,32,1024]{3,2,1,0:T(8,128)(2,1)S(1)}, u32[]{:S(2)}, u32[]{:S(2)}) collective-permute-start(bf16[1,2,32,1024]{3,2,1,0:T(8,128)(2,1)S(1)} %get-tuple-element.61.refs_1_), channel_id=1, source_target_pairs={{4,0},{5,1},{6,2},{7,3},{20,16},{21,17},{22,18},{23,19}} | collective-permute-start | bytes 393224 | tf_op jit(solution)/shard_map/ppermute | solution.py:399
  20.4 12.4 %collective-permute-start.2 = (bf16[1,2,32,1024]{3,2,1,0:T(8,128)(2,1)S(1)}, bf16[1,2,32,1024]{3,2,1,0:T(8,128)(2,1)}, u32[]{:S(2)}, u32[]{:S(2)}) collective-permute-start(bf16[1,2,32,1024]{3,2,1,0:T(8,128)(2,1)S(1)} %get-tuple-element.61.refs_1_), channel_id=1, source_target_pairs={{8,0},{9,1},{10,2},{11,3},{24,16},{25,17},{26,18},{27,19}} | collective-permute-start | bytes 393224 | tf_op jit(solution)/shard_map/ppermute | solution.py:399
  21.7 11.1 %collective-permute-start.3 = (bf16[1,2,32,1024]{3,2,1,0:T(8,128)(2,1)S(1)}, bf16[1,2,32,1024]{3,2,1,0:T(8,128)(2,1)}, u32[]{:S(2)}, u32[]{:S(2)}) collective-permute-start(bf16[1,2,32,1024]{3,2,1,0:T(8,128)(2,1)S(1)} %get-tuple-element.61.refs_1_), channel_id=1, source_target_pairs={{12,0},{13,1},{14,2},{15,3},{28,16},{29,17},{30,18},{31,19}} | collective-permute-start | bytes 393224 | tf_op jit(solution)/shard_map/ppermute | solution.py:399
  35.9 31.1 %collective-permute-start.4 = (bf16[2,128,1024]{2,1,0:T(8,128)(2,1)}, bf16[2,128,1024]{2,1,0:T(8,128)(2,1)}, u32[]{:S(2)}, u32[]{:S(2)}) collective-permute-start(bf16[2,128,1024]{2,1,0:T(8,128)(2,1)} %get-tuple-element.67), channel_id=1, source_target_pairs={{0,4},{1,5},{2,6},{3,7},{16,20},{17,21},{18,22},{19,23}} | collective-permute-start | bytes 1572872 | tf_op jit(solution)/shard_map/ppermute | solution.py:429
  39.0 27.9 %collective-permute-start.5 = (bf16[1,2,32,1024]{3,2,1,0:T(8,128)(2,1)S(1)}, bf16[1,2,32,1024]{3,2,1,0:T(8,128)(2,1)S(1)}, u32[]{:S(2)}, u32[]{:S(2)}) collective-permute-start(bf16[1,2,32,1024]{3,2,1,0:T(8,128)(2,1)S(1)} %get-tuple-element.74.refs_2_), channel_id=1, source_target_pairs={{4,0},{5,1},{6,2},{7,3},{20,16},{21,17},{22,18},{23,19}} | collective-permute-start | bytes 393224 | tf_op jit(solution)/shard_map/ppermute | solution.py:399
  44.3 22.6 %collective-permute-start.6 = (bf16[1,2,32,1024]{3,2,1,0:T(8,128)(2,1)S(1)}, bf16[1,2,32,1024]{3,2,1,0:T(8,128)(2,1)S(1)}, u32[]{:S(2)}, u32[]{:S(2)}) collective-permute-start(bf16[1,2,32,1024]{3,2,1,0:T(8,128)(2,1)S(1)} %get-tuple-element.74.refs_2_), channel_id=1, source_target_pairs={{8,0},{9,1},{10,2},{11,3},{24,16},{25,17},{26,18},{27,19}} | collective-permute-start | bytes 393224 | tf_op jit(solution)/shard_map/ppermute | solution.py:399
  45.0 21.9 %collective-permute-start.7 = (bf16[1,2,32,1024]{3,2,1,0:T(8,128)(2,1)S(1)}, bf16[1,2,32,1024]{3,2,1,0:T(8,128)(2,1)S(1)}, u32[]{:S(2)}, u32[]{:S(2)}) collective-permute-start(bf16[1,2,32,1024]{3,2,1,0:T(8,128)(2,1)S(1)} %get-tuple-element.74.refs_2_), channel_id=1, source_target_pairs={{12,0},{13,1},{14,2},{15,3},{28,16},{29,17},{30,18},{31,19}} | collective-permute-start | bytes 393224 | tf_op jit(solution)/shard_map/ppermute | solution.py:399
  70.3 27.8 %collective-permute-start.8 = (bf16[2,128,1024]{2,1,0:T(8,128)(2,1)}, bf16[2,128,1024]{2,1,0:T(8,128)(2,1)}, u32[]{:S(2)}, u32[]{:S(2)}) collective-permute-start(bf16[2,128,1024]{2,1,0:T(8,128)(2,1)} %get-tuple-element.78), channel_id=1, source_target_pairs={{0,4},{4,8},{1,5},{5,9},{2,6},{6,10},{3,7},{7,11},{16,20},{20,24},... | collective-permute-start | bytes 1572872 | tf_op jit(solution)/shard_map/ppermute | solution.py:429
  74.3 14.1 %collective-permute-start.9 = (bf16[1,2,32,1024]{3,2,1,0:T(8,128)(2,1)S(1)}, bf16[1,2,32,1024]{3,2,1,0:T(8,128)(2,1)S(1)}, u32[]{:S(2)}, u32[]{:S(2)}) collective-permute-start(bf16[1,2,32,1024]{3,2,1,0:T(8,128)(2,1)S(1)} %get-tuple-element.83.refs_2_), channel_id=1, source_target_pairs={{4,0},{5,1},{6,2},{7,3},{20,16},{21,17},{22,18},{23,19}} | collective-permute-start | bytes 393224 | tf_op jit(solution)/shard_map/ppermute | solution.py:399
  76.9 11.5 %collective-permute-start.10 = (bf16[1,2,32,1024]{3,2,1,0:T(8,128)(2,1)S(1)}, bf16[1,2,32,1024]{3,2,1,0:T(8,128)(2,1)}, u32[]{:S(2)}, u32[]{:S(2)}) collective-permute-start(bf16[1,2,32,1024]{3,2,1,0:T(8,128)(2,1)S(1)} %get-tuple-element.83.refs_2_), channel_id=1, source_target_pairs={{8,0},{9,1},{10,2},{11,3},{24,16},{25,17},{26,18},{27,19}} | collective-permute-start | bytes 393224 | tf_op jit(solution)/shard_map/ppermute | solution.py:399
  78.2 10.2 %collective-permute-start.11 = (bf16[1,2,32,1024]{3,2,1,0:T(8,128)(2,1)S(1)}, bf16[1,2,32,1024]{3,2,1,0:T(8,128)(2,1)}, u32[]{:S(2)}, u32[]{:S(2)}) collective-permute-start(bf16[1,2,32,1024]{3,2,1,0:T(8,128)(2,1)S(1)} %get-tuple-element.83.refs_2_), channel_id=1, source_target_pairs={{12,0},{13,1},{14,2},{15,3},{28,16},{29,17},{30,18},{31,19}} | collective-permute-start | bytes 393224 | tf_op jit(solution)/shard_map/ppermute | solution.py:399
  79.6 75.5 %copy-start.39 = (s32[2]{0:T(128)}, s32[2]{0:T(128)S(1)}, u32[]{:S(2)}) copy-start(s32[2]{0:T(128)S(1)} %get-tuple-element.126.refs_0_.at_ref) | copy-start | bytes 28
  96.0 11.4 %copy-start.10 = (f32[2,128,4096]{2,1,0:T(8,128)S(1)}, f32[2,128,4096]{2,1,0:T(8,128)}, u32[]{:S(2)}) copy-start(f32[2,128,4096]{2,1,0:T(8,128)} %copy-done.8) | copy-start | bytes 12582916
  100.1 27.2 %collective-permute-start.12 = (bf16[2,128,1024]{2,1,0:T(8,128)(2,1)S(1)}, bf16[2,128,1024]{2,1,0:T(8,128)(2,1)S(1)}, u32[]{:S(2)}, u32[]{:S(2)}) collective-permute-start(bf16[2,128,1024]{2,1,0:T(8,128)(2,1)S(1)} %get-tuple-element.87), channel_id=1, source_target_pairs={{0,4},{4,8},{8,12},{1,5},{5,9},{9,13},{2,6},{6,10},{10,14},{3,7},{... | collective-permute-start | bytes 1572872 | tf_op jit(solution)/shard_map/ppermute | solution.py:429
  104.0 23.3 %collective-permute-start.13 = (bf16[1,2,32,1024]{3,2,1,0:T(8,128)(2,1)S(1)}, bf16[1,2,32,1024]{3,2,1,0:T(8,128)(2,1)S(1)}, u32[]{:S(2)}, u32[]{:S(2)}) collective-permute-start(bf16[1,2,32,1024]{3,2,1,0:T(8,128)(2,1)S(1)} %get-tuple-element.91.refs_2_), channel_id=1, source_target_pairs={{4,0},{5,1},{6,2},{7,3},{20,16},{21,17},{22,18},{23,19}} | collective-permute-start | bytes 393224 | tf_op jit(solution)/shard_map/ppermute | solution.py:399
  106.0 21.3 %collective-permute-start.14 = (bf16[1,2,32,1024]{3,2,1,0:T(8,128)(2,1)S(1)}, bf16[1,2,32,1024]{3,2,1,0:T(8,128)(2,1)S(1)}, u32[]{:S(2)}, u32[]{:S(2)}) collective-permute-start(bf16[1,2,32,1024]{3,2,1,0:T(8,128)(2,1)S(1)} %get-tuple-element.91.refs_2_), channel_id=1, source_target_pairs={{8,0},{9,1},{10,2},{11,3},{24,16},{25,17},{26,18},{27,19}} | collective-permute-start | bytes 393224 | tf_op jit(solution)/shard_map/ppermute | solution.py:399
  106.7 20.6 %collective-permute-start.15 = (bf16[1,2,32,1024]{3,2,1,0:T(8,128)(2,1)S(1)}, bf16[1,2,32,1024]{3,2,1,0:T(8,128)(2,1)S(1)}, u32[]{:S(2)}, u32[]{:S(2)}) collective-permute-start(bf16[1,2,32,1024]{3,2,1,0:T(8,128)(2,1)S(1)} %get-tuple-element.91.refs_2_), channel_id=1, source_target_pairs={{12,0},{13,1},{14,2},{15,3},{28,16},{29,17},{30,18},{31,19}} | collective-permute-start | bytes 393224 | tf_op jit(solution)/shard_map/ppermute | solution.py:399
  107.4 19.9 %copy-start.36 = (s32[2]{0:T(128)S(1)}, s32[2]{0:T(128)}, u32[]{:S(2)}) copy-start(s32[2]{0:T(128)} %get-tuple-element.128.refs_0_.at_ref) | copy-start | bytes 28
  128.2 26.9 %collective-permute-start.16 = (bf16[2,128,1024]{2,1,0:T(8,128)(2,1)S(1)}, bf16[2,128,1024]{2,1,0:T(8,128)(2,1)S(1)}, u32[]{:S(2)}, u32[]{:S(2)}) collective-permute-start(bf16[2,128,1024]{2,1,0:T(8,128)(2,1)S(1)} %get-tuple-element.92), channel_id=1, source_target_pairs={{0,4},{4,8},{8,12},{1,5},{5,9},{9,13},{2,6},{6,10},{10,14},{3,7},{... | collective-permute-start | bytes 1572872 | tf_op jit(solution)/shard_map/ppermute | solution.py:429
  157.4 26.5 %collective-permute-start.17 = (bf16[2,128,1024]{2,1,0:T(8,128)(2,1)}, bf16[2,128,1024]{2,1,0:T(8,128)(2,1)}, u32[]{:S(2)}, u32[]{:S(2)}) collective-permute-start(bf16[2,128,1024]{2,1,0:T(8,128)(2,1)} %get-tuple-element.96), channel_id=1, source_target_pairs={{4,8},{8,12},{5,9},{9,13},{6,10},{10,14},{7,11},{11,15},{20,24},{2... | collective-permute-start | bytes 1572872 | tf_op jit(solution)/shard_map/ppermute | solution.py:429
  169.7 16.6 %copy-start.12 = (f32[2,128,4096]{2,1,0:T(8,128)S(1)}, f32[2,128,4096]{2,1,0:T(8,128)}, u32[]{:S(2)}) copy-start(f32[2,128,4096]{2,1,0:T(8,128)} %copy-done.8) | copy-start | bytes 12582916
  185.6 2.4 collective-permute-start.18
  193.0 49.0 %collective-permute-start.22 = (bf16[4,2,64,1024]{3,2,1,0:T(8,128)(2,1)}, bf16[4,2,64,1024]{3,2,1,0:T(8,128)(2,1)}, u32[]{:S(2)}, u32[]{:S(2)}) collective-permute-start(bf16[4,2,64,1024]{3,2,1,0:T(8,128)(2,1)} %slice.46), channel_id=1, source_target_pairs={{12,4},{13,5},{14,6},{15,7},{28,20},{29,21},{30,22},{31,23}} | collective-permute-start | bytes 3145736 | tf_op jit(solution)/shard_map/ppermute | solution.py:443
  227.2 14.7 %copy-start.51 = (bf16[4,2,128,1024]{3,2,1,0:T(8,128)(2,1)S(1)}, bf16[4,2,128,1024]{3,2,1,0:T(8,128)(2,1)}, u32[]{:S(2)}) copy-start(bf16[4,2,128,1024]{3,2,1,0:T(8,128)(2,1)} %copy-done.50) | copy-start | bytes 6291460
  227.2 36.5 %collective-permute-start.19 = (bf16[256,512]{1,0:T(8,128)(2,1)S(1)}, bf16[256,512]{1,0:T(8,128)(2,1)S(1)}, u32[]{:S(2)}, u32[]{:S(2)}) collective-permute-start(bf16[256,512]{1,0:T(8,128)(2,1)S(1)} %product.4), channel_id=1, source_target_pairs={{0,2},{2,0},{1,3},{3,1},{4,6},{6,4},{5,7},{7,5},{8,10},{10,8},{9,1... | collective-permute-start | bytes 786440 | tf_op jit(solution)/shard_map/ppermute | solution.py:468
  232.2 31.5 %collective-permute-start.20 = (bf16[256,512]{1,0:T(8,128)(2,1)S(1)}, bf16[256,512]{1,0:T(8,128)(2,1)S(1)}, u32[]{:S(2)}, u32[]{:S(2)}) collective-permute-start(bf16[256,512]{1,0:T(8,128)(2,1)S(1)} %product.5), channel_id=1, source_target_pairs={{0,2},{2,0},{1,3},{3,1},{4,6},{6,4},{5,7},{7,5},{8,10},{10,8},{9,1... | collective-permute-start | bytes 786440 | tf_op jit(solution)/shard_map/ppermute | solution.py:468
  243.4 17.0 %collective-permute-start.23 = (bf16[4,2,32,1024]{3,2,1,0:T(8,128)(2,1)S(1)}, bf16[4,2,32,1024]{3,2,1,0:T(8,128)(2,1)S(1)}, u32[]{:S(2)}, u32[]{:S(2)}) collective-permute-start(bf16[4,2,32,1024]{3,2,1,0:T(8,128)(2,1)S(1)} %slice.48), channel_id=1, source_target_pairs={{4,0},{12,8},{5,1},{13,9},{6,2},{14,10},{7,3},{15,11},{20,16},{28,... | collective-permute-start | bytes 1572872 | tf_op jit(solution)/shard_map/ppermute | solution.py:443
  249.5 14.2 %collective-permute-start.21 = (bf16[256,1024]{1,0:T(8,128)(2,1)S(1)}, bf16[256,1024]{1,0:T(8,128)(2,1)S(1)}, u32[]{:S(2)}, u32[]{:S(2)}) collective-permute-start(bf16[256,1024]{1,0:T(8,128)(2,1)S(1)} %product.6), channel_id=1, source_target_pairs={{0,2},{2,0},{1,3},{3,1},{4,6},{6,4},{5,7},{7,5},{8,10},{10,8},{9,1... | collective-permute-start | bytes 1572872 | tf_op jit(solution)/shard_map/ppermute | solution.py:468
  (52 other events, 129.3 us)
Sparse Core Ops, SparseCore 0:
  10.5 213.2 all-gather.1
